TPU v7x, 32 devices: a whole 2x2x4 slice. The times are simulated.
32 devices in a mesh: grp: 4 (over y, core), seq: 2 (over x), head: 4 (over z).
Axes of the slice: x: 2, y: 2, z: 4, core: 2. Of those that a mesh axis runs over, the one named last changes fastest.
Arguments:
- keys: bfloat16 [32, 1024, 1536], P('grp', 'seq', 'head'), may hold values from -6 to 6
- values: bfloat16 [32, 1024, 1536], P('grp', 'seq', 'head'), may hold values from -6 to 6
- log_forget: float32 [32, 24, 1024], P('grp', 'head', 'seq'), may hold values from -0.6 to 0, as said below
- keep: int32 [32, 1024], P('grp', 'seq'), may hold values from 0 to 1, as said below
- merge_weight: float32 [32, 1024], P('grp', 'seq'), may hold values from 0.1 to 10
- lengths: int32 [32], P('grp'), may hold values from 64 to 1024, as said below
- route: int32 [32], P('grp'), may hold values from 0 to 31, as said below
- fresh: bfloat16 [3, 32, 1536], P(None, 'grp', 'head'), may hold values from -7.5 to 7.5
- new_forget: bfloat16 [32, 24], P('grp', 'head'), may hold values from -1 to -0.049804688
- out_weight: bfloat16 [1536, 1536], P('head', 'seq'), may hold values from -0.15625 to 0.15625
Outputs:
- compact_keys: bfloat16 [32, 512, 1536], P('grp', 'seq', 'head')
- compact_values: bfloat16 [32, 512, 1536], P('grp', 'seq', 'head')
- compact_decay: float32 [32, 24, 512], P('grp', 'head', 'seq')
- layer_out: bfloat16 [32, 1536], P('grp', 'seq')
Inputs may be any that keep to these rules, and one draw needn't show every extreme that they name: `keep`: within every aligned block of 64 positions of a request, between 16 and 31 entries are 1, and some block has exactly 31. `lengths`: multiples of 64; the first request of every 8 in order has 1024. `route`: A permutation of the requests. `log_forget`: Negative.
All inputs are finite; a program needn't handle non-finite values.
Results may differ from a plain program's by a relative error of at most 0.0085.
Values may be sent and summed in bfloat16 or wider, within the bound.
No kernel may reach another device: no remote copies, remote signals or barrier semaphores. Data moves between devices by JAX's collectives and lax.ppermute only.
A program may use at most 64 MiB of HBM per device.

v0:
```python
import jax
import jax.numpy as jnp
from jax import lax
from jax.sharding import PartitionSpec as P

BLOCK = 64
SLOTS = 32


EMPTY_LOG = -10000.0


def carried_in(value, axis, join, neutral):
    count, mine = (lax.axis_size(axis), lax.axis_index(axis))
    pieces = lax.all_gather(value, axis)
    pieces = pieces[::-1]
    mine = count - 1 - mine
    so_far = jnp.full_like(value, 0) + jnp.asarray(neutral, value.dtype)

    def turn(position, so_far):
        longer = join(so_far, pieces[position])
        return jnp.where(position < mine, longer, so_far)

    return lax.fori_loop(0, count - 1, turn, so_far)


def merged(value, axis, join):
    pieces = jax.tree.map(lambda part: lax.all_gather(part, axis), value)
    head = jax.tree.map(lambda part: part[0], pieces)
    tail = jax.tree.map(lambda part: part[1:], pieces)
    so_far, _ = lax.scan(lambda so_far, section: (join(so_far, section), None), head, tail)
    return so_far


def add_totals(earlier, later):
    return earlier + later


def merge_parts(first, second):
    top_one, sum_one, acc_one = first
    top_two, sum_two, acc_two = second
    joint = jnp.maximum(top_one, top_two)
    scale_one = jnp.exp(top_one - joint)
    scale_two = jnp.exp(top_two - joint)
    return (
        joint,
        sum_one * scale_one + sum_two * scale_two,
        acc_one * scale_one[..., None] + acc_two * scale_two[..., None],
    )


def shards(
    keys, values, log_forget, keep, merge_weight, lengths, route, fresh, new_forget, out_weight
):
    req_dev, pos_dev, width_dev = keys.shape
    heads_dev = log_forget.shape[1]
    head_size = width_dev // heads_dev
    blocks_dev = pos_dev // BLOCK
    rows_dev = blocks_dev * SLOTS
    shard = lax.axis_index("seq")
    position = shard * pos_dev + jnp.arange(pos_dev, dtype=jnp.int32)
    live = position[None, :] < lengths[:, None]
    forget = jnp.where(live[:, None, :], log_forget, 0.0)
    own_total = jnp.sum(forget, axis=2)
    inner = own_total[:, :, None] - jnp.cumsum(forget, axis=2)
    later_sum = carried_in(own_total, "seq", add_totals, jnp.zeros_like(own_total))
    log_decay = inner + later_sum[:, :, None]
    flags = keep.reshape(req_dev, blocks_dev, BLOCK)
    rank = jnp.cumsum(flags, axis=2) - 1
    slot_ids = jnp.arange(SLOTS - 1, dtype=jnp.int32)
    block_start = shard * pos_dev + jnp.arange(blocks_dev, dtype=jnp.int32) * BLOCK
    block_live = (block_start[None, :] < lengths[:, None]).astype(jnp.float32)
    chosen = (
        (flags[:, :, None, :] == 1) & (rank[:, :, None, :] == slot_ids[None, None, :, None])
    ).astype(jnp.float32)
    chosen = chosen * block_live[:, :, None, None]
    dropped = flags == 0
    weighted = jnp.where(dropped, merge_weight.reshape(req_dev, blocks_dev, BLOCK), 0.0)
    share = (
        (weighted / jnp.sum(weighted, axis=2, keepdims=True))
        .astype(jnp.bfloat16)
        .astype(jnp.float32)
    )
    merged_row = (share * block_live[:, :, None])[:, :, None, :]
    select = jnp.concatenate([chosen, merged_row], axis=2).astype(jnp.bfloat16)
    key_blocks = keys.reshape(req_dev, blocks_dev, BLOCK, width_dev)
    value_blocks = values.reshape(req_dev, blocks_dev, BLOCK, width_dev)
    packed_keys = (
        jnp.einsum("rbej,rbjc->rbec", select, key_blocks, preferred_element_type=jnp.float32)
        .astype(jnp.bfloat16)
        .reshape(req_dev, rows_dev, width_dev)
    )
    packed_values = (
        jnp.einsum("rbej,rbjc->rbec", select, value_blocks, preferred_element_type=jnp.float32)
        .astype(jnp.bfloat16)
        .reshape(req_dev, rows_dev, width_dev)
    )
    decay_blocks = log_decay.reshape(req_dev, heads_dev, blocks_dev, BLOCK)
    kept_log = jnp.einsum("rbej,rhbj->rhbe", chosen, decay_blocks, precision=lax.Precision.HIGHEST)
    filled = jnp.sum(chosen, axis=3)
    kept_log = kept_log + (1.0 - filled)[:, None, :, :] * EMPTY_LOG
    drop_mask = dropped[:, None, :, :]
    drop_peak = jnp.max(jnp.where(drop_mask, decay_blocks, -jnp.inf), axis=3)
    spread = jnp.where(drop_mask, jnp.exp(decay_blocks - drop_peak[..., None]), 0.0)
    merged_log = drop_peak + jnp.log(jnp.sum(share[:, None, :, :] * spread, axis=3))
    merged_log = jnp.where(block_live[:, None, :] > 0, merged_log, EMPTY_LOG)
    slot_log = jnp.concatenate([kept_log, merged_log[..., None]], axis=3).reshape(
        req_dev, heads_dev, rows_dev
    )
    compact_decay = jnp.exp(slot_log)
    dealt_keys, dealt_values = (
        lax.all_to_all(packed_keys, "seq", split_axis=1, concat_axis=1, tiled=True),
        lax.all_to_all(packed_values, "seq", split_axis=1, concat_axis=1, tiled=True),
    )
    arrived, arrived_forget = (
        lax.all_gather(fresh, "grp", axis=1, tiled=True),
        lax.all_gather(new_forget, "grp", axis=0, tiled=True),
    )
    picked = jnp.take(arrived, route, axis=1)
    new_log = jnp.take(arrived_forget, route, axis=0).astype(jnp.float32)
    query = picked[0].reshape(req_dev, heads_dev, head_size)
    own_key = picked[1].reshape(req_dev, heads_dev, head_size)
    own_value = picked[2].reshape(req_dev, heads_dev, head_size).astype(jnp.float32)
    scale = head_size ** (-0.5)
    key_rows = packed_keys.reshape(req_dev, rows_dev, heads_dev, head_size)
    value_rows = packed_values.reshape(req_dev, rows_dev, heads_dev, head_size)
    scores = (
        jnp.einsum("rhd,rnhd->rhn", query, key_rows, preferred_element_type=jnp.float32) * scale
        + slot_log
    )
    local_top = jnp.max(scores, axis=2)
    weights = jnp.exp(scores - local_top[..., None]).astype(jnp.bfloat16)
    local_sum = jnp.sum(weights.astype(jnp.float32), axis=2)
    local_acc = jnp.einsum("rhn,rnhd->rhd", weights, value_rows, preferred_element_type=jnp.float32)
    top, total_sum, total_acc = merged((local_top, local_sum, local_acc), "seq", merge_parts)
    own_score = jnp.sum(query.astype(jnp.float32) * own_key.astype(jnp.float32), axis=2) * scale
    cache_top = top + new_log
    joint = jnp.maximum(cache_top, own_score)
    cache_scale = jnp.exp(cache_top - joint)
    self_weight = jnp.exp(own_score - joint)
    attended = (cache_scale[..., None] * total_acc + self_weight[..., None] * own_value) / (
        cache_scale * total_sum + self_weight
    )[..., None]
    attended = attended.reshape(req_dev, width_dev).astype(jnp.bfloat16)
    partial_out = jnp.dot(attended, out_weight, preferred_element_type=jnp.float32)
    layer_out = lax.psum(partial_out, "head").astype(jnp.bfloat16)
    return (dealt_keys, dealt_values, compact_decay, layer_out)


def solution(mesh):
    return jax.shard_map(
        shards,
        mesh=mesh,
        in_specs=(
            P("grp", "seq", "head"),
            P("grp", "seq", "head"),
            P("grp", "head", "seq"),
            P("grp", "seq"),
            P("grp", "seq"),
            P("grp"),
            P("grp"),
            P(None, "grp", "head"),
            P("grp", "head"),
            P("head", "seq"),
        ),
        out_specs=(
            P("grp", "seq", "head"),
            P("grp", "seq", "head"),
            P("grp", "head", "seq"),
            P("grp", "seq"),
        ),
        check_vma=False,
    )
```

profile of v0, /device:TPU:0, one launch (start us, length us, event | category | flops | bytes accessed | tf_op | source)
XLA Modules:
  0.0 144.4 jit_solution(3110049765206679879)
XLA Ops:
  0.6 0.9 broadcast_in_dim_reshape.3
  1.6 0.8 reshape.395
  2.4 0.7 compare_select_fusion
  3.2 1.8 %reduce_window_sum.24 = s32[8,8,64]{2,1,0:T(8,128)S(1)} reduce-window(s32[8,8,64]{2,1,0:T(8,128)S(1)} %broadcast_in_dim_reshape.3, s32[]{:T(128)} %constant.42.clone.1), window={size=1x1x64 pad=0_0x0_0x63_0}, to_apply=%region_0.1 | reduce-window | flops 258048 | bytes 32772 | tf_op jit(solution)/shard_map/jit(cumsum)/reduce_window_sum | solution.py:69
  5.1 1.3 broadcast_compare_fusion.3
  6.4 0.3 select_convert_fusion
  6.9 0.5 copy-done.2
  7.5 0.7 convolution_convert_fusion
  8.2 1.1 copy-done.1
  9.4 2.1 %copy.59 = bf16[8,256,384]{2,0,1:T(8,128)(2,1)} copy(bf16[8,256,384]{2,1,0:T(8,128)(2,1)S(1)} %bitcast.49) | data formatting | bytes 3145728 | tf_op jit(solution)/shard_map/reshape | solution.py:96
  11.5 4.6 %all-to-all-start.1 = ((bf16[8,256,384]{2,0,1:T(8,128)(2,1)}), bf16[8,256,384]{2,0,1:T(8,128)(2,1)}, u32[]{:S(2)}, u32[]{:S(2)}) async-start(bf16[8,256,384]{2,0,1:T(8,128)(2,1)} %copy.59), calls=%async_computation.1 | async-start | bytes 3145728 | tf_op jit(solution)/shard_map/all_to_all | solution.py:113
  16.2 0.7 select_bitcast_fusion
  16.9 6.8 %reduce-window.6 = f32[8,6,4,128]{3,0,1,2:T(8,128)S(1)} reduce-window(f32[8,6,4,128]{3,0,1,2:T(8,128)S(1)} %copy.61, f32[]{:T(128)} %constant.54.clone.1), window={size=1x1x1x128 pad=0_0x0_0x0_0x127_0}, to_apply=%region_3.4 | reduce-window | flops 3121152 | bytes 196612 | tf_op jit(solution)/shard_map/reduce-window
  23.8 1.8 %select_reduce_fusion = f32[8,8,31]{2,1,0:T(8,128)} fusion(f32[8,8]{1,0:T(8,128)} %copy-done.9, s32[8,8,64]{2,1,0:T(8,128)} %copy-done.5, pred[8,8,64]{2,1,0:T(8,128)(4,1)S(1)} %broadcast_compare_fusion.1), kind=kLoop, calls=%fused_computation.6 | loop fusion | flops 505920 | bytes 28672 | tf_op jit(solution)/shard_map/reduce_sum | solution.py:100
  25.6 1.2 compare_select_fusion.1
  26.8 1.2 compare_and_fusion
  28.0 0.8 copy.60
  28.8 8.3 %all-gather = f32[16,6]{1,0:T(8,128)} all-gather(f32[8,6]{1,0:T(8,128)S(1)} %copy.60), channel_id=2, replica_groups=mesh['grp'=4,'seq'=2,'head'=4] {'seq'}, dimensions={0}, use_global_device_ids=true | all-gather | bytes 576 | tf_op jit(solution)/shard_map/all_gather | solution.py:15
  37.2 0.2 copy.63
  37.5 0.8 fusion.23
  38.4 0.7 slice_select_fusion
  39.1 1.0 select_reduce_fusion.1
  40.1 0.2 multiply_reduce_fusion
  40.3 0.4 copy-done.3
  40.8 0.5 copy.68
  41.2 0.8 subtract_multiply_fusion
  42.0 3.5 %fusion.9 = f32[8,6,8,31]{3,1,2,0:T(8,128)} fusion(f32[8,8]{1,0:T(8,128)} %copy-done.9, s32[8,8,64]{2,1,0:T(8,128)} %copy-done.5, pred[8,8,64]{2,1,0:T(8,128)(4,1)S(1)} %broadcast_compare_fusion.1, f32[8,6,8,64]{3,2,1,0:T(8,128)} %copy-done.3, f32[8,8,31]{2,1,0:T(8,128)S(1)} %subtract_multiply_fusion), kind=kOutput, calls=%fused_computation.13 | convolution fusion | flops 9535104 | bytes 174592 | tf_op jit(solution)/shard_map/rbej,rhbj->rhbe/dot_general | solution.py:99
  45.5 3.9 %convolution_convert_fusion.1 = bf16[8,8,32,384]{3,2,1,0:T(8,128)(2,1)} fusion(bf16[8,8,64,384]{3,2,1,0:T(8,128)(2,1)} %bitcast.51, bf16[8,8,1,64]{3,2,1,0:T(2,128)(2,1)} %copy-done.4, bf16[8,8,31,64]{3,2,1,0:T(8,128)(2,1)} %copy-done.2), kind=kOutput, calls=%fused_computation.11 | convolution fusion | flops 101974016 | bytes 4980736 | tf_op jit(solution)/shard_map/rbej,rbjc->rbec/dot_general | solution.py:89
  49.4 5.9 %reshape_reshape.6 = bf16[8,256,6,64]{3,2,1,0:T(8,128)(2,1)} reshape(bf16[8,8,32,384]{3,2,1,0:T(8,128)(2,1)} %convolution_convert_fusion.1) | data formatting | bytes 3145728 | tf_op jit(solution)/shard_map/reshape;reshape | solution.py:125
  55.3 5.3 %all_gather.32 = bf16[3,32,384]{2,1,0:T(8,128)(2,1)S(1)} all-gather(bf16[3,8,384]{2,1,0:T(8,128)(2,1)S(1)} %copy-done.12), channel_id=1, replica_groups=mesh['grp'=4,'seq'=2,'head'=4] {'grp'}, dimensions={1}, use_global_device_ids=true | all-gather | bytes 92160 | tf_op jit(solution)/shard_map/all_gather | solution.py:116
  60.7 0.6 gather_fusion
  61.7 3.1 %fusion.2 = f32[8,6,1,256]{3,2,1,0:T(1,128)S(1)} fusion(bf16[8,6,64,1]{2,3,1,0:T(2,128)(2,1)S(1)} %reshape.455, bf16[8,256,6,64]{3,2,1,0:T(8,128)(2,1)} %reshape_reshape.6), kind=kOutput, calls=%fused_computation.4 | convolution fusion | flops 1572864 | bytes 1628160 | tf_op jit(solution)/shard_map/rhd,rnhd->rhn/dot_general | solution.py:128
  64.9 5.9 %reshape_reshape.7 = bf16[8,256,6,64]{3,2,1,0:T(8,128)(2,1)} reshape(bf16[8,8,32,384]{3,2,1,0:T(8,128)(2,1)} %copy-done.1) | data formatting | bytes 3145728 | tf_op jit(solution)/shard_map/reshape;reshape | solution.py:126
  70.9 0.7 copy.69
  71.6 1.0 reshape.404
  72.8 0.7 convert_reduce_fusion
  73.5 2.7 %fusion = f32[8,6,1,64]{3,2,1,0:T(1,128)S(1)} fusion(bf16[8,256,6,64]{3,2,1,0:T(8,128)(2,1)} %reshape_reshape.7, bf16[8,6,256,1]{2,0,1,3:T(8,128)(2,1)S(1)} %bitcast.55), kind=kOutput, calls=%fused_computation.2 | convolution fusion | flops 1572864 | bytes 1609728 | tf_op jit(solution)/shard_map/rhn,rnhd->rhd/dot_general | solution.py:134
  76.5 5.2 %all_gather.35 = bf16[32,6]{1,0:T(8,128)(2,1)S(1)} all-gather(bf16[8,6]{1,0:T(8,128)(2,1)S(1)} %copy-done.15), channel_id=1, replica_groups=mesh['grp'=4,'seq'=2,'head'=4] {'grp'}, dimensions={0}, use_global_device_ids=true | all-gather | bytes 480 | tf_op jit(solution)/shard_map/all_gather | solution.py:117
  81.6 0.6 gather_fusion.1
  82.2 3.5 %copy.58 = bf16[8,256,384]{2,0,1:T(8,128)(2,1)} copy(bf16[8,256,384]{2,1,0:T(8,128)(2,1)} %bitcast.50) | data formatting | bytes 3145728 | tf_op jit(solution)/shard_map/reshape | solution.py:91
  85.7 4.3 %all-gather.3 = f32[16,6]{1,0:T(8,128)S(1)} all-gather(f32[8,6]{1,0:T(8,128)S(1)} %copy.76), channel_id=5, replica_groups=mesh['grp'=4,'seq'=2,'head'=4] {'seq'}, dimensions={0}, use_global_device_ids=true | all-gather | bytes 576 | tf_op jit(solution)/shard_map/all_gather | solution.py:28
  90.0 4.3 %all-gather.1 = f32[16,6]{1,0:T(8,128)S(1)} all-gather(f32[8,6]{1,0:T(8,128)S(1)} %copy.71), channel_id=3, replica_groups=mesh['grp'=4,'seq'=2,'head'=4] {'seq'}, dimensions={0}, use_global_device_ids=true | all-gather | bytes 576 | tf_op jit(solution)/shard_map/all_gather | solution.py:28
  94.3 4.6 %all-to-all-start = ((bf16[8,256,384]{2,0,1:T(8,128)(2,1)}), bf16[8,256,384]{2,0,1:T(8,128)(2,1)}, u32[]{:S(2)}, u32[]{:S(2)}) async-start(bf16[8,256,384]{2,0,1:T(8,128)(2,1)} %copy.58), calls=%async_computation | async-start | bytes 3145728 | tf_op jit(solution)/shard_map/all_to_all | solution.py:112
  99.4 17.8 %all-gather.2 = f32[16,6,64]{2,0,1:T(8,128)S(1)} all-gather(f32[8,6,64]{2,0,1:T(8,128)S(1)} %bitcast.53), channel_id=4, replica_groups=mesh['grp'=4,'seq'=2,'head'=4] {'seq'}, dimensions={0}, use_global_device_ids=true | all-gather | bytes 36864 | tf_op jit(solution)/shard_map/all_gather | solution.py:28
  117.6 1.2 fusion.30
  118.8 20.0 %psum.7 = bf16[8,768]{1,0:T(8,128)(2,1)} all-reduce(f32[8,768]{1,0:T(8,128)S(1)} %fusion.30), channel_id=1, replica_groups=mesh['grp'=4,'seq'=2,'head'=4] {'head'}, use_global_device_ids=true, to_apply=%region_11.12 | all-reduce | flops 6144 | bytes 36864 | tf_op jit(solution)/shard_map/psum | solution.py:146
  138.9 2.8 %copy.78 = bf16[8,256,384]{2,1,0:T(8,128)(2,1)} copy(bf16[8,256,384]{2,0,1:T(8,128)(2,1)} %all-to-all-done.1) | data formatting | bytes 3145728
  141.6 2.8 %copy.77 = bf16[8,256,384]{2,1,0:T(8,128)(2,1)} copy(bf16[8,256,384]{2,0,1:T(8,128)(2,1)} %all-to-all-done) | data formatting | bytes 3145728
  (78 shorter events, 2.8 us)
Async XLA Ops:
  0.6 6.3 %copy-start = (bf16[8,512,384]{2,1,0:T(8,128)(2,1)S(1)}, bf16[8,512,384]{2,1,0:T(8,128)(2,1)}, u32[]{:S(2)}) copy-start(bf16[8,512,384]{2,1,0:T(8,128)(2,1)} %param.11) | copy-start | bytes 9437188
  2.4 9.1 %copy-start.6 = (f32[8,8,64]{2,1,0:T(8,128)}, f32[8,8,64]{2,1,0:T(8,128)S(1)}, u32[]{:S(2)}) copy-start(f32[8,8,64]{2,1,0:T(8,128)S(1)} %reshape.395) | copy-start | bytes 49156
  3.2 4.9 %copy-start.10 = (f32[8,8]{1,0:T(8,128)}, f32[8,8]{1,0:T(8,128)S(1)}, u32[]{:S(2)}) copy-start(f32[8,8]{1,0:T(8,128)S(1)} %get-tuple-element.57) | copy-start | bytes 772
  5.0 6.5 %copy-start.5 = (s32[8,8,64]{2,1,0:T(8,128)}, s32[8,8,64]{2,1,0:T(8,128)S(1)}, u32[]{:S(2)}) copy-start(s32[8,8,64]{2,1,0:T(8,128)S(1)} %broadcast_add_fusion) | copy-start | bytes 49156
  6.4 1.8 %copy-start.9 = (f32[8,8]{1,0:T(8,128)}, f32[8,8]{1,0:T(8,128)S(1)}, u32[]{:S(2)}) copy-start(f32[8,8]{1,0:T(8,128)S(1)} %get-tuple-element.65) | copy-start | bytes 772
  6.7 0.8 copy-start.2
  6.9 1.3 copy-start.4
  8.2 1.1 copy-start.1
  9.4 6.8 %copy-start.16 = (s32[8]{0:T(128)S(1)}, s32[8]{0:T(128)}, u32[]{:S(2)}) copy-start(s32[8]{0:T(128)} %param.15) | copy-start | bytes 100
  9.4 6.8 %copy-start.8 = (f32[8,6,512]{2,0,1:T(8,128)S(1)}, f32[8,6,512]{2,0,1:T(8,128)}, u32[]{:S(2)}) copy-start(f32[8,6,512]{2,0,1:T(8,128)} %param.12) | copy-start | bytes 294916
  11.5 82.9 %all-to-all-start.1 = ((bf16[8,256,384]{2,0,1:T(8,128)(2,1)}), bf16[8,256,384]{2,0,1:T(8,128)(2,1)}, u32[]{:S(2)}, u32[]{:S(2)}) async-start(bf16[8,256,384]{2,0,1:T(8,128)(2,1)} %copy.59), calls=%async_computation.1 | async-start | bytes 3145728 | tf_op jit(solution)/shard_map/all_to_all | solution.py:113
  28.8 8.3 %copy-start.11 = (f32[8,6]{1,0:T(8,128)}, f32[8,6]{1,0:T(8,128)S(1)}, u32[]{:S(2)}) copy-start(f32[8,6]{1,0:T(8,128)S(1)} %copy.60) | copy-start | bytes 580
  40.1 0.7 copy-start.3
  49.4 5.9 %copy-start.17 = (s32[8]{0:T(128)S(1)}, s32[8]{0:T(128)}, u32[]{:S(2)}) copy-start(s32[8]{0:T(128)} %compare_select_fusion.1) | copy-start | bytes 100
  49.4 5.9 %copy-start.12 = (bf16[3,8,384]{2,1,0:T(8,128)(2,1)S(1)}, bf16[3,8,384]{2,1,0:T(8,128)(2,1)}, u32[]{:S(2)}) copy-start(bf16[3,8,384]{2,1,0:T(8,128)(2,1)} %param.17) | copy-start | bytes 55300
  49.4 11.9 %copy-start.14 = (pred[8]{0:T(512)(128)(4,1)S(1)}, pred[8]{0:T(512)(128)(4,1)}, u32[]{:S(2)}) copy-start(pred[8]{0:T(512)(128)(4,1)} %compare_and_fusion) | copy-start | bytes 28
  49.4 12.1 %copy-start.13 = (pred[8,8]{1,0:T(8,128)(4,1)S(1)}, pred[8,8]{1,0:T(8,128)(4,1)}, u32[]{:S(2)}) copy-start(pred[8,8]{1,0:T(8,128)(4,1)} %get-tuple-element.64) | copy-start | bytes 196
  61.5 3.3 %copy-start.7 = (f32[8,6,8,31]{3,1,2,0:T(8,128)S(1)}, f32[8,6,8,31]{3,1,2,0:T(8,128)}, u32[]{:S(2)}) copy-start(f32[8,6,8,31]{3,1,2,0:T(8,128)} %fusion.9) | copy-start | bytes 142852
  70.8 5.6 %copy-start.15 = (bf16[8,6]{1,0:T(8,128)(2,1)S(1)}, bf16[8,6]{1,0:T(8,128)(2,1)}, u32[]{:S(2)}) copy-start(bf16[8,6]{1,0:T(8,128)(2,1)} %param.18) | copy-start | bytes 292
  94.3 47.3 %all-to-all-start = ((bf16[8,256,384]{2,0,1:T(8,128)(2,1)}), bf16[8,256,384]{2,0,1:T(8,128)(2,1)}, u32[]{:S(2)}, u32[]{:S(2)}) async-start(bf16[8,256,384]{2,0,1:T(8,128)(2,1)} %copy.58), calls=%async_computation | async-start | bytes 3145728 | tf_op jit(solution)/shard_map/all_to_all | solution.py:112
where the time goes:
time: 146 us; the launch traced here: 144 us
  blocking collectives  65.2 us (45%)
  local copies, waits for them, and re-layouts  32.6 us (22%)
  other arithmetic  21.3 us (15%)
  matrix products  15.1 us (10%)
  starting transfers between devices  9.21 us (6%)
    all_gather x3, blocking collectives, merged(): pieces = jax.tree.map(lambda part: lax.all_gather(part, axis), value)  26.4 us
    psum x1, blocking collectives, shards(): layer_out = lax.psum(partial_out, 'head').astype(jnp.bfloat16)  20 us
    all_gather x1, blocking collectives, carried_in(): pieces = lax.all_gather(value, axis)  8.25 us
    unnamed x38, local copies, waits for them, and re-layouts  7.68 us
    another operation x4, other arithmetic  7.28 us
    another operation x1, local copies, waits for them, and re-layouts, shards(): key_rows = packed_keys.reshape(req_dev, rows_dev, heads_dev, head_size)  5.89 us
    another operation x1, local copies, waits for them, and re-layouts, shards(): value_rows = packed_values.reshape(req_dev, rows_dev, heads_dev, head_size)  5.89 us
    all_gather x1, blocking collectives, shards(): lax.all_gather(fresh, 'grp', axis=1, tiled=True)  5.3 us
  transfers between devices with their start and end apart: 2, of which 0 were waited for; matrix products, arithmetic and copies ran while one was open for 38% of the time, Pallas kernels for 0%

commit v1 on v0

v1 whole, which is shorter than its diff:
```python
import functools

import jax
import jax.numpy as jnp
from jax import lax
from jax.experimental import pallas as pl
from jax.experimental.pallas import tpu as pltpu
from jax.sharding import PartitionSpec as P

BLOCK = 64
SLOTS = 32
EMPTY_LOG = -10000.0
CHUNKS = 4
VMEM_LIMIT = 48 * 1024 * 1024


def dot(a, b):
    return lax.dot_general(a, b, (((1,), (0,)), ((), ())), preferred_element_type=jnp.float32)


def dot_nt(a, b):
    return lax.dot_general(a, b, (((1,), (1,)), ((), ())), preferred_element_type=jnp.float32)


def iota(shape, dim):
    return lax.broadcasted_iota(jnp.int32, shape, dim)


def three(x):
    hi = x.astype(jnp.bfloat16).astype(jnp.float32)
    rest = x - hi
    mid = rest.astype(jnp.bfloat16).astype(jnp.float32)
    return hi, mid, rest - mid


def split_dot(x, ones):
    rows = x.shape[0]
    parts = dot(jnp.concatenate(three(x), axis=0).astype(jnp.bfloat16), ones)
    return parts[:rows] + parts[rows : 2 * rows] + parts[2 * rows :]


def half_of(axis, count):
    own = lax.axis_index(axis) if count == 2 else jnp.int32(0)
    return own, 1 - own


def plan(keep, weight, start, len_ref):
    rows, width = keep.shape
    one, two = iota((width, width), 0), iota((width, width), 1)
    same = (one // BLOCK) == (two // BLOCK)
    upto = (same & (one <= two)).astype(jnp.float32).astype(jnp.bfloat16)
    block = same.astype(jnp.float32).astype(jnp.bfloat16)
    kept = keep == 1
    rank = dot(keep.astype(jnp.float32).astype(jnp.bfloat16), upto) - 1.0
    weighted = jnp.where(kept, 0.0, weight)
    share = (weighted / split_dot(weighted, block)).astype(jnp.bfloat16).astype(jnp.float32)
    lane, row = iota((rows, width), 1), iota((rows, width), 0)
    slot = jnp.where(kept, rank.astype(jnp.int32), SLOTS - 1) + (lane // BLOCK) * SLOTS
    length = jnp.zeros((rows, width), jnp.int32)
    for r in range(rows):
        length = jnp.where(row == r, len_ref[r], length)
    slot = jnp.where(start + lane < length, slot, -1)
    return slot, jnp.where(kept, 1.0, share)


def select(slot, factor, r):
    width = slot.shape[1]
    shape = (width // 2, width)
    hit = iota(shape, 0) == slot[r : r + 1, :]
    return jnp.where(hit, jnp.broadcast_to(factor[r : r + 1, :], shape), 0.0).astype(jnp.bfloat16)


def lanes(half, width):
    return pl.ds(pl.multiple_of(half * width, width), width)


def send_kernel(n_seq, first, count, len_ref, keep_ref, weight_ref, keys, values, out, buf, sem):
    _, sent = half_of("seq", n_seq)
    width = buf.shape[2]
    copies = []
    for i, source in enumerate((keys, values)):
        for j in range(count):
            copies.append(
                pltpu.make_async_copy(
                    source.at[first + j, lanes(sent, width), :], buf.at[i, j], sem.at[i, j]
                )
            )
    for copy in copies:
        copy.start()
    start = lax.axis_index("seq") * (2 * width) + sent * width
    slot, factor = plan(
        keep_ref[:, lanes(sent, width)], weight_ref[:, lanes(sent, width)], start, len_ref
    )
    chosen = [select(slot, factor, first + j) for j in range(count)]
    for i in range(2):
        for j in range(count):
            copies[i * count + j].wait()
            out[i, j] = dot(chosen[j], buf[i, j]).astype(jnp.bfloat16)


def send_part(n_seq, first, count, lengths, keep, weight, keys, values):
    req, pos, width = keys.shape
    half = pos // 2
    vmem = pl.BlockSpec(memory_space=pltpu.VMEM)
    hbm = pl.BlockSpec(memory_space=pl.ANY)
    return pl.pallas_call(
        functools.partial(send_kernel, n_seq, first, count),
        out_shape=jax.ShapeDtypeStruct((2, count, half // 2, width), jnp.bfloat16),
        in_specs=[pl.BlockSpec(memory_space=pltpu.SMEM), vmem, vmem, hbm, hbm],
        out_specs=vmem,
        scratch_shapes=[
            pltpu.VMEM((2, count, half, width), jnp.bfloat16),
            pltpu.SemaphoreType.DMA((2, count)),
        ],
        compiler_params=pltpu.CompilerParams(vmem_limit_bytes=VMEM_LIMIT),
        cost_estimate=pl.CostEstimate(
            flops=4 * count * half * half * width,
            bytes_accessed=6 * count * half * width,
            transcendentals=0,
        ),
        name="compact_sent",
    )(lengths, keep, weight, keys, values)


def main_kernel(
    n_seq, n_grp, n_chunk, len_ref, route_ref, keep_ref, weight_ref, forget_ref, keys, values, *rest
):
    chunks, rest = rest[:n_chunk], rest[n_chunk:]
    fresh, rest = rest[:n_grp], rest[n_grp:]
    out_k, out_v, log_ref, stats_ref, picked_ref = rest[:5]
    raw, own_rows, sent_rows, forget, logs, scores, sem_raw, sem_sent, sem_out = rest[5:]
    own, sent = half_of("seq", n_seq)
    seq = lax.axis_index("seq")
    req, heads, pos = forget_ref.shape
    half = pos // 2
    rows = half // 2
    width = keys.shape[2]
    size = width // heads
    pad = forget.shape[0] // req

    raw_copies = [
        [
            pltpu.make_async_copy(source.at[r, lanes(own, half), :], raw.at[i, r], sem_raw.at[i, r])
            for i, source in enumerate((keys, values))
        ]
        for r in range(req)
    ]
    for pair in raw_copies:
        for copy in pair:
            copy.start()
    count = req // n_chunk
    sent_copies = [
        pltpu.make_async_copy(
            chunks[c], sent_rows.at[:, pl.ds(c * count, count)], sem_sent.at[c]
        )
        for c in range(n_chunk)
    ]
    for copy in sent_copies:
        copy.start()

    kinds = 4 * req
    shape = (kinds, kinds)
    to, frm = iota(shape, 0), iota(shape, 1)
    wanted = jnp.zeros(shape, jnp.int32)
    for r in range(req):
        wanted = jnp.where(to % req == r, route_ref[r], wanted)
    me = lax.axis_index("grp")
    picked = jnp.zeros((kinds, width), jnp.float32)
    for k in range(n_grp):
        source = lax.rem(me + n_grp - k, n_grp)
        hit = (to // req == frm // req) & (wanted == source * req + frm % req)
        picked = picked + dot(hit.astype(jnp.float32).astype(jnp.bfloat16), fresh[k][...])
    picked_ref[...] = picked

    forget[...] = jnp.zeros_like(forget)
    lane = iota((heads, pos), 1)
    for r in range(req):
        live = seq * pos + lane < len_ref[r]
        forget[r * pad : r * pad + heads, :] = jnp.where(live, forget_ref[r], 0.0)
    gates = forget[...]
    total = jnp.sum(gates, axis=1, keepdims=True)
    one, two = iota((half, half), 0), iota((half, half), 1)
    after = ((one // BLOCK == two // BLOCK) & (one > two)).astype(jnp.float32).astype(jnp.bfloat16)
    ends = iota((pos, rows), 1) // SLOTS
    begins = iota((pos, rows), 0) // BLOCK
    last = iota((req * pad, rows), 1) % SLOTS == SLOTS - 1

    for i, h in enumerate((own, sent)):
        slot, factor = plan(
            keep_ref[:, lanes(h, half)], weight_ref[:, lanes(h, half)], seq * pos + h * half, len_ref
        )
        inner = split_dot(forget[:, lanes(h, half)], after)
        beyond = split_dot(
            gates, (begins > ends + h * (half // BLOCK)).astype(jnp.float32).astype(jnp.bfloat16)
        )
        spread = jnp.exp(inner)
        high = spread.astype(jnp.bfloat16).astype(jnp.float32)
        planes = three(inner) + (high, spread - high, jnp.ones_like(inner))
        found = []
        for r in range(req):
            chosen = select(slot, factor, r)
            stack = jnp.concatenate([x[r * pad : (r + 1) * pad] for x in planes], axis=0)
            found.append(dot_nt(stack.astype(jnp.bfloat16), chosen))
            if i == 0:
                for copy in raw_copies[r]:
                    copy.wait()
                own_rows[0, r] = dot(chosen, raw[0, r]).astype(jnp.bfloat16)
                own_rows[1, r] = dot(chosen, raw[1, r]).astype(jnp.bfloat16)
        at = [
            jnp.concatenate([x[p * pad : (p + 1) * pad] for x in found], axis=0) for p in range(6)
        ]
        filled = at[5] > 0.5
        kept = at[0] + at[1] + at[2]
        merged = jnp.log(jnp.where(filled, at[3] + at[4], 1.0))
        level = jnp.where(filled, jnp.where(last, merged, kept) + beyond, EMPTY_LOG)
        logs[:, i * rows : (i + 1) * rows] = level
        for r in range(req):
            log_ref[r, :, lanes(h, rows)] = level[r * pad : r * pad + heads]

    out_copies = [
        pltpu.make_async_copy(own_rows.at[i], out.at[:, lanes(own, rows), :], sem_out.at[i])
        for i, out in enumerate((out_k, out_v))
    ]
    for copy in out_copies:
        copy.start()
    for copy in sent_copies:
        copy.wait()

    mine = iota((pad, width), 0) == iota((pad, width), 1) // size
    for r in range(req):
        query = jnp.where(mine, picked[r : r + 1, :], 0.0).astype(jnp.bfloat16)
        here = slice(r * pad, (r + 1) * pad)
        scores[here, :rows] = dot_nt(query, own_rows[0, r])
        scores[here, rows:] = dot_nt(query, sent_rows[0, r])
    level = scores[...] * (size**-0.5) + logs[...]
    top = jnp.max(level, axis=1, keepdims=True)
    weights = jnp.exp(level - top).astype(jnp.bfloat16).astype(jnp.float32)
    mass = jnp.sum(weights, axis=1, keepdims=True)

    def spread_out(column, r):
        return jnp.sum(
            jnp.where(mine, column[r * pad : (r + 1) * pad], 0.0), axis=0, keepdims=True
        )

    for r in range(req):
        w = weights[r * pad : (r + 1) * pad].astype(jnp.bfloat16)
        acc = dot(w[:, :rows], own_rows[1, r]) + dot(w[:, rows:], sent_rows[1, r])
        acc = jnp.sum(jnp.where(mine, acc, 0.0), axis=0, keepdims=True)
        for p, row in enumerate(
            (spread_out(top, r), spread_out(mass, r), spread_out(total, r), acc)
        ):
            stats_ref[p * req + r : p * req + r + 1, :] = row
    for copy in out_copies:
        copy.wait()


def main_part(n_seq, n_grp, lengths, route, keep, weight, forget, keys, values, chunks, fresh):
    req, pos, width = keys.shape
    heads = forget.shape[1]
    half, rows, pad = pos // 2, pos // 4, -(-heads // 8) * 8
    n_chunk = len(chunks)
    vmem = pl.BlockSpec(memory_space=pltpu.VMEM)
    hbm = pl.BlockSpec(memory_space=pl.ANY)
    smem = pl.BlockSpec(memory_space=pltpu.SMEM)
    whole = jax.ShapeDtypeStruct((req, 2 * rows, width), jnp.bfloat16)
    return pl.pallas_call(
        functools.partial(main_kernel, n_seq, n_grp, n_chunk),
        out_shape=(
            whole,
            whole,
            jax.ShapeDtypeStruct((req, heads, 2 * rows), jnp.float32),
            jax.ShapeDtypeStruct((4 * req, width), jnp.float32),
            jax.ShapeDtypeStruct((4 * req, width), jnp.float32),
        ),
        in_specs=[smem, smem, vmem, vmem, vmem, hbm, hbm] + [hbm] * n_chunk + [vmem] * n_grp,
        out_specs=(hbm, hbm, vmem, vmem, vmem),
        scratch_shapes=[
            pltpu.VMEM((2, req, half, width), jnp.bfloat16),
            pltpu.VMEM((2, req, rows, width), jnp.bfloat16),
            pltpu.VMEM((2, req, rows, width), jnp.bfloat16),
            pltpu.VMEM((req * pad, pos), jnp.float32),
            pltpu.VMEM((req * pad, 2 * rows), jnp.float32),
            pltpu.VMEM((req * pad, 2 * rows), jnp.float32),
            pltpu.SemaphoreType.DMA((2, req)),
            pltpu.SemaphoreType.DMA((n_chunk,)),
            pltpu.SemaphoreType.DMA((2,)),
        ],
        compiler_params=pltpu.CompilerParams(vmem_limit_bytes=VMEM_LIMIT),
        cost_estimate=pl.CostEstimate(
            flops=8 * req * half * half * width,
            bytes_accessed=8 * req * half * width,
            transcendentals=4 * req * heads * pos,
        ),
        name="compact_own_and_attend",
    )(lengths, route, keep, weight, forget, keys, values, *chunks, *fresh)


def merge_kernel(count, relative, size, *refs):
    stats, (picked_ref, weight_ref, log_ref, decay_ref, out_ref) = refs[:count], refs[count:]
    req, heads, rows = log_ref.shape
    width = picked_ref.shape[1]
    seq = lax.axis_index("seq")
    places = [lax.rem(seq + count - k, count) if relative else jnp.int32(k) for k in range(count)]
    tops, masses, totals, accs = [
        [ref[p * req : (p + 1) * req, :] for ref in stats] for p in range(4)
    ]

    def later(place):
        total = jnp.zeros_like(totals[0])
        for k in range(count):
            total = total + jnp.where(places[k] > place, totals[k], 0.0)
        return total

    tops = [tops[k] + later(places[k]) for k in range(count)]
    top = functools.reduce(jnp.maximum, tops)
    scales = [jnp.exp(t - top) for t in tops]
    mass = sum(s * x for s, x in zip(scales, masses))
    acc = sum(s * x for s, x in zip(scales, accs))
    query, key, value, gate = [picked_ref[p * req : (p + 1) * req, :] for p in range(4)]
    one, two = iota((width, width), 0), iota((width, width), 1)
    same = (one // size == two // size).astype(jnp.float32).astype(jnp.bfloat16)
    own = split_dot(query * key, same) * (size**-0.5)
    past = top + gate
    joint = jnp.maximum(past, own)
    scale, self_weight = jnp.exp(past - joint), jnp.exp(own - joint)
    attended = (scale * acc + self_weight * value) / (scale * mass + self_weight)
    out_ref[...] = dot(attended.astype(jnp.bfloat16), weight_ref[...])

    beyond = later(seq)
    head = iota((heads, width), 0)
    first = head * size == iota((heads, width), 1)
    for r in range(req):
        column = jnp.sum(jnp.where(first, beyond[r : r + 1, :], 0.0), axis=1, keepdims=True)
        decay_ref[r] = jnp.exp(log_ref[r] + column)


def merge_part(stats, relative, picked, out_weight, logs, size):
    req = logs.shape[0]
    vmem = pl.BlockSpec(memory_space=pltpu.VMEM)
    return pl.pallas_call(
        functools.partial(merge_kernel, len(stats), relative, size),
        out_shape=(
            jax.ShapeDtypeStruct(logs.shape, jnp.float32),
            jax.ShapeDtypeStruct((req, out_weight.shape[1]), jnp.float32),
        ),
        in_specs=[vmem] * (len(stats) + 3),
        out_specs=(vmem, vmem),
        compiler_params=pltpu.CompilerParams(vmem_limit_bytes=VMEM_LIMIT),
        name="merge_and_project",
    )(*stats, picked, out_weight, logs)


def sum_kernel(count, *refs):
    parts, out = refs[:count], refs[count]
    me = lax.axis_index("head")
    total = jnp.zeros(out.shape, jnp.float32)
    for place in range(count):
        for k in range(count):
            total = total + jnp.where(lax.rem(me + count - k, count) == place, parts[k][...], 0.0)
    out[...] = total.astype(out.dtype)


def sum_part(parts):
    return pl.pallas_call(
        functools.partial(sum_kernel, len(parts)),
        out_shape=jax.ShapeDtypeStruct(parts[0].shape, jnp.bfloat16),
        in_specs=[pl.BlockSpec(memory_space=pltpu.VMEM)] * len(parts),
        out_specs=pl.BlockSpec(memory_space=pltpu.VMEM),
        name="sum_heads",
    )(*parts)


def place_kernel(n_seq, first, part, old_k, old_v, out_k, out_v, sem):
    _, sent = half_of("seq", n_seq)
    _, count, rows, _ = part.shape
    copies = [
        pltpu.make_async_copy(
            part.at[i, j], out.at[first + j, lanes(sent, rows), :], sem.at[i, j]
        )
        for i, out in enumerate((out_k, out_v))
        for j in range(count)
    ]
    for copy in copies:
        copy.start()
    for copy in copies:
        copy.wait()


def place_part(n_seq, first, part, out_k, out_v):
    hbm = pl.BlockSpec(memory_space=pl.ANY)
    shape = jax.ShapeDtypeStruct(out_k.shape, out_k.dtype)
    return pl.pallas_call(
        functools.partial(place_kernel, n_seq, first),
        out_shape=(shape, shape),
        in_specs=[hbm] * 3,
        out_specs=(hbm, hbm),
        scratch_shapes=[pltpu.SemaphoreType.DMA((2, part.shape[1]))],
        input_output_aliases={1: 0, 2: 1},
        name="place_received",
    )(part, out_k, out_v)


def others(value, axis):
    count = lax.axis_size(axis)
    return [value] + [
        lax.ppermute(value, axis, [(i, (i + k) % count) for i in range(count)])
        for k in range(1, count)
    ]


def shards(
    keys, values, log_forget, keep, merge_weight, lengths, route, fresh, new_forget, out_weight
):
    req, pos, width = keys.shape
    heads = log_forget.shape[1]
    size = width // heads
    n_seq, n_grp = lax.axis_size("seq"), lax.axis_size("grp")
    gates = jnp.repeat(new_forget, size, axis=1)
    tokens = others(jnp.concatenate([fresh.reshape(3 * req, width), gates], axis=0), "grp")
    count = req // CHUNKS
    chunks = [
        send_part(n_seq, c * count, count, lengths, keep, merge_weight, keys, values)
        for c in range(CHUNKS)
    ]
    if n_seq == 2:
        received = [lax.ppermute(x, "seq", [(0, 1), (1, 0)]) for x in chunks]
    else:
        received = chunks
    out_k, out_v, logs, stats, picked = main_part(
        n_seq, n_grp, lengths, route, keep, merge_weight, log_forget, keys, values, chunks, tokens
    )
    if n_seq == 2:
        all_stats = others(stats, "seq")
    else:
        gathered = lax.all_gather(stats, "seq")
        all_stats = [gathered[i] for i in range(n_seq)]
    decay, partial = merge_part(all_stats, n_seq == 2, picked, out_weight, logs, size)
    layer_out = sum_part(others(partial, "head"))
    for c in range(CHUNKS):
        out_k, out_v = place_part(n_seq, c * count, received[c], out_k, out_v)
    if n_seq != 2:
        out_k, out_v = (
            lax.all_to_all(x, "seq", split_axis=1, concat_axis=1, tiled=True) for x in (out_k, out_v)
        )
    return out_k, out_v, decay, layer_out


def solution(mesh):
    return jax.shard_map(
        shards,
        mesh=mesh,
        in_specs=(
            P("grp", "seq", "head"),
            P("grp", "seq", "head"),
            P("grp", "head", "seq"),
            P("grp", "seq"),
            P("grp", "seq"),
            P("grp"),
            P("grp"),
            P(None, "grp", "head"),
            P("grp", "head"),
            P("head", "seq"),
        ),
        out_specs=(
            P("grp", "seq", "head"),
            P("grp", "seq", "head"),
            P("grp", "head", "seq"),
            P("grp", "seq"),
        ),
        check_vma=False,
    )
```

time: 146 us -> 118 us (0.81)
  Pallas kernels: 0 us -> 72.5 us
  blocking collectives: 65.2 us -> 0 us
  local copies, waits for them, and re-layouts: 32.6 us -> 10.3 us
  other arithmetic: 21.3 us -> 0.74 us
  waiting for transfers between devices: 0.01 us -> 18.7 us
  matrix products: 15.1 us -> 0 us
  starting transfers between devices: 9.21 us -> 14.2 us
    pallas_call x0 -> x11, Pallas kernels: none -> 72.5 us  [the longest x4 52.2 us: place_part(): pl.pallas_call(functools.partial(place_kernel, n_seq, first), out_shape=(...]
    all_gather x6 -> x0, blocking collectives: 45.1 us -> none  [the longest x3 26.4 us: merged(): pieces = jax.tree.map(lambda part: lax.all_gather(part, axis), value)]
    psum x1 -> x0, blocking collectives: 20 us -> none  [shards(): layer_out = lax.psum(partial_out, 'head').astype(jnp.bfloat16)]
    ppermute x0 -> x11, waiting for transfers between devices: none -> 18.7 us  [the longest x7 18.7 us: others(): lax.ppermute(value, axis, [(i, (i + k) % count) for i in range(count)])]
    dot_general x6 -> x0, matrix products: 15.1 us -> none  [the longest x1 3.89 us: shards(): jnp.einsum('rbej,rbjc->rbec', select, key_blocks, preferred_element_type=...]
    ppermute x0 -> x11, starting transfers between devices: none -> 14.2 us  [the longest x7 8.94 us: others(): lax.ppermute(value, axis, [(i, (i + k) % count) for i in range(count)])]
    another operation x10 -> x0, local copies, waits for them, and re-layouts: 13.2 us -> none  [the longest x1 5.89 us: shards(): key_rows = packed_keys.reshape(req_dev, rows_dev, heads_dev, head_size)]
    all_to_all x2 -> x0, starting transfers between devices: 9.21 us -> none  [the longest x1 4.6 us: shards(): lax.all_to_all(packed_values, 'seq', split_axis=1, concat_axis=1, tiled=T...]
  transfers between devices with their start and end apart: 2 -> 11, of which waited for: 0 -> 7; matrix products, arithmetic and copies ran while one was open for 38% -> 4% of each run, Pallas kernels for 0% -> 48%
where the time goes in v1:
time: 118 us; the launch traced here: 117 us
  Pallas kernels  72.5 us (61%)
  waiting for transfers between devices  18.7 us (16%)
  starting transfers between devices  14.2 us (12%)
  local copies, waits for them, and re-layouts  10.3 us (9%)
    pallas_call x4, Pallas kernels, place_part(): pl.pallas_call(functools.partial(place_kernel, n_seq, first), out_shape=(...  52.2 us
    ppermute x7, waiting for transfers between devices, others(): lax.ppermute(value, axis, [(i, (i + k) % count) for i in range(count)])  18.7 us
    pallas_call x4, Pallas kernels, send_part(): pl.pallas_call(functools.partial(send_kernel, n_seq, first, count), out_s...  11.9 us
    ppermute x7, starting transfers between devices, others(): lax.ppermute(value, axis, [(i, (i + k) % count) for i in range(count)])  8.94 us
    unnamed x32, local copies, waits for them, and re-layouts  8.22 us
    pallas_call x1, Pallas kernels, main_part(): pl.pallas_call(functools.partial(main_kernel, n_seq, n_grp, n_chunk), out...  6.6 us
    ppermute x4, starting transfers between devices, shards(): received = [lax.ppermute(x, 'seq', [(0, 1), (1, 0)]) for x in chunks]  5.25 us
  transfers between devices with their start and end apart: 11, of which 7 were waited for; matrix products, arithmetic and copies ran while one was open for 4% of the time, Pallas kernels for 48%

profile of v1, /device:TPU:0, one launch (start us, length us, event | category | flops | bytes accessed | tf_op | source)
XLA Modules:
  0.0 117.2 jit_solution(4697589440195989964)
XLA Ops:
  0.6 0.0 copy-start
  0.6 1.9 %copy-done = bf16[8,512,384]{2,1,0:T(8,128)(2,1)S(1)} copy-done((bf16[8,512,384]{2,1,0:T(8,128)(2,1)S(1)}, bf16[8,512,384]{2,1,0:T(8,128)(2,1)}, u32[]{:S(2)}) %copy-start) | copy-done | bytes 3145752
  2.5 0.7 copy-done.3
  3.2 0.7 copy-done.5
  4.0 0.7 copy-done.8
  4.6 3.2 %compact_sent.7.rest_0_ = bf16[2,2,128,384]{3,2,1,0:T(8,128)(2,1)} custom-call(s32[8]{0:T(128)S(1)} %copy-done.8, s32[8,512]{1,0:T(8,128)S(1)} %copy-done.3, f32[8,512]{1,0:T(8,128)S(1)} %copy-done.5, bf16[8,512,384]{2,1,0:T(8,128)(2,1)S(1)} %copy-done, bf16[8,512,384]{2,1,0:T(8,128)(2,1)} %values.9), custom_call_target="tpu_custom_call" | custom-call | flops 201326592 | bytes 1179648 | tf_op jit(solution)/shard_map/compact_sent/pallas_call | solution.py:106
  7.8 3.0 %collective-permute-start.3 = (bf16[2,2,128,384]{3,2,1,0:T(8,128)(2,1)}, bf16[2,2,128,384]{3,2,1,0:T(8,128)(2,1)}, u32[]{:S(2)}, u32[]{:S(2)}) collective-permute-start(bf16[2,2,128,384]{3,2,1,0:T(8,128)(2,1)} %compact_sent.7.rest_0_), channel_id=1, source_target_pairs={{0,4},{4,0},{1,5},{5,1},{2,6},{6,2},{3,7},{7,3},{8,12},{12,8},{9,1... | collective-permute-start | bytes 1179656 | tf_op jit(solution)/shard_map/ppermute | solution.py:426
  10.8 3.2 %compact_sent.6.rest_1_ = bf16[2,2,128,384]{3,2,1,0:T(8,128)(2,1)} custom-call(s32[8]{0:T(128)S(1)} %copy-done.8, s32[8,512]{1,0:T(8,128)S(1)} %copy-done.3, f32[8,512]{1,0:T(8,128)S(1)} %copy-done.5, bf16[8,512,384]{2,1,0:T(8,128)(2,1)S(1)} %copy-done, bf16[8,512,384]{2,1,0:T(8,128)(2,1)} %values.9), custom_call_target="tpu_custom_call" | custom-call | flops 201326592 | bytes 1179648 | tf_op jit(solution)/shard_map/compact_sent/pallas_call | solution.py:106
  13.9 0.1 collective-permute-start.2
  14.0 3.2 %compact_sent.5.rest_2_ = bf16[2,2,128,384]{3,2,1,0:T(8,128)(2,1)} custom-call(s32[8]{0:T(128)S(1)} %copy-done.8, s32[8,512]{1,0:T(8,128)S(1)} %copy-done.3, f32[8,512]{1,0:T(8,128)S(1)} %copy-done.5, bf16[8,512,384]{2,1,0:T(8,128)(2,1)S(1)} %copy-done, bf16[8,512,384]{2,1,0:T(8,128)(2,1)} %values.9), custom_call_target="tpu_custom_call" | custom-call | flops 201326592 | bytes 1179648 | tf_op jit(solution)/shard_map/compact_sent/pallas_call | solution.py:106
  17.2 0.0 copy-start.14
  17.2 0.0 copy-start.4
  17.2 2.1 %collective-permute-start.1 = (bf16[2,2,128,384]{3,2,1,0:T(8,128)(2,1)}, bf16[2,2,128,384]{3,2,1,0:T(8,128)(2,1)}, u32[]{:S(2)}, u32[]{:S(2)}) collective-permute-start(bf16[2,2,128,384]{3,2,1,0:T(8,128)(2,1)} %compact_sent.5.rest_2_), channel_id=1, source_target_pairs={{0,4},{4,0},{1,5},{5,1},{2,6},{6,2},{3,7},{7,3},{8,12},{12,8},{9,1... | collective-permute-start | bytes 1179656 | tf_op jit(solution)/shard_map/ppermute | solution.py:426
  19.3 2.4 %compact_sent.4.rest_3_ = bf16[2,2,128,384]{3,2,1,0:T(8,128)(2,1)S(1)} custom-call(s32[8]{0:T(128)S(1)} %copy-done.8, s32[8,512]{1,0:T(8,128)S(1)} %copy-done.3, f32[8,512]{1,0:T(8,128)S(1)} %copy-done.5, bf16[8,512,384]{2,1,0:T(8,128)(2,1)S(1)} %copy-done, bf16[8,512,384]{2,1,0:T(8,128)(2,1)} %values.9), custom_call_target="tpu_custom_call" | custom-call | flops 201326592 | bytes 1179648 | tf_op jit(solution)/shard_map/compact_sent/pallas_call | solution.py:106
  21.7 0.1 collective-permute-start
  21.8 0.7 broadcast_in_dim.3
  22.5 1.4 %reshape.15 = bf16[8,384]{1,0:T(8,128)(2,1)} reshape(bf16[8,6,64]{2,1,0:T(8,128)(2,1)} %broadcast_in_dim.3) | data formatting | bytes 12288 | tf_op jit(solution)/shard_map/reshape | solution.py:418
  23.9 0.7 pad_maximum_fusion.rest_4_
  24.6 3.2 %collective-permute-done.4.rest_5_ = bf16[32,384]{1,0:T(8,128)(2,1)S(1)} collective-permute-done((bf16[32,384]{1,0:T(8,128)(2,1)S(1)}, bf16[32,384]{1,0:T(8,128)(2,1)S(1)}, u32[]{:S(2)}, u32[]{:S(2)}) %collective-permute-start.4) | collective-permute-done | bytes 24608 | tf_op jit(solution)/shard_map/ppermute | solution.py:406
  27.9 2.0 %collective-permute-start.5 = (bf16[32,384]{1,0:T(8,128)(2,1)S(1)}, bf16[32,384]{1,0:T(8,128)(2,1)S(1)}, u32[]{:S(2)}, u32[]{:S(2)}) collective-permute-start(bf16[32,384]{1,0:T(8,128)(2,1)S(1)} %pad_maximum_fusion.rest_4_), channel_id=1, source_target_pairs={{0,16},{8,24},{16,0},{24,8},{1,17},{9,25},{17,1},{25,9},{2,18},{10... | collective-permute-start | bytes 73736 | tf_op jit(solution)/shard_map/ppermute | solution.py:406
  29.9 1.8 %collective-permute-done.5.rest_6_ = bf16[32,384]{1,0:T(8,128)(2,1)S(1)} collective-permute-done((bf16[32,384]{1,0:T(8,128)(2,1)S(1)}, bf16[32,384]{1,0:T(8,128)(2,1)S(1)}, u32[]{:S(2)}, u32[]{:S(2)}) %collective-permute-start.5) | collective-permute-done | bytes 24608 | tf_op jit(solution)/shard_map/ppermute | solution.py:406
  31.7 0.0 collective-permute-start.6
  31.7 1.0 copy.24.forget_ref
  32.7 0.0 copy-start.2
  32.7 0.6 collective-permute-done.6.rest_7_
  33.3 0.7 copy-done.6
  34.0 0.7 copy-done.9
  34.6 0.7 copy-done.10
  35.3 6.6 %compact_own_and_attend.1 = (bf16[8,256,384]{2,1,0:T(8,128)(2,1)}, bf16[8,256,384]{2,1,0:T(8,128)(2,1)}, f32[8,6,256]{2,1,0:T(8,128)S(1)}, f32[32,384]{1,0:T(8,128)S(1)}, f32[32,384]{1,0:T(8,128)S(1)}) custom-call(s32[8]{0:T(128)S(1)} %copy-done.9, s32[8]{0:T(128)S(1)} %copy-done.10, s32[8,512]{1,0:T(8,128)S(1)} %copy-done.4, f32[8,512]{1,0:T(8,128)S(1)} %copy-done.6, ...), custom_call_target="tpu_custom_call" | custom-call | flops 1610612736 | bytes 6291456 | tf_op jit(solution)/shard_map/compact_own_and_attend/pallas_call | solution.py:266
  41.9 2.0 %collective-permute-start.7 = (f32[32,384]{1,0:T(8,128)S(1)}, f32[32,384]{1,0:T(8,128)S(1)}, u32[]{:S(2)}, u32[]{:S(2)}) collective-permute-start(f32[32,384]{1,0:T(8,128)S(1)} %get-tuple-element.29.refs_0_), channel_id=1, source_target_pairs={{0,4},{4,0},{1,5},{5,1},{2,6},{6,2},{3,7},{7,3},{8,12},{12,8},{9,1... | collective-permute-start | bytes 147464 | tf_op jit(solution)/shard_map/ppermute | solution.py:406
  43.9 2.1 %collective-permute-done.7.refs_1_ = f32[32,384]{1,0:T(8,128)S(1)} collective-permute-done((f32[32,384]{1,0:T(8,128)S(1)}, f32[32,384]{1,0:T(8,128)S(1)}, u32[]{:S(2)}, u32[]{:S(2)}) %collective-permute-start.7) | collective-permute-done | bytes 49184 | tf_op jit(solution)/shard_map/ppermute | solution.py:406
  46.1 0.3 merge_and_project.1
  46.4 4.1 %collective-permute-start.10 = (f32[8,768]{1,0:T(8,128)S(1)}, f32[8,768]{1,0:T(8,128)S(1)}, u32[]{:S(2)}, u32[]{:S(2)}) collective-permute-start(f32[8,768]{1,0:T(8,128)S(1)} %get-tuple-element.33.refs_0_), channel_id=1, source_target_pairs={{0,3},{1,0},{2,1},{3,2},{4,7},{5,4},{6,5},{7,6},{8,11},{9,8},{10,9... | collective-permute-start | bytes 73736 | tf_op jit(solution)/shard_map/ppermute | solution.py:406
  50.5 1.5 %collective-permute-done.10.refs_3_ = f32[8,768]{1,0:T(8,128)S(1)} collective-permute-done((f32[8,768]{1,0:T(8,128)S(1)}, f32[8,768]{1,0:T(8,128)S(1)}, u32[]{:S(2)}, u32[]{:S(2)}) %collective-permute-start.10) | collective-permute-done | bytes 24608 | tf_op jit(solution)/shard_map/ppermute | solution.py:406
  52.0 0.4 collective-permute-start.8
  52.5 5.6 %collective-permute-done.8.refs_1_ = f32[8,768]{1,0:T(8,128)S(1)} collective-permute-done((f32[8,768]{1,0:T(8,128)S(1)}, f32[8,768]{1,0:T(8,128)S(1)}, u32[]{:S(2)}, u32[]{:S(2)}) %collective-permute-start.8) | collective-permute-done | bytes 24608 | tf_op jit(solution)/shard_map/ppermute | solution.py:406
  58.1 0.3 collective-permute-start.9
  58.4 0.6 copy.25
  59.0 3.8 %collective-permute-done.9.refs_2_ = f32[8,768]{1,0:T(8,128)S(1)} collective-permute-done((f32[8,768]{1,0:T(8,128)S(1)}, f32[8,768]{1,0:T(8,128)S(1)}, u32[]{:S(2)}, u32[]{:S(2)}) %collective-permute-start.9) | collective-permute-done | bytes 24608 | tf_op jit(solution)/shard_map/ppermute | solution.py:406
  62.9 0.6 copy-done.13
  63.5 1.4 %sum_heads.1 = bf16[8,768]{1,0:T(8,128)(2,1)} custom-call(f32[8,768]{1,0:T(8,128)} %copy-done.7, f32[8,768]{1,0:T(8,128)} %copy-done.12, f32[8,768]{1,0:T(8,128)} %copy-done.13, f32[8,768]{1,0:T(8,128)} %copy-done.11), custom_call_target="tpu_custom_call" | custom-call | tf_op jit(solution)/shard_map/sum_heads/pallas_call | solution.py:364
  64.9 0.0 collective-permute-done.3.part
  64.9 13.0 %place_received.4 = (bf16[8,256,384]{2,1,0:T(8,128)(2,1)}, bf16[8,256,384]{2,1,0:T(8,128)(2,1)}) custom-call(bf16[2,2,128,384]{3,2,1,0:T(8,128)(2,1)} %collective-permute-done.3.part, bf16[8,256,384]{2,1,0:T(8,128)(2,1)} %get-tuple-element.19.old_k, bf16[8,256,384]{2,1,0:T(8,128)(2,1)} %get-tuple-element.20.old_v), custom_call_target="tpu_custom_call", output_to_operand_aliasing={{0}: (1, {}), {1}: (2, {})} | custom-call | tf_op jit(solution)/shard_map/place_received/pallas_call | solution.py:392
  77.9 0.0 collective-permute-done.2.part
  78.0 13.1 %place_received.5 = (bf16[8,256,384]{2,1,0:T(8,128)(2,1)}, bf16[8,256,384]{2,1,0:T(8,128)(2,1)}) custom-call(bf16[2,2,128,384]{3,2,1,0:T(8,128)(2,1)} %collective-permute-done.2.part, bf16[8,256,384]{2,1,0:T(8,128)(2,1)} %get-tuple-element.21.old_k, bf16[8,256,384]{2,1,0:T(8,128)(2,1)} %get-tuple-element.22.old_v), custom_call_target="tpu_custom_call", output_to_operand_aliasing={{0}: (1, {}), {1}: (2, {})} | custom-call | tf_op jit(solution)/shard_map/place_received/pallas_call | solution.py:392
  91.0 0.0 collective-permute-done.1.part
  91.0 13.1 %place_received.6 = (bf16[8,256,384]{2,1,0:T(8,128)(2,1)}, bf16[8,256,384]{2,1,0:T(8,128)(2,1)}) custom-call(bf16[2,2,128,384]{3,2,1,0:T(8,128)(2,1)} %collective-permute-done.1.part, bf16[8,256,384]{2,1,0:T(8,128)(2,1)} %get-tuple-element.23.old_k, bf16[8,256,384]{2,1,0:T(8,128)(2,1)} %get-tuple-element.24.old_v), custom_call_target="tpu_custom_call", output_to_operand_aliasing={{0}: (1, {}), {1}: (2, {})} | custom-call | tf_op jit(solution)/shard_map/place_received/pallas_call | solution.py:392
  104.1 13.1 %place_received.7 = (bf16[8,256,384]{2,1,0:T(8,128)(2,1)}, bf16[8,256,384]{2,1,0:T(8,128)(2,1)}) custom-call(bf16[2,2,128,384]{3,2,1,0:T(8,128)(2,1)} %collective-permute-done.part, bf16[8,256,384]{2,1,0:T(8,128)(2,1)} %get-tuple-element.25.old_k, bf16[8,256,384]{2,1,0:T(8,128)(2,1)} %get-tuple-element.26.old_v), custom_call_target="tpu_custom_call", output_to_operand_aliasing={{0}: (1, {}), {1}: (2, {})} | custom-call | tf_op jit(solution)/shard_map/place_received/pallas_call | solution.py:392
  (20 shorter events, 0.0 us)
Async XLA Ops:
  0.6 1.9 %copy-start = (bf16[8,512,384]{2,1,0:T(8,128)(2,1)S(1)}, bf16[8,512,384]{2,1,0:T(8,128)(2,1)}, u32[]{:S(2)}) copy-start(bf16[8,512,384]{2,1,0:T(8,128)(2,1)} %keys.9) | copy-start | bytes 9437188
  2.5 0.7 copy-start.3
  3.2 0.7 copy-start.5
  4.0 0.7 copy-start.8
  7.8 57.1 %collective-permute-start.3 = (bf16[2,2,128,384]{3,2,1,0:T(8,128)(2,1)}, bf16[2,2,128,384]{3,2,1,0:T(8,128)(2,1)}, u32[]{:S(2)}, u32[]{:S(2)}) collective-permute-start(bf16[2,2,128,384]{3,2,1,0:T(8,128)(2,1)} %compact_sent.7.rest_0_), channel_id=1, source_target_pairs={{0,4},{4,0},{1,5},{5,1},{2,6},{6,2},{3,7},{7,3},{8,12},{12,8},{9,1... | collective-permute-start | bytes 1179656 | tf_op jit(solution)/shard_map/ppermute | solution.py:426
  13.9 64.0 %collective-permute-start.2 = (bf16[2,2,128,384]{3,2,1,0:T(8,128)(2,1)}, bf16[2,2,128,384]{3,2,1,0:T(8,128)(2,1)}, u32[]{:S(2)}, u32[]{:S(2)}) collective-permute-start(bf16[2,2,128,384]{3,2,1,0:T(8,128)(2,1)} %compact_sent.6.rest_1_), channel_id=1, source_target_pairs={{0,4},{4,0},{1,5},{5,1},{2,6},{6,2},{3,7},{7,3},{8,12},{12,8},{9,1... | collective-permute-start | bytes 1179656 | tf_op jit(solution)/shard_map/ppermute | solution.py:426
  17.2 4.6 %copy-start.14 = (bf16[8,6]{1,0:T(8,128)(2,1)S(1)}, bf16[8,6]{1,0:T(8,128)(2,1)}, u32[]{:S(2)}) copy-start(bf16[8,6]{1,0:T(8,128)(2,1)} %param.18) | copy-start | bytes 292
  17.2 16.0 %copy-start.4 = (s32[8,512]{1,0:T(8,128)S(1)}, s32[8,512]{1,0:T(8,128)}, u32[]{:S(2)}) copy-start(s32[8,512]{1,0:T(8,128)} %keep_ref.9) | copy-start | bytes 49156
  17.2 73.8 %collective-permute-start.1 = (bf16[2,2,128,384]{3,2,1,0:T(8,128)(2,1)}, bf16[2,2,128,384]{3,2,1,0:T(8,128)(2,1)}, u32[]{:S(2)}, u32[]{:S(2)}) collective-permute-start(bf16[2,2,128,384]{3,2,1,0:T(8,128)(2,1)} %compact_sent.5.rest_2_), channel_id=1, source_target_pairs={{0,4},{4,0},{1,5},{5,1},{2,6},{6,2},{3,7},{7,3},{8,12},{12,8},{9,1... | collective-permute-start | bytes 1179656 | tf_op jit(solution)/shard_map/ppermute | solution.py:426
  19.3 14.0 %copy-start.1 = (bf16[8,512,384]{2,1,0:T(8,128)(2,1)S(1)}, bf16[8,512,384]{2,1,0:T(8,128)(2,1)}, u32[]{:S(2)}) copy-start(bf16[8,512,384]{2,1,0:T(8,128)(2,1)} %keys.9) | copy-start | bytes 9437188
  21.7 82.4 %collective-permute-start = (bf16[2,2,128,384]{3,2,1,0:T(8,128)(2,1)S(1)}, bf16[2,2,128,384]{3,2,1,0:T(8,128)(2,1)}, u32[]{:S(2)}, u32[]{:S(2)}) collective-permute-start(bf16[2,2,128,384]{3,2,1,0:T(8,128)(2,1)S(1)} %compact_sent.4.rest_3_), channel_id=1, source_target_pairs={{0,4},{4,0},{1,5},{5,1},{2,6},{6,2},{3,7},{7,3},{8,12},{12,8},{9,1... | collective-permute-start | bytes 1179656 | tf_op jit(solution)/shard_map/ppermute | solution.py:426
  24.6 3.3 %collective-permute-start.4 = (bf16[32,384]{1,0:T(8,128)(2,1)S(1)}, bf16[32,384]{1,0:T(8,128)(2,1)S(1)}, u32[]{:S(2)}, u32[]{:S(2)}) collective-permute-start(bf16[32,384]{1,0:T(8,128)(2,1)S(1)} %pad_maximum_fusion.rest_4_), channel_id=1, source_target_pairs={{0,8},{8,16},{16,24},{24,0},{1,9},{9,17},{17,25},{25,1},{2,10},{10... | collective-permute-start | bytes 73736 | tf_op jit(solution)/shard_map/ppermute | solution.py:406
  27.9 3.8 %collective-permute-start.5 = (bf16[32,384]{1,0:T(8,128)(2,1)S(1)}, bf16[32,384]{1,0:T(8,128)(2,1)S(1)}, u32[]{:S(2)}, u32[]{:S(2)}) collective-permute-start(bf16[32,384]{1,0:T(8,128)(2,1)S(1)} %pad_maximum_fusion.rest_4_), channel_id=1, source_target_pairs={{0,16},{8,24},{16,0},{24,8},{1,17},{9,25},{17,1},{25,9},{2,18},{10... | collective-permute-start | bytes 73736 | tf_op jit(solution)/shard_map/ppermute | solution.py:406
  31.7 1.5 %collective-permute-start.6 = (bf16[32,384]{1,0:T(8,128)(2,1)S(1)}, bf16[32,384]{1,0:T(8,128)(2,1)S(1)}, u32[]{:S(2)}, u32[]{:S(2)}) collective-permute-start(bf16[32,384]{1,0:T(8,128)(2,1)S(1)} %pad_maximum_fusion.rest_4_), channel_id=1, source_target_pairs={{0,24},{8,0},{16,8},{24,16},{1,25},{9,1},{17,9},{25,17},{2,26},{10... | collective-permute-start | bytes 73736 | tf_op jit(solution)/shard_map/ppermute | solution.py:406
  32.7 13.4 %copy-start.2 = (bf16[384,768]{1,0:T(8,128)(2,1)S(1)}, bf16[384,768]{1,0:T(8,128)(2,1)}, u32[]{:S(2)}) copy-start(bf16[384,768]{1,0:T(8,128)(2,1)} %refs_3_.1) | copy-start | bytes 1769476
  33.3 0.7 copy-start.6
  34.0 0.7 copy-start.9
  34.6 0.7 copy-start.10
  41.9 4.2 %collective-permute-start.7 = (f32[32,384]{1,0:T(8,128)S(1)}, f32[32,384]{1,0:T(8,128)S(1)}, u32[]{:S(2)}, u32[]{:S(2)}) collective-permute-start(f32[32,384]{1,0:T(8,128)S(1)} %get-tuple-element.29.refs_0_), channel_id=1, source_target_pairs={{0,4},{4,0},{1,5},{5,1},{2,6},{6,2},{3,7},{7,3},{8,12},{12,8},{9,1... | collective-permute-start | bytes 147464 | tf_op jit(solution)/shard_map/ppermute | solution.py:406
  46.4 16.4 %copy-start.7 = (f32[8,768]{1,0:T(8,128)}, f32[8,768]{1,0:T(8,128)S(1)}, u32[]{:S(2)}) copy-start(f32[8,768]{1,0:T(8,128)S(1)} %get-tuple-element.33.refs_0_) | copy-start | bytes 73732
  46.4 5.6 %collective-permute-start.10 = (f32[8,768]{1,0:T(8,128)S(1)}, f32[8,768]{1,0:T(8,128)S(1)}, u32[]{:S(2)}, u32[]{:S(2)}) collective-permute-start(f32[8,768]{1,0:T(8,128)S(1)} %get-tuple-element.33.refs_0_), channel_id=1, source_target_pairs={{0,3},{1,0},{2,1},{3,2},{4,7},{5,4},{6,5},{7,6},{8,11},{9,8},{10,9... | collective-permute-start | bytes 73736 | tf_op jit(solution)/shard_map/ppermute | solution.py:406
  52.0 10.8 %copy-start.11 = (f32[8,768]{1,0:T(8,128)}, f32[8,768]{1,0:T(8,128)S(1)}, u32[]{:S(2)}) copy-start(f32[8,768]{1,0:T(8,128)S(1)} %collective-permute-done.10.refs_3_) | copy-start | bytes 73732
  52.0 6.1 %collective-permute-start.8 = (f32[8,768]{1,0:T(8,128)S(1)}, f32[8,768]{1,0:T(8,128)S(1)}, u32[]{:S(2)}, u32[]{:S(2)}) collective-permute-start(f32[8,768]{1,0:T(8,128)S(1)} %get-tuple-element.33.refs_0_), channel_id=1, source_target_pairs={{0,1},{1,2},{2,3},{3,0},{4,5},{5,6},{6,7},{7,4},{8,9},{9,10},{10,1... | collective-permute-start | bytes 73736 | tf_op jit(solution)/shard_map/ppermute | solution.py:406
  58.1 4.7 %copy-start.12 = (f32[8,768]{1,0:T(8,128)}, f32[8,768]{1,0:T(8,128)S(1)}, u32[]{:S(2)}) copy-start(f32[8,768]{1,0:T(8,128)S(1)} %collective-permute-done.8.refs_1_) | copy-start | bytes 73732
  58.1 4.7 %collective-permute-start.9 = (f32[8,768]{1,0:T(8,128)S(1)}, f32[8,768]{1,0:T(8,128)S(1)}, u32[]{:S(2)}, u32[]{:S(2)}) collective-permute-start(f32[8,768]{1,0:T(8,128)S(1)} %get-tuple-element.33.refs_0_), channel_id=1, source_target_pairs={{0,2},{1,3},{2,0},{3,1},{4,6},{5,7},{6,4},{7,5},{8,10},{9,11},{10,... | collective-permute-start | bytes 73736 | tf_op jit(solution)/shard_map/ppermute | solution.py:406
  62.9 0.6 copy-start.13

commit v2 on v1

--- a/solution.py
+++ b/solution.py
@@ -9,9 +9,17 @@
 
 BLOCK = 64
 SLOTS = 32
+LANES = 128
+BLOCK_LOG = BLOCK.bit_length() - 1
+SLOT_LOG = SLOTS.bit_length() - 1
 EMPTY_LOG = -10000.0
-CHUNKS = 4
-VMEM_LIMIT = 48 * 1024 * 1024
+FIRST = 4
+VMEM_LIMIT = 63 * 1024 * 1024
+MAIN_LIMIT = 63 * 1024 * 1024
+SMALL_LIMIT = 8 * 1024 * 1024
+
+
+LIGHT = pl.CostEstimate(flops=1, bytes_accessed=1, transcendentals=0)
 
 
 def dot(a, b):
@@ -44,10 +52,17 @@
     return own, 1 - own
 
 
+def by_row(ref, row):
+    picked = jnp.zeros_like(row)
+    for r in range(ref.shape[0]):
+        picked = jnp.where(row == r, ref[r], picked)
+    return picked
+
+
 def plan(keep, weight, start, len_ref):
     rows, width = keep.shape
     one, two = iota((width, width), 0), iota((width, width), 1)
-    same = (one // BLOCK) == (two // BLOCK)
+    same = (one ^ two) < BLOCK
     upto = (same & (one <= two)).astype(jnp.float32).astype(jnp.bfloat16)
     block = same.astype(jnp.float32).astype(jnp.bfloat16)
     kept = keep == 1
@@ -55,11 +70,8 @@
     weighted = jnp.where(kept, 0.0, weight)
     share = (weighted / split_dot(weighted, block)).astype(jnp.bfloat16).astype(jnp.float32)
     lane, row = iota((rows, width), 1), iota((rows, width), 0)
-    slot = jnp.where(kept, rank.astype(jnp.int32), SLOTS - 1) + (lane // BLOCK) * SLOTS
-    length = jnp.zeros((rows, width), jnp.int32)
-    for r in range(rows):
-        length = jnp.where(row == r, len_ref[r], length)
-    slot = jnp.where(start + lane < length, slot, -1)
+    slot = jnp.where(kept, rank.astype(jnp.int32), SLOTS - 1) + (lane >> BLOCK_LOG) * SLOTS
+    slot = jnp.where(start + lane < by_row(len_ref, row), slot, -1)
     return slot, jnp.where(kept, 1.0, share)
 
 
@@ -74,12 +86,16 @@
     return pl.ds(pl.multiple_of(half * width, width), width)
 
 
-def send_kernel(n_seq, first, count, len_ref, keep_ref, weight_ref, keys, values, out, buf, sem):
+def send_kernel(n_seq, first, count, len_ref, keep_ref, weight_ref, keys, values, *rest):
+    if first == 0:
+        *tokens, out, packed, buf, sem = rest
+    else:
+        _, out, buf, sem = rest
     _, sent = half_of("seq", n_seq)
     width = buf.shape[2]
     copies = []
-    for i, source in enumerate((keys, values)):
-        for j in range(count):
+    for j in range(count):
+        for i, source in enumerate((keys, values)):
             copies.append(
                 pltpu.make_async_copy(
                     source.at[first + j, lanes(sent, width), :], buf.at[i, j], sem.at[i, j]
@@ -91,35 +107,45 @@
     slot, factor = plan(
         keep_ref[:, lanes(sent, width)], weight_ref[:, lanes(sent, width)], start, len_ref
     )
-    chosen = [select(slot, factor, first + j) for j in range(count)]
-    for i in range(2):
-        for j in range(count):
-            copies[i * count + j].wait()
-            out[i, j] = dot(chosen[j], buf[i, j]).astype(jnp.bfloat16)
-
-
-def send_part(n_seq, first, count, lengths, keep, weight, keys, values):
+    if first == 0:
+        fresh, gates = tokens[0][...].astype(jnp.float32), tokens[1][...].astype(jnp.float32)
+        req, heads = gates.shape
+        lane = iota((req, fresh.shape[1]), 1)
+        size = fresh.shape[1] // heads
+        spread = jnp.zeros((req, fresh.shape[1]), jnp.float32)
+        for h in range(heads):
+            inside = (lane >= h * size) & (lane < (h + 1) * size)
+            spread = jnp.where(inside, gates[:, h : h + 1], spread)
+        packed[...] = jnp.concatenate([fresh, spread], axis=0).astype(jnp.bfloat16)
+    for j in range(count):
+        chosen = select(slot, factor, first + j)
+        for i in range(2):
+            copies[j * 2 + i].wait()
+            out[i, j] = dot(chosen, buf[i, j]).astype(jnp.bfloat16)
+
+
+def send_part(n_seq, first, count, lengths, keep, weight, keys, values, extra):
     req, pos, width = keys.shape
     half = pos // 2
     vmem = pl.BlockSpec(memory_space=pltpu.VMEM)
     hbm = pl.BlockSpec(memory_space=pl.ANY)
+    shapes = [jax.ShapeDtypeStruct((2, count, half // 2, width), jnp.bfloat16)]
+    if first == 0:
+        shapes.append(jax.ShapeDtypeStruct((extra[0].shape[0] + req, width), jnp.bfloat16))
     return pl.pallas_call(
         functools.partial(send_kernel, n_seq, first, count),
-        out_shape=jax.ShapeDtypeStruct((2, count, half // 2, width), jnp.bfloat16),
-        in_specs=[pl.BlockSpec(memory_space=pltpu.SMEM), vmem, vmem, hbm, hbm],
-        out_specs=vmem,
+        out_shape=tuple(shapes),
+        in_specs=[pl.BlockSpec(memory_space=pltpu.SMEM), vmem, vmem, hbm, hbm]
+        + ([vmem] * 2 if first == 0 else [hbm]),
+        out_specs=(vmem,) * len(shapes),
         scratch_shapes=[
             pltpu.VMEM((2, count, half, width), jnp.bfloat16),
             pltpu.SemaphoreType.DMA((2, count)),
         ],
         compiler_params=pltpu.CompilerParams(vmem_limit_bytes=VMEM_LIMIT),
-        cost_estimate=pl.CostEstimate(
-            flops=4 * count * half * half * width,
-            bytes_accessed=6 * count * half * width,
-            transcendentals=0,
-        ),
+        cost_estimate=LIGHT,
         name="compact_sent",
-    )(lengths, keep, weight, keys, values)
+    )(lengths, keep, weight, keys, values, *extra)
 
 
 def main_kernel(
@@ -131,12 +157,12 @@
     raw, own_rows, sent_rows, forget, logs, scores, sem_raw, sem_sent, sem_out = rest[5:]
     own, sent = half_of("seq", n_seq)
     seq = lax.axis_index("seq")
-    req, heads, pos = forget_ref.shape
+    heads, req, pos = forget_ref.shape
     half = pos // 2
     rows = half // 2
     width = keys.shape[2]
     size = width // heads
-    pad = forget.shape[0] // req
+    pad = forget.shape[1] // req
 
     raw_copies = [
         [
@@ -148,12 +174,12 @@
     for pair in raw_copies:
         for copy in pair:
             copy.start()
-    count = req // n_chunk
+    firsts = [sum(x.shape[1] for x in chunks[:c]) for c in range(n_chunk)]
     sent_copies = [
         pltpu.make_async_copy(
-            chunks[c], sent_rows.at[:, pl.ds(c * count, count)], sem_sent.at[c]
-        )
-        for c in range(n_chunk)
+            chunk, sent_rows.at[:, pl.ds(firsts[c], chunk.shape[1])], sem_sent.at[c]
+        )
+        for c, chunk in enumerate(chunks)
     ]
     for copy in sent_copies:
         copy.start()
@@ -161,9 +187,7 @@
     kinds = 4 * req
     shape = (kinds, kinds)
     to, frm = iota(shape, 0), iota(shape, 1)
-    wanted = jnp.zeros(shape, jnp.int32)
-    for r in range(req):
-        wanted = jnp.where(to % req == r, route_ref[r], wanted)
+    wanted = by_row(route_ref, to % req)
     me = lax.axis_index("grp")
     picked = jnp.zeros((kinds, width), jnp.float32)
     for k in range(n_grp):
@@ -173,23 +197,27 @@
     picked_ref[...] = picked
 
     forget[...] = jnp.zeros_like(forget)
-    lane = iota((heads, pos), 1)
-    for r in range(req):
-        live = seq * pos + lane < len_ref[r]
-        forget[r * pad : r * pad + heads, :] = jnp.where(live, forget_ref[r], 0.0)
-    gates = forget[...]
+    live = seq * pos + iota((req, pos), 1) < by_row(len_ref, iota((req, pos), 0))
+    for h in range(heads):
+        gate = jnp.where(live, forget_ref[h], 0.0)
+        for c in range(pos // LANES):
+            forget[c, pl.ds(h, req, stride=pad), :] = gate[:, c * LANES : (c + 1) * LANES]
+    gates = jnp.concatenate([forget[c] for c in range(pos // LANES)], axis=1)
     total = jnp.sum(gates, axis=1, keepdims=True)
     one, two = iota((half, half), 0), iota((half, half), 1)
-    after = ((one // BLOCK == two // BLOCK) & (one > two)).astype(jnp.float32).astype(jnp.bfloat16)
-    ends = iota((pos, rows), 1) // SLOTS
-    begins = iota((pos, rows), 0) // BLOCK
-    last = iota((req * pad, rows), 1) % SLOTS == SLOTS - 1
+    after = (((one ^ two) < BLOCK) & (one > two)).astype(jnp.float32).astype(jnp.bfloat16)
+    ends = iota((pos, rows), 1) >> SLOT_LOG
+    begins = iota((pos, rows), 0) >> BLOCK_LOG
+    last = iota((req * pad, rows), 1) & (SLOTS - 1) == SLOTS - 1
 
     for i, h in enumerate((own, sent)):
         slot, factor = plan(
             keep_ref[:, lanes(h, half)], weight_ref[:, lanes(h, half)], seq * pos + h * half, len_ref
         )
-        inner = split_dot(forget[:, lanes(h, half)], after)
+        near = half // LANES
+        inner = split_dot(
+            jnp.concatenate([forget[h * near + c] for c in range(near)], axis=1), after
+        )
         beyond = split_dot(
             gates, (begins > ends + h * (half // BLOCK)).astype(jnp.float32).astype(jnp.bfloat16)
         )
@@ -213,9 +241,9 @@
         kept = at[0] + at[1] + at[2]
         merged = jnp.log(jnp.where(filled, at[3] + at[4], 1.0))
         level = jnp.where(filled, jnp.where(last, merged, kept) + beyond, EMPTY_LOG)
-        logs[:, i * rows : (i + 1) * rows] = level
-        for r in range(req):
-            log_ref[r, :, lanes(h, rows)] = level[r * pad : r * pad + heads]
+        logs[i] = level
+        for k in range(heads):
+            log_ref[k, :, lanes(h, rows)] = logs[i, pl.ds(k, req, stride=pad), :]
 
     out_copies = [
         pltpu.make_async_copy(own_rows.at[i], out.at[:, lanes(own, rows), :], sem_out.at[i])
@@ -226,13 +254,14 @@
     for copy in sent_copies:
         copy.wait()
 
-    mine = iota((pad, width), 0) == iota((pad, width), 1) // size
+    lane, row = iota((pad, width), 1), iota((pad, width), 0)
+    mine = (lane >= row * size) & (lane < (row + 1) * size)
     for r in range(req):
         query = jnp.where(mine, picked[r : r + 1, :], 0.0).astype(jnp.bfloat16)
         here = slice(r * pad, (r + 1) * pad)
         scores[here, :rows] = dot_nt(query, own_rows[0, r])
         scores[here, rows:] = dot_nt(query, sent_rows[0, r])
-    level = scores[...] * (size**-0.5) + logs[...]
+    level = scores[...] * (size**-0.5) + jnp.concatenate([logs[0], logs[1]], axis=1)
     top = jnp.max(level, axis=1, keepdims=True)
     weights = jnp.exp(level - top).astype(jnp.bfloat16).astype(jnp.float32)
     mass = jnp.sum(weights, axis=1, keepdims=True)
@@ -256,7 +285,7 @@
 
 def main_part(n_seq, n_grp, lengths, route, keep, weight, forget, keys, values, chunks, fresh):
     req, pos, width = keys.shape
-    heads = forget.shape[1]
+    heads = forget.shape[0]
     half, rows, pad = pos // 2, pos // 4, -(-heads // 8) * 8
     n_chunk = len(chunks)
     vmem = pl.BlockSpec(memory_space=pltpu.VMEM)
@@ -268,7 +297,7 @@
         out_shape=(
             whole,
             whole,
-            jax.ShapeDtypeStruct((req, heads, 2 * rows), jnp.float32),
+            jax.ShapeDtypeStruct((heads, req, 2 * rows), jnp.float32),
             jax.ShapeDtypeStruct((4 * req, width), jnp.float32),
             jax.ShapeDtypeStruct((4 * req, width), jnp.float32),
         ),
@@ -278,26 +307,22 @@
             pltpu.VMEM((2, req, half, width), jnp.bfloat16),
             pltpu.VMEM((2, req, rows, width), jnp.bfloat16),
             pltpu.VMEM((2, req, rows, width), jnp.bfloat16),
-            pltpu.VMEM((req * pad, pos), jnp.float32),
-            pltpu.VMEM((req * pad, 2 * rows), jnp.float32),
+            pltpu.VMEM((pos // LANES, req * pad, LANES), jnp.float32),
+            pltpu.VMEM((2, req * pad, rows), jnp.float32),
             pltpu.VMEM((req * pad, 2 * rows), jnp.float32),
             pltpu.SemaphoreType.DMA((2, req)),
             pltpu.SemaphoreType.DMA((n_chunk,)),
             pltpu.SemaphoreType.DMA((2,)),
         ],
-        compiler_params=pltpu.CompilerParams(vmem_limit_bytes=VMEM_LIMIT),
-        cost_estimate=pl.CostEstimate(
-            flops=8 * req * half * half * width,
-            bytes_accessed=8 * req * half * width,
-            transcendentals=4 * req * heads * pos,
-        ),
+        compiler_params=pltpu.CompilerParams(vmem_limit_bytes=MAIN_LIMIT),
+        cost_estimate=LIGHT,
         name="compact_own_and_attend",
     )(lengths, route, keep, weight, forget, keys, values, *chunks, *fresh)
 
 
 def merge_kernel(count, relative, size, *refs):
     stats, (picked_ref, weight_ref, log_ref, decay_ref, out_ref) = refs[:count], refs[count:]
-    req, heads, rows = log_ref.shape
+    heads, req, rows = log_ref.shape
     width = picked_ref.shape[1]
     seq = lax.axis_index("seq")
     places = [lax.rem(seq + count - k, count) if relative else jnp.int32(k) for k in range(count)]
@@ -327,15 +352,12 @@
     out_ref[...] = dot(attended.astype(jnp.bfloat16), weight_ref[...])
 
     beyond = later(seq)
-    head = iota((heads, width), 0)
-    first = head * size == iota((heads, width), 1)
-    for r in range(req):
-        column = jnp.sum(jnp.where(first, beyond[r : r + 1, :], 0.0), axis=1, keepdims=True)
-        decay_ref[r] = jnp.exp(log_ref[r] + column)
+    for h in range(heads):
+        decay_ref[h] = jnp.exp(log_ref[h] + beyond[:, h * size : h * size + 1])
 
 
 def merge_part(stats, relative, picked, out_weight, logs, size):
-    req = logs.shape[0]
+    req = logs.shape[1]
     vmem = pl.BlockSpec(memory_space=pltpu.VMEM)
     return pl.pallas_call(
         functools.partial(merge_kernel, len(stats), relative, size),
@@ -345,7 +367,8 @@
         ),
         in_specs=[vmem] * (len(stats) + 3),
         out_specs=(vmem, vmem),
-        compiler_params=pltpu.CompilerParams(vmem_limit_bytes=VMEM_LIMIT),
+        compiler_params=pltpu.CompilerParams(vmem_limit_bytes=SMALL_LIMIT),
+        cost_estimate=LIGHT,
         name="merge_and_project",
     )(*stats, picked, out_weight, logs)
 
@@ -366,24 +389,32 @@
         out_shape=jax.ShapeDtypeStruct(parts[0].shape, jnp.bfloat16),
         in_specs=[pl.BlockSpec(memory_space=pltpu.VMEM)] * len(parts),
         out_specs=pl.BlockSpec(memory_space=pltpu.VMEM),
+        compiler_params=pltpu.CompilerParams(vmem_limit_bytes=SMALL_LIMIT),
+        cost_estimate=LIGHT,
         name="sum_heads",
     )(*parts)
 
 
-def place_kernel(n_seq, first, part, old_k, old_v, out_k, out_v, sem):
+def place_kernel(n_seq, first, part, old_k, old_v, out_k, out_v, buf, sem_in, sem_out):
     _, sent = half_of("seq", n_seq)
     _, count, rows, _ = part.shape
-    copies = [
-        pltpu.make_async_copy(
-            part.at[i, j], out.at[first + j, lanes(sent, rows), :], sem.at[i, j]
-        )
+    pairs = [
+        (
+            pltpu.make_async_copy(part.at[i, j], buf.at[i, j], sem_in.at[i, j]),
+            pltpu.make_async_copy(
+                buf.at[i, j], out.at[first + j, lanes(sent, rows), :], sem_out.at[i, j]
+            ),
+        )
+        for j in range(count)
         for i, out in enumerate((out_k, out_v))
-        for j in range(count)
     ]
-    for copy in copies:
-        copy.start()
-    for copy in copies:
-        copy.wait()
+    for load, _ in pairs:
+        load.start()
+    for load, store in pairs:
+        load.wait()
+        store.start()
+    for _, store in pairs:
+        store.wait()
 
 
 def place_part(n_seq, first, part, out_k, out_v):
@@ -394,8 +425,14 @@
         out_shape=(shape, shape),
         in_specs=[hbm] * 3,
         out_specs=(hbm, hbm),
-        scratch_shapes=[pltpu.SemaphoreType.DMA((2, part.shape[1]))],
+        scratch_shapes=[
+            pltpu.VMEM(part.shape, part.dtype),
+            pltpu.SemaphoreType.DMA((2, part.shape[1])),
+            pltpu.SemaphoreType.DMA((2, part.shape[1])),
+        ],
         input_output_aliases={1: 0, 2: 1},
+        compiler_params=pltpu.CompilerParams(vmem_limit_bytes=SMALL_LIMIT),
+        cost_estimate=LIGHT,
         name="place_received",
     )(part, out_k, out_v)
 
@@ -415,19 +452,28 @@
     heads = log_forget.shape[1]
     size = width // heads
     n_seq, n_grp = lax.axis_size("seq"), lax.axis_size("grp")
-    gates = jnp.repeat(new_forget, size, axis=1)
-    tokens = others(jnp.concatenate([fresh.reshape(3 * req, width), gates], axis=0), "grp")
-    count = req // CHUNKS
-    chunks = [
-        send_part(n_seq, c * count, count, lengths, keep, merge_weight, keys, values)
-        for c in range(CHUNKS)
-    ]
+    cache = (lengths, keep, merge_weight, keys, values)
+    chunk, packed = send_part(
+        n_seq, 0, FIRST, *cache, (fresh.reshape(3 * req, width), new_forget)
+    )
+    chunks = [chunk, send_part(n_seq, FIRST, req - FIRST, *cache, (chunk,))[0]]
     if n_seq == 2:
         received = [lax.ppermute(x, "seq", [(0, 1), (1, 0)]) for x in chunks]
     else:
         received = chunks
+    tokens = others(packed, "grp")
     out_k, out_v, logs, stats, picked = main_part(
-        n_seq, n_grp, lengths, route, keep, merge_weight, log_forget, keys, values, chunks, tokens
+        n_seq,
+        n_grp,
+        lengths,
+        route,
+        keep,
+        merge_weight,
+        log_forget.transpose(1, 0, 2),
+        keys,
+        values,
+        chunks,
+        tokens,
     )
     if n_seq == 2:
         all_stats = others(stats, "seq")
@@ -436,13 +482,13 @@
         all_stats = [gathered[i] for i in range(n_seq)]
     decay, partial = merge_part(all_stats, n_seq == 2, picked, out_weight, logs, size)
     layer_out = sum_part(others(partial, "head"))
-    for c in range(CHUNKS):
-        out_k, out_v = place_part(n_seq, c * count, received[c], out_k, out_v)
+    out_k, out_v = place_part(n_seq, 0, received[0], out_k, out_v)
+    out_k, out_v = place_part(n_seq, FIRST, received[1], out_k, out_v)
     if n_seq != 2:
         out_k, out_v = (
             lax.all_to_all(x, "seq", split_axis=1, concat_axis=1, tiled=True) for x in (out_k, out_v)
         )
-    return out_k, out_v, decay, layer_out
+    return out_k, out_v, decay.transpose(1, 0, 2), layer_out
 
 
 def solution(mesh):

time: 118 us -> 61.3 us (0.52)
  Pallas kernels: 72.5 us -> 20.1 us
  local copies, waits for them, and re-layouts: 10.3 us -> 4.07 us
  waiting for transfers between devices: 18.7 us -> 22 us
    pallas_call x4 -> x2, Pallas kernels: 52.2 us -> 4.03 us  [place_part(): pl.pallas_call(functools.partial(place_kernel, n_seq, first), out_shape=(...]
    unnamed x32 -> x16, local copies, waits for them, and re-layouts: 8.22 us -> 4.07 us
    pallas_call x4 -> x2, Pallas kernels: 11.9 us -> 8.39 us  [send_part(): pl.pallas_call(functools.partial(send_kernel, n_seq, first, count), out_s...]
    ppermute x7, waiting for transfers between devices: 18.7 us -> 22 us  [others(): lax.ppermute(value, axis, [(i, (i + k) % count) for i in range(count)])]
    ppermute x4 -> x2, starting transfers between devices: 5.25 us -> 3.09 us  [shards(): received = [lax.ppermute(x, 'seq', [(0, 1), (1, 0)]) for x in chunks]]
    ppermute x7, starting transfers between devices: 8.94 us -> 10.8 us  [others(): lax.ppermute(value, axis, [(i, (i + k) % count) for i in range(count)])]
    reshape x1 -> x0, local copies, waits for them, and re-layouts: 1.4 us -> none  [shards(): gates = jnp.repeat(new_forget, size, axis=1)]
  transfers between devices with their start and end apart: 11 -> 9, of which waited for: 7 -> 5; matrix products, arithmetic and copies ran while one was open for 4% -> 0% of each run, Pallas kernels for 48% -> 23%
where the time goes in v2:
time: 61.3 us; the launch traced here: 60.8 us
  waiting for transfers between devices  22 us (36%)
  Pallas kernels  20.1 us (33%)
  starting transfers between devices  13.9 us (23%)
  local copies, waits for them, and re-layouts  4.07 us (7%)
  between operations  0.7 us (1%)
    ppermute x7, waiting for transfers between devices, others(): lax.ppermute(value, axis, [(i, (i + k) % count) for i in range(count)])  22 us
    ppermute x7, starting transfers between devices, others(): lax.ppermute(value, axis, [(i, (i + k) % count) for i in range(count)])  10.8 us
    pallas_call x2, Pallas kernels, send_part(): pl.pallas_call(functools.partial(send_kernel, n_seq, first, count), out_s...  8.39 us
    pallas_call x1, Pallas kernels, main_part(): pl.pallas_call(functools.partial(main_kernel, n_seq, n_grp, n_chunk), out...  6.2 us
    unnamed x16, local copies, waits for them, and re-layouts  4.07 us
    pallas_call x2, Pallas kernels, place_part(): pl.pallas_call(functools.partial(place_kernel, n_seq, first), out_shape=(...  4.03 us
    ppermute x2, starting transfers between devices, shards(): received = [lax.ppermute(x, 'seq', [(0, 1), (1, 0)]) for x in chunks]  3.09 us
  transfers between devices with their start and end apart: 9, of which 5 were waited for; matrix products, arithmetic and copies ran while one was open for 0% of the time, Pallas kernels for 23%

profile of v2, /device:TPU:0, one launch (start us, length us, event | category | flops | bytes accessed | tf_op | source)
XLA Modules:
  0.0 60.8 jit_solution(12305936294332463530)
XLA Ops:
  0.6 4.2 %compact_sent.2 = (bf16[2,4,128,384]{3,2,1,0:T(8,128)(2,1)}, bf16[32,384]{1,0:T(8,128)(2,1)}) custom-call(s32[8]{0:T(128)} %len_ref.5, s32[8,512]{1,0:T(8,128)} %keep_ref.5, f32[8,512]{1,0:T(8,128)} %weight_ref.5, bf16[8,512,384]{2,1,0:T(8,128)(2,1)} %keys.5, bf16[8,512,384]{2,1,0:T(8,128)(2,1)} %values.5, bf16[24,384]{1,0:T(8,128)(2,1)} %bitcast.4, ...), custom_call_target="tpu_custom_call" | custom-call | flops 1 | bytes 1 | tf_op jit(solution)/shard_map/compact_sent/pallas_call | solution.py:135
  4.8 0.0 copy-start.4
  4.9 3.0 %collective-permute-start.1 = (bf16[2,4,128,384]{3,2,1,0:T(8,128)(2,1)}, bf16[2,4,128,384]{3,2,1,0:T(8,128)(2,1)}, u32[]{:S(2)}, u32[]{:S(2)}) collective-permute-start(bf16[2,4,128,384]{3,2,1,0:T(8,128)(2,1)} %get-tuple-element.17.rest_0_), channel_id=1, source_target_pairs={{0,4},{4,0},{1,5},{5,1},{2,6},{6,2},{3,7},{7,3},{8,12},{12,8},{9,1... | collective-permute-start | bytes 2359304 | tf_op jit(solution)/shard_map/ppermute | solution.py:461
  7.9 4.2 %compact_sent.3.rest_1_ = bf16[2,4,128,384]{3,2,1,0:T(8,128)(2,1)} custom-call(s32[8]{0:T(128)} %len_ref.5, s32[8,512]{1,0:T(8,128)} %keep_ref.5, f32[8,512]{1,0:T(8,128)} %weight_ref.5, bf16[8,512,384]{2,1,0:T(8,128)(2,1)} %keys.5, bf16[8,512,384]{2,1,0:T(8,128)(2,1)} %values.5, bf16[2,4,128,384]{3,2,1,0:T(8,128)(2,1)} %get-tuple-element.17.rest_0_), custom_call_target="tpu_custom_call" | custom-call | flops 1 | bytes 1 | tf_op jit(solution)/shard_map/compact_sent/pallas_call | solution.py:135
  12.0 0.1 collective-permute-start
  12.1 0.0 copy-done.4
  12.1 0.1 collective-permute-start.2
  12.2 2.0 %collective-permute-start.3 = (bf16[32,384]{1,0:T(8,128)(2,1)S(1)}, bf16[32,384]{1,0:T(8,128)(2,1)S(1)}, u32[]{:S(2)}, u32[]{:S(2)}) collective-permute-start(bf16[32,384]{1,0:T(8,128)(2,1)S(1)} %copy-done.4), channel_id=1, source_target_pairs={{0,16},{8,24},{16,0},{24,8},{1,17},{9,25},{17,1},{25,9},{2,18},{10... | collective-permute-start | bytes 73736 | tf_op jit(solution)/shard_map/ppermute | solution.py:443
  14.2 1.4 %collective-permute-start.4 = (bf16[32,384]{1,0:T(8,128)(2,1)S(1)}, bf16[32,384]{1,0:T(8,128)(2,1)S(1)}, u32[]{:S(2)}, u32[]{:S(2)}) collective-permute-start(bf16[32,384]{1,0:T(8,128)(2,1)S(1)} %copy-done.4), channel_id=1, source_target_pairs={{0,24},{8,0},{16,8},{24,16},{1,25},{9,1},{17,9},{25,17},{2,26},{10... | collective-permute-start | bytes 73736 | tf_op jit(solution)/shard_map/ppermute | solution.py:443
  15.6 0.0 collective-permute-done.2.rest_3_
  15.6 0.0 copy-start.5
  15.6 0.4 collective-permute-done.3.rest_4_
  16.1 0.0 copy-start.6
  16.1 1.1 %collective-permute-done.4.rest_5_ = bf16[32,384]{1,0:T(8,128)(2,1)S(1)} collective-permute-done((bf16[32,384]{1,0:T(8,128)(2,1)S(1)}, bf16[32,384]{1,0:T(8,128)(2,1)S(1)}, u32[]{:S(2)}, u32[]{:S(2)}) %collective-permute-start.4) | collective-permute-done | bytes 24608 | tf_op jit(solution)/shard_map/ppermute | solution.py:443
  17.2 0.0 copy-start.7
  17.2 0.0 copy-done.5
  17.2 0.0 copy-done.6
  17.2 0.6 copy-done.7
  17.8 6.2 %compact_own_and_attend.1 = (bf16[8,256,384]{2,1,0:T(8,128)(2,1)}, bf16[8,256,384]{2,1,0:T(8,128)(2,1)}, f32[6,8,256]{2,1,0:T(8,128)}, f32[32,384]{1,0:T(8,128)}, f32[32,384]{1,0:T(8,128)}) custom-call(s32[8]{0:T(128)} %len_ref.5, s32[8]{0:T(128)} %route_ref.1, s32[8,512]{1,0:T(8,128)} %keep_ref.5, f32[8,512]{1,0:T(8,128)} %weight_ref.5, ...), custom_call_target="tpu_custom_call" | custom-call | flops 1 | bytes 1 | tf_op jit(solution)/shard_map/compact_own_and_attend/pallas_call | solution.py:295
  24.0 1.6 %collective-permute-start.5 = (f32[32,384]{1,0:T(8,128)}, f32[32,384]{1,0:T(8,128)S(1)}, u32[]{:S(2)}, u32[]{:S(2)}) collective-permute-start(f32[32,384]{1,0:T(8,128)} %get-tuple-element.25.refs_0_), channel_id=1, source_target_pairs={{0,4},{4,0},{1,5},{5,1},{2,6},{6,2},{3,7},{7,3},{8,12},{12,8},{9,1... | collective-permute-start | bytes 147464 | tf_op jit(solution)/shard_map/ppermute | solution.py:443
  25.5 18.0 %collective-permute-done.5.refs_1_ = f32[32,384]{1,0:T(8,128)S(1)} collective-permute-done((f32[32,384]{1,0:T(8,128)}, f32[32,384]{1,0:T(8,128)S(1)}, u32[]{:S(2)}, u32[]{:S(2)}) %collective-permute-start.5) | collective-permute-done | bytes 49184 | tf_op jit(solution)/shard_map/ppermute | solution.py:443
  43.5 0.0 copy-start
  43.5 1.1 %copy-done = bf16[384,768]{1,0:T(8,128)(2,1)S(1)} copy-done((bf16[384,768]{1,0:T(8,128)(2,1)S(1)}, bf16[384,768]{1,0:T(8,128)(2,1)}, u32[]{:S(2)}) %copy-start) | copy-done | bytes 589848
  44.6 0.0 copy-start.1
  44.6 0.8 %copy-done.1 = f32[6,8,256]{2,1,0:T(8,128)S(1)} copy-done((f32[6,8,256]{2,1,0:T(8,128)S(1)}, f32[6,8,256]{2,1,0:T(8,128)}, u32[]{:S(2)}) %copy-start.1) | copy-done | bytes 49176
  45.4 0.0 copy-start.2
  45.4 0.8 %copy-done.2 = f32[32,384]{1,0:T(8,128)S(1)} copy-done((f32[32,384]{1,0:T(8,128)S(1)}, f32[32,384]{1,0:T(8,128)}, u32[]{:S(2)}) %copy-start.2) | copy-done | bytes 49176
  46.2 0.0 copy-start.3
  46.2 0.8 %copy-done.3 = f32[32,384]{1,0:T(8,128)S(1)} copy-done((f32[32,384]{1,0:T(8,128)S(1)}, f32[32,384]{1,0:T(8,128)}, u32[]{:S(2)}) %copy-start.3) | copy-done | bytes 49176
  47.0 0.9 %merge_and_project.1 = (f32[6,8,256]{2,1,0:T(8,128)}, f32[8,768]{1,0:T(8,128)S(1)}) custom-call(f32[32,384]{1,0:T(8,128)S(1)} %copy-done.2, f32[32,384]{1,0:T(8,128)S(1)} %collective-permute-done.5.refs_1_, f32[32,384]{1,0:T(8,128)S(1)} %copy-done.3, bf16[384,768]{1,0:T(8,128)(2,1)S(1)} %copy-done, f32[6,8,256]{2,1,0:T(8,128)S(1)} %copy-done.1), custom_call_target="tpu_custom_call" | custom-call | flops 1 | bytes 1 | tf_op jit(solution)/shard_map/merge_and_project/pallas_call | solution.py:362
  47.9 1.8 %collective-permute-start.6 = (f32[8,768]{1,0:T(8,128)S(1)}, f32[8,768]{1,0:T(8,128)S(1)}, u32[]{:S(2)}, u32[]{:S(2)}) collective-permute-start(f32[8,768]{1,0:T(8,128)S(1)} %get-tuple-element.29.refs_0_), channel_id=1, source_target_pairs={{0,1},{1,2},{2,3},{3,0},{4,5},{5,6},{6,7},{7,4},{8,9},{9,10},{10,1... | collective-permute-start | bytes 73736 | tf_op jit(solution)/shard_map/ppermute | solution.py:443
  49.7 2.6 %collective-permute-start.7 = (f32[8,768]{1,0:T(8,128)S(1)}, f32[8,768]{1,0:T(8,128)S(1)}, u32[]{:S(2)}, u32[]{:S(2)}) collective-permute-start(f32[8,768]{1,0:T(8,128)S(1)} %get-tuple-element.29.refs_0_), channel_id=1, source_target_pairs={{0,2},{1,3},{2,0},{3,1},{4,6},{5,7},{6,4},{7,5},{8,10},{9,11},{10,... | collective-permute-start | bytes 73736 | tf_op jit(solution)/shard_map/ppermute | solution.py:443
  52.3 1.3 %collective-permute-start.8 = (f32[8,768]{1,0:T(8,128)S(1)}, f32[8,768]{1,0:T(8,128)S(1)}, u32[]{:S(2)}, u32[]{:S(2)}) collective-permute-start(f32[8,768]{1,0:T(8,128)S(1)} %get-tuple-element.29.refs_0_), channel_id=1, source_target_pairs={{0,3},{1,0},{2,1},{3,2},{4,7},{5,4},{6,5},{7,6},{8,11},{9,8},{10,9... | collective-permute-start | bytes 73736 | tf_op jit(solution)/shard_map/ppermute | solution.py:443
  53.6 0.0 collective-permute-done.6.refs_1_
  53.7 0.7 %collective-permute-done.7.refs_2_ = f32[8,768]{1,0:T(8,128)S(1)} collective-permute-done((f32[8,768]{1,0:T(8,128)S(1)}, f32[8,768]{1,0:T(8,128)S(1)}, u32[]{:S(2)}, u32[]{:S(2)}) %collective-permute-start.7) | collective-permute-done | bytes 24608 | tf_op jit(solution)/shard_map/ppermute | solution.py:443
  54.4 1.7 %collective-permute-done.8.refs_3_ = f32[8,768]{1,0:T(8,128)S(1)} collective-permute-done((f32[8,768]{1,0:T(8,128)S(1)}, f32[8,768]{1,0:T(8,128)S(1)}, u32[]{:S(2)}, u32[]{:S(2)}) %collective-permute-start.8) | collective-permute-done | bytes 24608 | tf_op jit(solution)/shard_map/ppermute | solution.py:443
  56.1 0.6 %sum_heads.1 = bf16[8,768]{1,0:T(8,128)(2,1)} custom-call(f32[8,768]{1,0:T(8,128)S(1)} %get-tuple-element.29.refs_0_, f32[8,768]{1,0:T(8,128)S(1)} %collective-permute-done.6.refs_1_, f32[8,768]{1,0:T(8,128)S(1)} %collective-permute-done.7.refs_2_, f32[8,768]{1,0:T(8,128)S(1)} %collective-permute-done.8.refs_3_), custom_call_target="tpu_custom_call" | custom-call | flops 1 | bytes 1 | tf_op jit(solution)/shard_map/sum_heads/pallas_call | solution.py:387
  56.7 0.0 collective-permute-done.1.part
  56.7 2.0 %place_received.2 = (bf16[8,256,384]{2,1,0:T(8,128)(2,1)}, bf16[8,256,384]{2,1,0:T(8,128)(2,1)}) custom-call(bf16[2,4,128,384]{3,2,1,0:T(8,128)(2,1)} %collective-permute-done.1.part, bf16[8,256,384]{2,1,0:T(8,128)(2,1)} %get-tuple-element.19.old_k, bf16[8,256,384]{2,1,0:T(8,128)(2,1)} %get-tuple-element.20.old_v), custom_call_target="tpu_custom_call", output_to_operand_aliasing={{0}: (1, {}), {1}: (2, {})} | custom-call | flops 1 | bytes 1 | tf_op jit(solution)/shard_map/place_received/pallas_call | solution.py:423
  58.7 0.0 collective-permute-done.part
  58.7 2.0 %place_received.3 = (bf16[8,256,384]{2,1,0:T(8,128)(2,1)}, bf16[8,256,384]{2,1,0:T(8,128)(2,1)}) custom-call(bf16[2,4,128,384]{3,2,1,0:T(8,128)(2,1)S(1)} %collective-permute-done.part, bf16[8,256,384]{2,1,0:T(8,128)(2,1)} %get-tuple-element.21.old_k, bf16[8,256,384]{2,1,0:T(8,128)(2,1)} %get-tuple-element.22.old_v), custom_call_target="tpu_custom_call", output_to_operand_aliasing={{0}: (1, {}), {1}: (2, {})} | custom-call | flops 1 | bytes 1 | tf_op jit(solution)/shard_map/place_received/pallas_call | solution.py:423
Async XLA Ops:
  4.8 7.3 %copy-start.4 = (bf16[32,384]{1,0:T(8,128)(2,1)S(1)}, bf16[32,384]{1,0:T(8,128)(2,1)}, u32[]{:S(2)}) copy-start(bf16[32,384]{1,0:T(8,128)(2,1)} %get-tuple-element.18.rest_2_) | copy-start | bytes 73732
  4.9 51.9 %collective-permute-start.1 = (bf16[2,4,128,384]{3,2,1,0:T(8,128)(2,1)}, bf16[2,4,128,384]{3,2,1,0:T(8,128)(2,1)}, u32[]{:S(2)}, u32[]{:S(2)}) collective-permute-start(bf16[2,4,128,384]{3,2,1,0:T(8,128)(2,1)} %get-tuple-element.17.rest_0_), channel_id=1, source_target_pairs={{0,4},{4,0},{1,5},{5,1},{2,6},{6,2},{3,7},{7,3},{8,12},{12,8},{9,1... | collective-permute-start | bytes 2359304 | tf_op jit(solution)/shard_map/ppermute | solution.py:461
  12.0 46.7 %collective-permute-start = (bf16[2,4,128,384]{3,2,1,0:T(8,128)(2,1)}, bf16[2,4,128,384]{3,2,1,0:T(8,128)(2,1)S(1)}, u32[]{:S(2)}, u32[]{:S(2)}) collective-permute-start(bf16[2,4,128,384]{3,2,1,0:T(8,128)(2,1)} %compact_sent.3.rest_1_), channel_id=1, source_target_pairs={{0,4},{4,0},{1,5},{5,1},{2,6},{6,2},{3,7},{7,3},{8,12},{12,8},{9,1... | collective-permute-start | bytes 2359304 | tf_op jit(solution)/shard_map/ppermute | solution.py:461
  12.1 3.5 %collective-permute-start.2 = (bf16[32,384]{1,0:T(8,128)(2,1)S(1)}, bf16[32,384]{1,0:T(8,128)(2,1)S(1)}, u32[]{:S(2)}, u32[]{:S(2)}) collective-permute-start(bf16[32,384]{1,0:T(8,128)(2,1)S(1)} %copy-done.4), channel_id=1, source_target_pairs={{0,8},{8,16},{16,24},{24,0},{1,9},{9,17},{17,25},{25,1},{2,10},{10... | collective-permute-start | bytes 73736 | tf_op jit(solution)/shard_map/ppermute | solution.py:443
  12.2 3.9 %collective-permute-start.3 = (bf16[32,384]{1,0:T(8,128)(2,1)S(1)}, bf16[32,384]{1,0:T(8,128)(2,1)S(1)}, u32[]{:S(2)}, u32[]{:S(2)}) collective-permute-start(bf16[32,384]{1,0:T(8,128)(2,1)S(1)} %copy-done.4), channel_id=1, source_target_pairs={{0,16},{8,24},{16,0},{24,8},{1,17},{9,25},{17,1},{25,9},{2,18},{10... | collective-permute-start | bytes 73736 | tf_op jit(solution)/shard_map/ppermute | solution.py:443
  14.2 3.0 %collective-permute-start.4 = (bf16[32,384]{1,0:T(8,128)(2,1)S(1)}, bf16[32,384]{1,0:T(8,128)(2,1)S(1)}, u32[]{:S(2)}, u32[]{:S(2)}) collective-permute-start(bf16[32,384]{1,0:T(8,128)(2,1)S(1)} %copy-done.4), channel_id=1, source_target_pairs={{0,24},{8,0},{16,8},{24,16},{1,25},{9,1},{17,9},{25,17},{2,26},{10... | collective-permute-start | bytes 73736 | tf_op jit(solution)/shard_map/ppermute | solution.py:443
  15.6 1.5 %copy-start.5 = (bf16[32,384]{1,0:T(8,128)(2,1)}, bf16[32,384]{1,0:T(8,128)(2,1)S(1)}, u32[]{:S(2)}) copy-start(bf16[32,384]{1,0:T(8,128)(2,1)S(1)} %collective-permute-done.2.rest_3_) | copy-start | bytes 73732
  16.1 1.1 %copy-start.6 = (bf16[32,384]{1,0:T(8,128)(2,1)}, bf16[32,384]{1,0:T(8,128)(2,1)S(1)}, u32[]{:S(2)}) copy-start(bf16[32,384]{1,0:T(8,128)(2,1)S(1)} %collective-permute-done.3.rest_4_) | copy-start | bytes 73732
  17.2 0.6 copy-start.7
  24.0 19.5 %collective-permute-start.5 = (f32[32,384]{1,0:T(8,128)}, f32[32,384]{1,0:T(8,128)S(1)}, u32[]{:S(2)}, u32[]{:S(2)}) collective-permute-start(f32[32,384]{1,0:T(8,128)} %get-tuple-element.25.refs_0_), channel_id=1, source_target_pairs={{0,4},{4,0},{1,5},{5,1},{2,6},{6,2},{3,7},{7,3},{8,12},{12,8},{9,1... | collective-permute-start | bytes 147464 | tf_op jit(solution)/shard_map/ppermute | solution.py:443
  43.5 1.1 %copy-start = (bf16[384,768]{1,0:T(8,128)(2,1)S(1)}, bf16[384,768]{1,0:T(8,128)(2,1)}, u32[]{:S(2)}) copy-start(bf16[384,768]{1,0:T(8,128)(2,1)} %refs_3_.1) | copy-start | bytes 1769476
  44.6 0.8 %copy-start.1 = (f32[6,8,256]{2,1,0:T(8,128)S(1)}, f32[6,8,256]{2,1,0:T(8,128)}, u32[]{:S(2)}) copy-start(f32[6,8,256]{2,1,0:T(8,128)} %get-tuple-element.27.refs_4_) | copy-start | bytes 147460
  45.4 0.8 %copy-start.2 = (f32[32,384]{1,0:T(8,128)S(1)}, f32[32,384]{1,0:T(8,128)}, u32[]{:S(2)}) copy-start(f32[32,384]{1,0:T(8,128)} %get-tuple-element.25.refs_0_) | copy-start | bytes 147460
  46.2 0.8 %copy-start.3 = (f32[32,384]{1,0:T(8,128)S(1)}, f32[32,384]{1,0:T(8,128)}, u32[]{:S(2)}) copy-start(f32[32,384]{1,0:T(8,128)} %get-tuple-element.26.refs_2_) | copy-start | bytes 147460
  47.9 5.8 %collective-permute-start.6 = (f32[8,768]{1,0:T(8,128)S(1)}, f32[8,768]{1,0:T(8,128)S(1)}, u32[]{:S(2)}, u32[]{:S(2)}) collective-permute-start(f32[8,768]{1,0:T(8,128)S(1)} %get-tuple-element.29.refs_0_), channel_id=1, source_target_pairs={{0,1},{1,2},{2,3},{3,0},{4,5},{5,6},{6,7},{7,4},{8,9},{9,10},{10,1... | collective-permute-start | bytes 73736 | tf_op jit(solution)/shard_map/ppermute | solution.py:443
  49.7 4.7 %collective-permute-start.7 = (f32[8,768]{1,0:T(8,128)S(1)}, f32[8,768]{1,0:T(8,128)S(1)}, u32[]{:S(2)}, u32[]{:S(2)}) collective-permute-start(f32[8,768]{1,0:T(8,128)S(1)} %get-tuple-element.29.refs_0_), channel_id=1, source_target_pairs={{0,2},{1,3},{2,0},{3,1},{4,6},{5,7},{6,4},{7,5},{8,10},{9,11},{10,... | collective-permute-start | bytes 73736 | tf_op jit(solution)/shard_map/ppermute | solution.py:443
  52.3 3.8 %collective-permute-start.8 = (f32[8,768]{1,0:T(8,128)S(1)}, f32[8,768]{1,0:T(8,128)S(1)}, u32[]{:S(2)}, u32[]{:S(2)}) collective-permute-start(f32[8,768]{1,0:T(8,128)S(1)} %get-tuple-element.29.refs_0_), channel_id=1, source_target_pairs={{0,3},{1,0},{2,1},{3,2},{4,7},{5,4},{6,5},{7,6},{8,11},{9,8},{10,9... | collective-permute-start | bytes 73736 | tf_op jit(solution)/shard_map/ppermute | solution.py:443

commit v3 on v2

v3 whole, which is shorter than its diff:
```python
import functools

import jax
import jax.numpy as jnp
from jax import lax
from jax.experimental import pallas as pl
from jax.experimental.pallas import tpu as pltpu
from jax.sharding import PartitionSpec as P

BLOCK = 64
SLOTS = 32
LANES = 128
BLOCK_LOG = BLOCK.bit_length() - 1
SLOT_LOG = SLOTS.bit_length() - 1
EMPTY_LOG = -10000.0
FIRST = 4
VMEM_LIMIT = 63 * 1024 * 1024
SMALL_LIMIT = 8 * 1024 * 1024


LIGHT = pl.CostEstimate(flops=1, bytes_accessed=1, transcendentals=0)
MERGE = pl.CostEstimate(flops=1 << 36, bytes_accessed=1, transcendentals=0)


def dot(a, b):
    return lax.dot_general(a, b, (((1,), (0,)), ((), ())), preferred_element_type=jnp.float32)


def dot_nt(a, b):
    return lax.dot_general(a, b, (((1,), (1,)), ((), ())), preferred_element_type=jnp.float32)


def iota(shape, dim):
    return lax.broadcasted_iota(jnp.int32, shape, dim)


def three(x):
    hi = x.astype(jnp.bfloat16).astype(jnp.float32)
    rest = x - hi
    mid = rest.astype(jnp.bfloat16).astype(jnp.float32)
    return hi, mid, rest - mid


def split_dot(x, ones):
    rows = x.shape[0]
    parts = dot(jnp.concatenate(three(x), axis=0).astype(jnp.bfloat16), ones)
    return parts[:rows] + parts[rows : 2 * rows] + parts[2 * rows :]


def half_of(axis, count):
    own = lax.axis_index(axis) if count == 2 else jnp.int32(0)
    return own, 1 - own


def by_row(ref, row):
    picked = jnp.zeros_like(row)
    for r in range(ref.shape[0]):
        picked = jnp.where(row == r, ref[r], picked)
    return picked


def plan(keep, weight, start, len_ref):
    rows, width = keep.shape
    one, two = iota((width, width), 0), iota((width, width), 1)
    same = (one ^ two) < BLOCK
    upto = (same & (one <= two)).astype(jnp.float32).astype(jnp.bfloat16)
    block = same.astype(jnp.float32).astype(jnp.bfloat16)
    kept = keep == 1
    rank = dot(keep.astype(jnp.float32).astype(jnp.bfloat16), upto) - 1.0
    weighted = jnp.where(kept, 0.0, weight)
    share = (weighted / split_dot(weighted, block)).astype(jnp.bfloat16).astype(jnp.float32)
    lane, row = iota((rows, width), 1), iota((rows, width), 0)
    slot = jnp.where(kept, rank.astype(jnp.int32), SLOTS - 1) + (lane >> BLOCK_LOG) * SLOTS
    slot = jnp.where(start + lane < by_row(len_ref, row), slot, -1)
    return slot, jnp.where(kept, 1.0, share)


def select(slot, factor, r):
    width = slot.shape[1]
    shape = (width // 2, width)
    hit = iota(shape, 0) == slot[r : r + 1, :]
    return jnp.where(hit, jnp.broadcast_to(factor[r : r + 1, :], shape), 0.0).astype(jnp.bfloat16)


def lanes(half, width):
    return pl.ds(pl.multiple_of(half * width, width), width)


def fetch(pairs, sem):
    copies = [pltpu.make_async_copy(src, dst, sem.at[i]) for i, (src, dst) in enumerate(pairs)]
    for copy in copies:
        copy.start()
    return copies


def first_kernel(n_seq, len_hbm, keep_hbm, weight_hbm, fresh_hbm, gate_hbm, keys, values, *rest):
    out, packed, lengths, keep, weight, fresh, gates, raw, rows, sem_s, sem_r, sem_o = rest
    _, sent = half_of("seq", n_seq)
    width = raw.shape[2]
    count = raw.shape[1]
    small = fetch(
        [
            (len_hbm, lengths),
            (keep_hbm.at[:, lanes(sent, width)], keep),
            (weight_hbm.at[:, lanes(sent, width)], weight),
            (fresh_hbm, fresh),
            (gate_hbm, gates),
        ],
        sem_s,
    )
    slabs = fetch(
        [
            (source.at[j, lanes(sent, width), :], raw.at[i, j])
            for j in range(count)
            for i, source in enumerate((keys, values))
        ],
        sem_r,
    )
    for copy in small:
        copy.wait()
    start = lax.axis_index("seq") * (2 * width) + sent * width
    slot, factor = plan(keep[...], weight[...], start, lengths)

    new, gate = fresh[...].astype(jnp.float32), gates[...].astype(jnp.float32)
    req, heads = gate.shape
    lane = iota((req, new.shape[1]), 1)
    size = new.shape[1] // heads
    spread = jnp.zeros((req, new.shape[1]), jnp.float32)
    for h in range(heads):
        inside = (lane >= h * size) & (lane < (h + 1) * size)
        spread = jnp.where(inside, gate[:, h : h + 1], spread)
    packed[...] = jnp.concatenate([new, spread], axis=0).astype(jnp.bfloat16)

    stores = []
    for j in range(count):
        chosen = select(slot, factor, j)
        for i in range(2):
            slabs[j * 2 + i].wait()
            rows[i, j] = dot(chosen, raw[i, j]).astype(jnp.bfloat16)
        stores.append(pltpu.make_async_copy(rows.at[:, j], out.at[:, j], sem_o.at[j]))
        stores[-1].start()
    for copy in stores:
        copy.wait()


def first_part(n_seq, count, lengths, keep, weight, fresh, gates, keys, values):
    req, pos, width = keys.shape
    half = pos // 2
    hbm = pl.BlockSpec(memory_space=pl.ANY)
    vmem = pl.BlockSpec(memory_space=pltpu.VMEM)
    rows = (2, count, half // 2, width)
    return pl.pallas_call(
        functools.partial(first_kernel, n_seq),
        out_shape=(
            jax.ShapeDtypeStruct(rows, jnp.bfloat16),
            jax.ShapeDtypeStruct((fresh.shape[0] + req, width), jnp.bfloat16),
        ),
        in_specs=[hbm] * 7,
        out_specs=(hbm, vmem),
        scratch_shapes=[
            pltpu.SMEM(lengths.shape, jnp.int32),
            pltpu.VMEM((req, half), jnp.int32),
            pltpu.VMEM((req, half), jnp.float32),
            pltpu.VMEM(fresh.shape, fresh.dtype),
            pltpu.VMEM(gates.shape, gates.dtype),
            pltpu.VMEM((2, count, half, width), jnp.bfloat16),
            pltpu.VMEM(rows, jnp.bfloat16),
            pltpu.SemaphoreType.DMA((5,)),
            pltpu.SemaphoreType.DMA((2 * count,)),
            pltpu.SemaphoreType.DMA((count,)),
        ],
        compiler_params=pltpu.CompilerParams(vmem_limit_bytes=VMEM_LIMIT),
        cost_estimate=LIGHT,
        name="compact_first_sent",
    )(lengths, keep, weight, fresh, gates, keys, values)


def own_kernel(
    n_seq, first, len_hbm, keep_hbm, weight_hbm, forget_hbm, keys, values, packed_hbm, *rest
):
    out_k, out_v, chunk, log_ref, level_ref, total_ref = rest[:6]
    lengths, keep, weight, gates, raw, late, forget, rows, rows_late = rest[6:15]
    sem_s, sem_l, sem_r, sem_c, sem_o = rest[15:]
    own, sent = half_of("seq", n_seq)
    seq = lax.axis_index("seq")
    heads, req, pos = forget_hbm.shape
    half = pos // 2
    slots = half // 2
    pad = forget.shape[1] // req
    small = fetch(
        [(len_hbm, lengths), (keep_hbm, keep), (weight_hbm, weight), (forget_hbm, gates)], sem_s
    )
    both = ((0, keys), (1, values))
    late_slabs = fetch(
        [
            (source.at[r, lanes(sent, half), :], late.at[i, r - first])
            for r in range(first, req)
            for i, source in both
        ],
        sem_l,
    )
    slabs = fetch(
        [
            (source.at[r, lanes(own, half), :], raw.at[i, r])
            for r in range(req)
            for i, source in both
        ],
        sem_r,
    )
    for copy in small:
        copy.wait()

    forget[...] = jnp.zeros_like(forget)
    live = seq * pos + iota((req, pos), 1) < by_row(lengths, iota((req, pos), 0))
    for h in range(heads):
        gate = jnp.where(live, gates[h], 0.0)
        for c in range(pos // LANES):
            forget[c, pl.ds(h, req, stride=pad), :] = gate[:, c * LANES : (c + 1) * LANES]
    flat = jnp.concatenate([forget[c] for c in range(pos // LANES)], axis=1)
    total_ref[...] = jnp.broadcast_to(jnp.sum(flat, axis=1, keepdims=True), total_ref.shape)
    one, two = iota((half, half), 0), iota((half, half), 1)
    after = (((one ^ two) < BLOCK) & (one > two)).astype(jnp.float32).astype(jnp.bfloat16)
    ends = iota((pos, slots), 1) >> SLOT_LOG
    begins = iota((pos, slots), 0) >> BLOCK_LOG
    last = iota((req * pad, slots), 1) & (SLOTS - 1) == SLOTS - 1

    stores = []
    for i, h in enumerate((own, sent)):
        slot, factor = plan(
            keep[:, lanes(h, half)], weight[:, lanes(h, half)], seq * pos + h * half, lengths
        )
        near = half // LANES
        inner = split_dot(
            jnp.concatenate([forget[h * near + c] for c in range(near)], axis=1), after
        )
        beyond = split_dot(
            flat, (begins > ends + h * (half // BLOCK)).astype(jnp.float32).astype(jnp.bfloat16)
        )
        spread = jnp.exp(inner)
        high = spread.astype(jnp.bfloat16).astype(jnp.float32)
        planes = three(inner) + (high, spread - high, jnp.ones_like(inner))
        found = []
        for r in range(req):
            chosen = select(slot, factor, r)
            stack = jnp.concatenate([x[r * pad : (r + 1) * pad] for x in planes], axis=0)
            found.append(dot_nt(stack.astype(jnp.bfloat16), chosen))
            if i == 0:
                for k, out in enumerate((out_k, out_v)):
                    slabs[2 * r + k].wait()
                    rows[k, r] = dot(chosen, raw[k, r]).astype(jnp.bfloat16)
                    stores.append(
                        pltpu.make_async_copy(
                            rows.at[k, r], out.at[r, lanes(own, slots), :], sem_o.at[2 * r + k]
                        )
                    )
                    stores[-1].start()
            elif r >= first:
                for k in range(2):
                    late_slabs[2 * (r - first) + k].wait()
                    rows_late[k, r - first] = dot(chosen, late[k, r - first]).astype(jnp.bfloat16)
                stores.append(
                    pltpu.make_async_copy(
                        rows_late.at[:, r - first], chunk.at[:, r - first], sem_c.at[r - first]
                    )
                )
                stores[-1].start()
        at = [
            jnp.concatenate([x[p * pad : (p + 1) * pad] for x in found], axis=0) for p in range(6)
        ]
        filled = at[5] > 0.5
        kept = at[0] + at[1] + at[2]
        merged = jnp.log(jnp.where(filled, at[3] + at[4], 1.0))
        level_ref[i] = jnp.where(filled, jnp.where(last, merged, kept) + beyond, EMPTY_LOG)
        for k in range(heads):
            log_ref[k, :, lanes(h, slots)] = level_ref[i, pl.ds(k, req, stride=pad), :]
    for copy in stores:
        copy.wait()


def own_part(n_seq, first, lengths, keep, weight, forget, keys, values, packed):
    req, pos, width = keys.shape
    heads = forget.shape[0]
    half, slots, pad = pos // 2, pos // 4, -(-heads // 8) * 8
    late = req - first
    hbm = pl.BlockSpec(memory_space=pl.ANY)
    vmem = pl.BlockSpec(memory_space=pltpu.VMEM)
    whole = jax.ShapeDtypeStruct((req, 2 * slots, width), jnp.bfloat16)
    return pl.pallas_call(
        functools.partial(own_kernel, n_seq, first),
        out_shape=(
            whole,
            whole,
            jax.ShapeDtypeStruct((2, late, slots, width), jnp.bfloat16),
            jax.ShapeDtypeStruct((heads, req, 2 * slots), jnp.float32),
            jax.ShapeDtypeStruct((2, req * pad, slots), jnp.float32),
            jax.ShapeDtypeStruct((req * pad, LANES), jnp.float32),
        ),
        in_specs=[hbm] * 7,
        out_specs=(hbm, hbm, hbm, vmem, vmem, vmem),
        scratch_shapes=[
            pltpu.SMEM(lengths.shape, jnp.int32),
            pltpu.VMEM(keep.shape, keep.dtype),
            pltpu.VMEM(weight.shape, weight.dtype),
            pltpu.VMEM(forget.shape, forget.dtype),
            pltpu.VMEM((2, req, half, width), jnp.bfloat16),
            pltpu.VMEM((2, late, half, width), jnp.bfloat16),
            pltpu.VMEM((pos // LANES, req * pad, LANES), jnp.float32),
            pltpu.VMEM((2, req, slots, width), jnp.bfloat16),
            pltpu.VMEM((2, late, slots, width), jnp.bfloat16),
            pltpu.SemaphoreType.DMA((4,)),
            pltpu.SemaphoreType.DMA((2 * late,)),
            pltpu.SemaphoreType.DMA((2 * req,)),
            pltpu.SemaphoreType.DMA((late,)),
            pltpu.SemaphoreType.DMA((2 * req,)),
        ],
        compiler_params=pltpu.CompilerParams(vmem_limit_bytes=VMEM_LIMIT),
        cost_estimate=LIGHT,
        name="compact_own",
    )(lengths, keep, weight, forget, keys, values, packed)


def attend_kernel(n_seq, n_grp, heads, first, *refs):
    route_hbm, out_k, out_v, early, late, level_hbm, total_hbm = refs[:7]
    tokens, rest = refs[7 : 7 + n_grp], refs[7 + n_grp :]
    _, _, _, stats_ref, picked_ref = rest[:5]
    route, own_rows, sent_rows, level, total, fresh, scores, sem_s, sem_r = rest[5:]
    own, _ = half_of("seq", n_seq)
    kinds, width = picked_ref.shape
    req = kinds // 4
    size = width // heads
    slots = own_rows.shape[2]
    pad = total.shape[0] // req
    small = fetch(
        [(route_hbm, route), (level_hbm, level), (total_hbm, total)]
        + [(x, fresh.at[k]) for k, x in enumerate(tokens)],
        sem_s,
    )
    slabs = fetch(
        [
            (out_k.at[:, lanes(own, slots), :], own_rows.at[0]),
            (early, sent_rows.at[:, pl.ds(0, first)]),
            (late, sent_rows.at[:, pl.ds(first, req - first)]),
            (out_v.at[:, lanes(own, slots), :], own_rows.at[1]),
        ],
        sem_r,
    )
    for copy in small:
        copy.wait()

    shape = (kinds, kinds)
    to, frm = iota(shape, 0), iota(shape, 1)
    wanted = by_row(route, to % req)
    me = lax.axis_index("grp")
    picked = jnp.zeros((kinds, width), jnp.float32)
    for k in range(n_grp):
        source = lax.rem(me + n_grp - k, n_grp)
        hit = (to // req == frm // req) & (wanted == source * req + frm % req)
        picked = picked + dot(hit.astype(jnp.float32).astype(jnp.bfloat16), fresh[k])
    picked_ref[...] = picked
    for copy in slabs:
        copy.wait()

    lane, row = iota((pad, width), 1), iota((pad, width), 0)
    mine = (lane >= row * size) & (lane < (row + 1) * size)
    for r in range(req):
        query = jnp.where(mine, picked[r : r + 1, :], 0.0).astype(jnp.bfloat16)
        here = slice(r * pad, (r + 1) * pad)
        scores[here, :slots] = dot_nt(query, own_rows[0, r])
        scores[here, slots:] = dot_nt(query, sent_rows[0, r])
    logit = scores[...] * (size**-0.5) + jnp.concatenate([level[0], level[1]], axis=1)
    top = jnp.max(logit, axis=1, keepdims=True)
    weights = jnp.exp(logit - top).astype(jnp.bfloat16).astype(jnp.float32)
    mass = jnp.sum(weights, axis=1, keepdims=True)

    def spread_out(column, r):
        return jnp.sum(
            jnp.where(mine, column[r * pad : (r + 1) * pad], 0.0), axis=0, keepdims=True
        )

    for r in range(req):
        w = weights[r * pad : (r + 1) * pad].astype(jnp.bfloat16)
        acc = dot(w[:, :slots], own_rows[1, r]) + dot(w[:, slots:], sent_rows[1, r])
        acc = jnp.sum(jnp.where(mine, acc, 0.0), axis=0, keepdims=True)
        for p, x in enumerate((top, mass, total[:, :1])):
            stats_ref[p * req + r : p * req + r + 1, :] = spread_out(x, r)
        stats_ref[3 * req + r : 3 * req + r + 1, :] = acc


def attend_part(n_seq, n_grp, heads, route, out_k, out_v, early, late, level, total, tokens):
    req, rows, width = out_k.shape
    slots, first = rows // 2, early.shape[1]
    hbm = pl.BlockSpec(memory_space=pl.ANY)
    vmem = pl.BlockSpec(memory_space=pltpu.VMEM)
    whole = jax.ShapeDtypeStruct(out_k.shape, out_k.dtype)
    small = jax.ShapeDtypeStruct((4 * req, width), jnp.float32)
    return pl.pallas_call(
        functools.partial(attend_kernel, n_seq, n_grp, heads, first),
        out_shape=(whole, whole, jax.ShapeDtypeStruct(late.shape, late.dtype), small, small),
        in_specs=[hbm] * (7 + n_grp),
        out_specs=(hbm, hbm, hbm, vmem, vmem),
        scratch_shapes=[
            pltpu.SMEM(route.shape, jnp.int32),
            pltpu.VMEM((2, req, slots, width), jnp.bfloat16),
            pltpu.VMEM((2, req, slots, width), jnp.bfloat16),
            pltpu.VMEM(level.shape, level.dtype),
            pltpu.VMEM(total.shape, total.dtype),
            pltpu.VMEM((n_grp,) + tokens[0].shape, tokens[0].dtype),
            pltpu.VMEM((total.shape[0], rows), jnp.float32),
            pltpu.SemaphoreType.DMA((3 + n_grp,)),
            pltpu.SemaphoreType.DMA((4,)),
        ],
        input_output_aliases={1: 0, 2: 1, 4: 2},
        compiler_params=pltpu.CompilerParams(vmem_limit_bytes=VMEM_LIMIT),
        cost_estimate=LIGHT,
        name="attend",
    )(route, out_k, out_v, early, late, level, total, *tokens)


def place(n_seq, first, part, out_k, out_v, sem):
    _, sent = half_of("seq", n_seq)
    _, count, rows, _ = part.shape
    return fetch(
        [
            (part.at[i], out.at[pl.ds(first, count), lanes(sent, rows), :])
            for i, out in enumerate((out_k, out_v))
        ],
        sem,
    )


def merge_kernel(n_seq, count, relative, size, *refs):
    stats, refs = refs[:count], refs[count:]
    picked_ref, weight_hbm, log_ref, part, _, _, decay_ref, out_ref, out_k, out_v = refs[:10]
    weight_ref, sem, sem_w = refs[10:]
    (load,) = fetch([(weight_hbm, weight_ref)], sem_w)
    placed = place(n_seq, 0, part, out_k, out_v, sem)
    heads, req, rows = log_ref.shape
    width = picked_ref.shape[1]
    seq = lax.axis_index("seq")
    places = [lax.rem(seq + count - k, count) if relative else jnp.int32(k) for k in range(count)]
    tops, masses, totals, accs = [
        [ref[p * req : (p + 1) * req, :] for ref in stats] for p in range(4)
    ]

    def later(place):
        total = jnp.zeros_like(totals[0])
        for k in range(count):
            total = total + jnp.where(places[k] > place, totals[k], 0.0)
        return total

    tops = [tops[k] + later(places[k]) for k in range(count)]
    top = functools.reduce(jnp.maximum, tops)
    scales = [jnp.exp(t - top) for t in tops]
    mass = sum(s * x for s, x in zip(scales, masses))
    acc = sum(s * x for s, x in zip(scales, accs))
    query, key, value, gate = [picked_ref[p * req : (p + 1) * req, :] for p in range(4)]
    one, two = iota((width, width), 0), iota((width, width), 1)
    same = (one // size == two // size).astype(jnp.float32).astype(jnp.bfloat16)
    own = split_dot(query * key, same) * (size**-0.5)
    past = top + gate
    joint = jnp.maximum(past, own)
    scale, self_weight = jnp.exp(past - joint), jnp.exp(own - joint)
    attended = (scale * acc + self_weight * value) / (scale * mass + self_weight)
    beyond = later(seq)
    for h in range(heads):
        decay_ref[h] = jnp.exp(log_ref[h] + beyond[:, h * size : h * size + 1])
    load.wait()
    out_ref[...] = dot(attended.astype(jnp.bfloat16), weight_ref[...])
    for copy in placed:
        copy.wait()


def merge_part(n_seq, stats, relative, picked, out_weight, logs, size, part, out_k, out_v):
    req = logs.shape[1]
    vmem = pl.BlockSpec(memory_space=pltpu.VMEM)
    hbm = pl.BlockSpec(memory_space=pl.ANY)
    whole = jax.ShapeDtypeStruct(out_k.shape, out_k.dtype)
    count = len(stats)
    return pl.pallas_call(
        functools.partial(merge_kernel, n_seq, count, relative, size),
        out_shape=(
            jax.ShapeDtypeStruct(logs.shape, jnp.float32),
            jax.ShapeDtypeStruct((req, out_weight.shape[1]), jnp.float32),
            whole,
            whole,
        ),
        in_specs=[vmem] * (count + 1) + [hbm] + [vmem] * 2 + [hbm] * 2,
        out_specs=(vmem, vmem, hbm, hbm),
        scratch_shapes=[
            pltpu.VMEM(out_weight.shape, out_weight.dtype),
            pltpu.SemaphoreType.DMA((2,)),
            pltpu.SemaphoreType.DMA((1,)),
        ],
        input_output_aliases={count + 4: 2, count + 5: 3},
        compiler_params=pltpu.CompilerParams(vmem_limit_bytes=VMEM_LIMIT),
        cost_estimate=MERGE,
        name="merge_and_project",
    )(*stats, picked, out_weight, logs, part, out_k, out_v)


def sum_kernel(count, *refs):
    parts, out = refs[:count], refs[count]
    me = lax.axis_index("head")
    total = jnp.zeros(out.shape, jnp.float32)
    for place in range(count):
        for k in range(count):
            total = total + jnp.where(lax.rem(me + count - k, count) == place, parts[k][...], 0.0)
    out[...] = total.astype(out.dtype)


def sum_part(parts):
    return pl.pallas_call(
        functools.partial(sum_kernel, len(parts)),
        out_shape=jax.ShapeDtypeStruct(parts[0].shape, jnp.bfloat16),
        in_specs=[pl.BlockSpec(memory_space=pltpu.VMEM)] * len(parts),
        out_specs=pl.BlockSpec(memory_space=pltpu.VMEM),
        compiler_params=pltpu.CompilerParams(vmem_limit_bytes=SMALL_LIMIT),
        cost_estimate=LIGHT,
        name="sum_heads",
    )(*parts)


def place_kernel(n_seq, first, part, old_k, old_v, out_k, out_v, sem):
    for copy in place(n_seq, first, part, out_k, out_v, sem):
        copy.wait()


def place_part(n_seq, first, part, out_k, out_v):
    hbm = pl.BlockSpec(memory_space=pl.ANY)
    vmem = pl.BlockSpec(memory_space=pltpu.VMEM)
    shape = jax.ShapeDtypeStruct(out_k.shape, out_k.dtype)
    return pl.pallas_call(
        functools.partial(place_kernel, n_seq, first),
        out_shape=(shape, shape),
        in_specs=[vmem, hbm, hbm],
        out_specs=(hbm, hbm),
        scratch_shapes=[pltpu.SemaphoreType.DMA((2,))],
        input_output_aliases={1: 0, 2: 1},
        compiler_params=pltpu.CompilerParams(vmem_limit_bytes=SMALL_LIMIT),
        cost_estimate=LIGHT,
        name="place_received",
    )(part, out_k, out_v)


def others(value, axis):
    count = lax.axis_size(axis)
    return [value] + [
        lax.ppermute(value, axis, [(i, (i + k) % count) for i in range(count)])
        for k in range(1, count)
    ]


def swap(value, n_seq):
    return lax.ppermute(value, "seq", [(0, 1), (1, 0)]) if n_seq == 2 else value


def shards(
    keys, values, log_forget, keep, merge_weight, lengths, route, fresh, new_forget, out_weight
):
    req, pos, width = keys.shape
    heads = log_forget.shape[1]
    size = width // heads
    n_seq, n_grp = lax.axis_size("seq"), lax.axis_size("grp")
    early, packed = first_part(
        n_seq,
        FIRST,
        lengths,
        keep,
        merge_weight,
        fresh.reshape(3 * req, width),
        new_forget,
        keys,
        values,
    )
    exchange = functools.partial(swap, n_seq=n_seq)
    first_received = exchange(early)
    tokens = others(packed, "grp")
    out_k, out_v, late, logs, level, total = own_part(
        n_seq,
        FIRST,
        lengths,
        keep,
        merge_weight,
        log_forget.transpose(1, 0, 2),
        keys,
        values,
        packed,
    )
    out_k, out_v, late, stats, picked = attend_part(
        n_seq, n_grp, heads, route, out_k, out_v, early, late, level, total, tokens
    )
    if n_seq == 2:
        all_stats = others(stats, "seq")
    else:
        gathered = lax.all_gather(stats, "seq")
        all_stats = [gathered[i] for i in range(n_seq)]
    late_received = exchange(late)
    decay, partial, out_k, out_v = merge_part(
        n_seq,
        all_stats,
        n_seq == 2,
        picked,
        out_weight,
        logs,
        size,
        first_received,
        out_k,
        out_v,
    )
    layer_out = sum_part(others(partial, "head"))
    out_k, out_v = place_part(n_seq, FIRST, late_received, out_k, out_v)
    if n_seq != 2:
        out_k, out_v = (
            lax.all_to_all(x, "seq", split_axis=1, concat_axis=1, tiled=True) for x in (out_k, out_v)
        )
    return out_k, out_v, decay.transpose(1, 0, 2), layer_out


def solution(mesh):
    return jax.shard_map(
        shards,
        mesh=mesh,
        in_specs=(
            P("grp", "seq", "head"),
            P("grp", "seq", "head"),
            P("grp", "head", "seq"),
            P("grp", "seq"),
            P("grp", "seq"),
            P("grp"),
            P("grp"),
            P(None, "grp", "head"),
            P("grp", "head"),
            P("head", "seq"),
        ),
        out_specs=(
            P("grp", "seq", "head"),
            P("grp", "seq", "head"),
            P("grp", "head", "seq"),
            P("grp", "seq"),
        ),
        check_vma=False,
    )
```

time: 61.3 us -> 45.7 us (0.75)
  waiting for transfers between devices: 22 us -> 6.71 us
  Pallas kernels: 20.1 us -> 22.4 us
  local copies, waits for them, and re-layouts: 4.07 us -> 1.94 us
    ppermute x7, waiting for transfers between devices: 22 us -> 5.55 us  [others(): lax.ppermute(value, axis, [(i, (i + k) % count) for i in range(count)])]
    pallas_call x4, Pallas kernels: 15.5 us -> 20.9 us  [the longest x1 9.42 us: own_part(): pl.pallas_call(functools.partial(own_kernel, n_seq, first), out_shape=(wh...]
    pallas_call x2 -> x1, Pallas kernels: 4.03 us -> 0.89 us  [place_part(): pl.pallas_call(functools.partial(place_kernel, n_seq, first), out_shape=(...]
    unnamed x16 -> x10, local copies, waits for them, and re-layouts: 4.07 us -> 1.94 us
    ppermute x7, starting transfers between devices: 10.8 us -> 9.16 us  [others(): lax.ppermute(value, axis, [(i, (i + k) % count) for i in range(count)])]
    ppermute x2, starting transfers between devices: 3.09 us -> 4.5 us  [swap(): return lax.ppermute(value, 'seq', [(0, 1), (1, 0)]) if n_seq == 2 else value]
    ppermute x2, waiting for transfers between devices: 0.01 us -> 1.16 us  [swap(): return lax.ppermute(value, 'seq', [(0, 1), (1, 0)]) if n_seq == 2 else value]
  transfers between devices with their start and end apart: 9 -> 9, of which waited for: 5 -> 5; matrix products, arithmetic and copies ran while one was open for 0% -> 0% of each run, Pallas kernels for 23% -> 38%
where the time goes in v3:
time: 45.7 us; the launch traced here: 45.5 us
  Pallas kernels  22.4 us (49%)
  starting transfers between devices  13.7 us (30%)
  waiting for transfers between devices  6.71 us (15%)
  local copies, waits for them, and re-layouts  1.94 us (4%)
  between operations  0.72 us (2%)
    pallas_call x1, Pallas kernels, own_part(): pl.pallas_call(functools.partial(own_kernel, n_seq, first), out_shape=(wh...  9.42 us
    ppermute x7, starting transfers between devices, others(): lax.ppermute(value, axis, [(i, (i + k) % count) for i in range(count)])  9.16 us
    ppermute x7, waiting for transfers between devices, others(): lax.ppermute(value, axis, [(i, (i + k) % count) for i in range(count)])  5.55 us
    ppermute x2, starting transfers between devices, swap(): return lax.ppermute(value, 'seq', [(0, 1), (1, 0)]) if n_seq == 2 else value  4.5 us
    pallas_call x1, Pallas kernels, first_part(): pl.pallas_call(functools.partial(first_kernel, n_seq), out_shape=(jax.Sha...  4.38 us
    pallas_call x1, Pallas kernels, attend_part(): pl.pallas_call(functools.partial(attend_kernel, n_seq, n_grp, heads, firs...  3.62 us
    pallas_call x1, Pallas kernels, merge_part(): pl.pallas_call(functools.partial(merge_kernel, n_seq, count, relative, si...  3.48 us
    unnamed x10, local copies, waits for them, and re-layouts  1.94 us
  transfers between devices with their start and end apart: 9, of which 5 were waited for; matrix products, arithmetic and copies ran while one was open for 0% of the time, Pallas kernels for 38%

profile of v3, /device:TPU:0, one launch (start us, length us, event | category | flops | bytes accessed | tf_op | source)
XLA Modules:
  0.0 45.5 jit_solution(11725749371100219646)
XLA Ops:
  0.6 4.4 %compact_first_sent.1 = (bf16[2,4,128,384]{3,2,1,0:T(8,128)(2,1)}, bf16[32,384]{1,0:T(8,128)(2,1)}) custom-call(s32[8]{0:T(128)} %len_hbm.3, s32[8,512]{1,0:T(8,128)} %keep_hbm.3, f32[8,512]{1,0:T(8,128)} %weight_hbm.3, bf16[24,384]{1,0:T(8,128)(2,1)} %bitcast.4, bf16[8,6]{1,0:T(8,128)(2,1)} %gate_hbm.1, bf16[8,512,384]{2,1,0:T(8,128)(2,1)} %keys.3, ...), custom_call_target="tpu_custom_call" | custom-call | flops 1 | bytes 1 | tf_op jit(solution)/shard_map/compact_first_sent/pallas_call | solution.py:152
  5.0 3.0 %collective-permute-start.5 = (bf16[2,4,128,384]{3,2,1,0:T(8,128)(2,1)}, bf16[2,4,128,384]{3,2,1,0:T(8,128)(2,1)}, u32[]{:S(2)}, u32[]{:S(2)}) collective-permute-start(bf16[2,4,128,384]{3,2,1,0:T(8,128)(2,1)} %get-tuple-element.26.refs_3_), channel_id=1, source_target_pairs={{0,4},{4,0},{1,5},{5,1},{2,6},{6,2},{3,7},{7,3},{8,12},{12,8},{9,1... | collective-permute-start | bytes 2359304 | tf_op jit(solution)/shard_map/ppermute | solution.py:554
  8.0 0.0 collective-permute-start
  8.0 1.6 %collective-permute-start.1 = (bf16[32,384]{1,0:T(8,128)(2,1)}, bf16[32,384]{1,0:T(8,128)(2,1)S(1)}, u32[]{:S(2)}, u32[]{:S(2)}) collective-permute-start(bf16[32,384]{1,0:T(8,128)(2,1)} %get-tuple-element.23.packed_hbm.refs_7_), channel_id=1, source_target_pairs={{0,16},{8,24},{16,0},{24,8},{1,17},{9,25},{17,1},{25,9},{2,18},{10... | collective-permute-start | bytes 73736 | tf_op jit(solution)/shard_map/ppermute | solution.py:548
  9.6 1.4 %collective-permute-start.2 = (bf16[32,384]{1,0:T(8,128)(2,1)}, bf16[32,384]{1,0:T(8,128)(2,1)S(1)}, u32[]{:S(2)}, u32[]{:S(2)}) collective-permute-start(bf16[32,384]{1,0:T(8,128)(2,1)} %get-tuple-element.23.packed_hbm.refs_7_), channel_id=1, source_target_pairs={{0,24},{8,0},{16,8},{24,16},{1,25},{9,1},{17,9},{25,17},{2,26},{10... | collective-permute-start | bytes 73736 | tf_op jit(solution)/shard_map/ppermute | solution.py:548
  11.0 9.4 %compact_own.1 = (bf16[8,256,384]{2,1,0:T(8,128)(2,1)}, bf16[8,256,384]{2,1,0:T(8,128)(2,1)}, bf16[2,4,128,384]{3,2,1,0:T(8,128)(2,1)}, f32[6,8,256]{2,1,0:T(8,1...) custom-call(s32[8]{0:T(128)} %len_hbm.3, s32[8,512]{1,0:T(8,128)} %keep_hbm.3, f32[8,512]{1,0:T(8,128)} %weight_hbm.3, ...), custom_call_target="tpu_custom_call" | custom-call | flops 1 | bytes 1 | tf_op jit(solution)/shard_map/compact_own/pallas_call | solution.py:288
  20.4 0.0 collective-permute-done.refs_8_
  20.5 0.0 copy-start.1
  20.5 0.0 collective-permute-done.1.refs_9_
  20.5 0.0 copy-start.2
  20.5 0.0 collective-permute-done.2.refs_10_
  20.5 0.0 copy-start.3
  20.5 0.6 %copy-done.1 = bf16[32,384]{1,0:T(8,128)(2,1)} copy-done((bf16[32,384]{1,0:T(8,128)(2,1)}, bf16[32,384]{1,0:T(8,128)(2,1)S(1)}, u32[]{:S(2)}) %copy-start.1) | copy-done | bytes 24600
  21.1 0.0 copy-done.2
  21.1 0.0 copy-done.3
  21.1 3.6 %attend.1 = (bf16[8,256,384]{2,1,0:T(8,128)(2,1)}, bf16[8,256,384]{2,1,0:T(8,128)(2,1)}, bf16[2,4,128,384]{3,2,1,0:T(8,128)(2,1)}, f32[32,384]{1,0:T(8,128)}, f32[32,384]{1,0:T(8,128)}) custom-call(s32[8]{0:T(128)} %refs_0_.1, bf16[8,256,384]{2,1,0:T(8,128)(2,1)} %get-tuple-element.24.refs_1_, ...), custom_call_target="tpu_custom_call", output_to_operand_aliasing={{0}: (1, {}), {1}: (2, {}), {2}: (4, {})} | custom-call | flops 1 | bytes 1 | tf_op jit(solution)/shard_map/attend/pallas_call | solution.py:396
  24.7 0.6 %collective-permute-start.4 = (f32[32,384]{1,0:T(8,128)}, f32[32,384]{1,0:T(8,128)S(1)}, u32[]{:S(2)}, u32[]{:S(2)}) collective-permute-start(f32[32,384]{1,0:T(8,128)} %get-tuple-element.31.refs_0_), channel_id=1, source_target_pairs={{0,4},{4,0},{1,5},{5,1},{2,6},{6,2},{3,7},{7,3},{8,12},{12,8},{9,1... | collective-permute-start | bytes 147464 | tf_op jit(solution)/shard_map/ppermute | solution.py:548
  25.3 1.5 %collective-permute-start.3 = (bf16[2,4,128,384]{3,2,1,0:T(8,128)(2,1)}, bf16[2,4,128,384]{3,2,1,0:T(8,128)(2,1)S(1)}, u32[]{:S(2)}, u32[]{:S(2)}) collective-permute-start(bf16[2,4,128,384]{3,2,1,0:T(8,128)(2,1)} %get-tuple-element.30), channel_id=1, source_target_pairs={{0,4},{4,0},{1,5},{5,1},{2,6},{6,2},{3,7},{7,3},{8,12},{12,8},{9,1... | collective-permute-start | bytes 2359304 | tf_op jit(solution)/shard_map/ppermute | solution.py:554
  26.8 2.9 %collective-permute-done.4.refs_1_ = f32[32,384]{1,0:T(8,128)S(1)} collective-permute-done((f32[32,384]{1,0:T(8,128)}, f32[32,384]{1,0:T(8,128)S(1)}, u32[]{:S(2)}, u32[]{:S(2)}) %collective-permute-start.4) | collective-permute-done | bytes 49184 | tf_op jit(solution)/shard_map/ppermute | solution.py:548
  29.7 0.0 copy-start.4
  29.7 0.0 collective-permute-done.5.refs_5_
  29.7 0.6 %copy-done.4 = f32[32,384]{1,0:T(8,128)} copy-done((f32[32,384]{1,0:T(8,128)}, f32[32,384]{1,0:T(8,128)S(1)}, u32[]{:S(2)}) %copy-start.4) | copy-done | bytes 49176
  30.3 3.5 %merge_and_project.1 = (f32[6,8,256]{2,1,0:T(8,128)}, f32[8,768]{1,0:T(8,128)}, bf16[8,256,384]{2,1,0:T(8,128)(2,1)}, bf16[8,256,384]{2,1,0:T(8,128)(2,1)}) custom-call(f32[32,384]{1,0:T(8,128)} %get-tuple-element.31.refs_0_, f32[32,384]{1,0:T(8,128)} %copy-done.4, ...), custom_call_target="tpu_custom_call", output_to_operand_aliasing={{2}: (6, {}), {3}: (7, {})} | custom-call | flops 68719476736 | bytes 1 | tf_op jit(solution)/shard_map/merge_and_project/pallas_call | solution.py:479
  33.8 1.6 %collective-permute-start.6 = (f32[8,768]{1,0:T(8,128)}, f32[8,768]{1,0:T(8,128)S(1)}, u32[]{:S(2)}, u32[]{:S(2)}) collective-permute-start(f32[8,768]{1,0:T(8,128)} %get-tuple-element.41.refs_0_), channel_id=1, source_target_pairs={{0,1},{1,2},{2,3},{3,0},{4,5},{5,6},{6,7},{7,4},{8,9},{9,10},{10,1... | collective-permute-start | bytes 73736 | tf_op jit(solution)/shard_map/ppermute | solution.py:548
  35.4 2.6 %collective-permute-start.7 = (f32[8,768]{1,0:T(8,128)}, f32[8,768]{1,0:T(8,128)S(1)}, u32[]{:S(2)}, u32[]{:S(2)}) collective-permute-start(f32[8,768]{1,0:T(8,128)} %get-tuple-element.41.refs_0_), channel_id=1, source_target_pairs={{0,2},{1,3},{2,0},{3,1},{4,6},{5,7},{6,4},{7,5},{8,10},{9,11},{10,... | collective-permute-start | bytes 73736 | tf_op jit(solution)/shard_map/ppermute | solution.py:548
  38.0 1.4 %collective-permute-start.8 = (f32[8,768]{1,0:T(8,128)}, f32[8,768]{1,0:T(8,128)S(1)}, u32[]{:S(2)}, u32[]{:S(2)}) collective-permute-start(f32[8,768]{1,0:T(8,128)} %get-tuple-element.41.refs_0_), channel_id=1, source_target_pairs={{0,3},{1,0},{2,1},{3,2},{4,7},{5,4},{6,5},{7,6},{8,11},{9,8},{10,9... | collective-permute-start | bytes 73736 | tf_op jit(solution)/shard_map/ppermute | solution.py:548
  39.4 0.3 collective-permute-done.6.refs_1_
  39.7 0.7 %collective-permute-done.7.refs_2_ = f32[8,768]{1,0:T(8,128)S(1)} collective-permute-done((f32[8,768]{1,0:T(8,128)}, f32[8,768]{1,0:T(8,128)S(1)}, u32[]{:S(2)}, u32[]{:S(2)}) %collective-permute-start.7) | collective-permute-done | bytes 24608 | tf_op jit(solution)/shard_map/ppermute | solution.py:548
  40.3 1.7 %collective-permute-done.8.refs_3_ = f32[8,768]{1,0:T(8,128)S(1)} collective-permute-done((f32[8,768]{1,0:T(8,128)}, f32[8,768]{1,0:T(8,128)S(1)}, u32[]{:S(2)}, u32[]{:S(2)}) %collective-permute-start.8) | collective-permute-done | bytes 24608 | tf_op jit(solution)/shard_map/ppermute | solution.py:548
  42.0 0.0 copy-start
  42.0 0.7 %copy-done = f32[8,768]{1,0:T(8,128)S(1)} copy-done((f32[8,768]{1,0:T(8,128)S(1)}, f32[8,768]{1,0:T(8,128)}, u32[]{:S(2)}) %copy-start) | copy-done | bytes 24600
  42.8 0.6 %sum_heads.1 = bf16[8,768]{1,0:T(8,128)(2,1)} custom-call(f32[8,768]{1,0:T(8,128)S(1)} %copy-done, f32[8,768]{1,0:T(8,128)S(1)} %collective-permute-done.6.refs_1_, f32[8,768]{1,0:T(8,128)S(1)} %collective-permute-done.7.refs_2_, f32[8,768]{1,0:T(8,128)S(1)} %collective-permute-done.8.refs_3_), custom_call_target="tpu_custom_call" | custom-call | flops 1 | bytes 1 | tf_op jit(solution)/shard_map/sum_heads/pallas_call | solution.py:512
  43.4 1.2 %collective-permute-done.3.part = bf16[2,4,128,384]{3,2,1,0:T(8,128)(2,1)S(1)} collective-permute-done((bf16[2,4,128,384]{3,2,1,0:T(8,128)(2,1)}, bf16[2,4,128,384]{3,2,1,0:T(8,128)(2,1)S(1)}, u32[]{:S(2)}, u32[]{:S(2)}) %collective-permute-start.3) | collective-permute-done | bytes 786464 | tf_op jit(solution)/shard_map/ppermute | solution.py:554
  44.6 0.9 %place_received.1 = (bf16[8,256,384]{2,1,0:T(8,128)(2,1)}, bf16[8,256,384]{2,1,0:T(8,128)(2,1)}) custom-call(bf16[2,4,128,384]{3,2,1,0:T(8,128)(2,1)S(1)} %collective-permute-done.3.part, bf16[8,256,384]{2,1,0:T(8,128)(2,1)} %get-tuple-element.36.old_k, bf16[8,256,384]{2,1,0:T(8,128)(2,1)} %get-tuple-element.37.old_v), custom_call_target="tpu_custom_call", output_to_operand_aliasing={{0}: (1, {}), {1}: (2, {})} | custom-call | flops 1 | bytes 1 | tf_op jit(solution)/shard_map/place_received/pallas_call | solution.py:532
Async XLA Ops:
  5.0 24.7 %collective-permute-start.5 = (bf16[2,4,128,384]{3,2,1,0:T(8,128)(2,1)}, bf16[2,4,128,384]{3,2,1,0:T(8,128)(2,1)}, u32[]{:S(2)}, u32[]{:S(2)}) collective-permute-start(bf16[2,4,128,384]{3,2,1,0:T(8,128)(2,1)} %get-tuple-element.26.refs_3_), channel_id=1, source_target_pairs={{0,4},{4,0},{1,5},{5,1},{2,6},{6,2},{3,7},{7,3},{8,12},{12,8},{9,1... | collective-permute-start | bytes 2359304 | tf_op jit(solution)/shard_map/ppermute | solution.py:554
  8.0 12.4 %collective-permute-start = (bf16[32,384]{1,0:T(8,128)(2,1)}, bf16[32,384]{1,0:T(8,128)(2,1)S(1)}, u32[]{:S(2)}, u32[]{:S(2)}) collective-permute-start(bf16[32,384]{1,0:T(8,128)(2,1)} %get-tuple-element.23.packed_hbm.refs_7_), channel_id=1, source_target_pairs={{0,8},{8,16},{16,24},{24,0},{1,9},{9,17},{17,25},{25,1},{2,10},{10... | collective-permute-start | bytes 73736 | tf_op jit(solution)/shard_map/ppermute | solution.py:548
  8.0 12.4 %collective-permute-start.1 = (bf16[32,384]{1,0:T(8,128)(2,1)}, bf16[32,384]{1,0:T(8,128)(2,1)S(1)}, u32[]{:S(2)}, u32[]{:S(2)}) collective-permute-start(bf16[32,384]{1,0:T(8,128)(2,1)} %get-tuple-element.23.packed_hbm.refs_7_), channel_id=1, source_target_pairs={{0,16},{8,24},{16,0},{24,8},{1,17},{9,25},{17,1},{25,9},{2,18},{10... | collective-permute-start | bytes 73736 | tf_op jit(solution)/shard_map/ppermute | solution.py:548
  9.6 10.9 %collective-permute-start.2 = (bf16[32,384]{1,0:T(8,128)(2,1)}, bf16[32,384]{1,0:T(8,128)(2,1)S(1)}, u32[]{:S(2)}, u32[]{:S(2)}) collective-permute-start(bf16[32,384]{1,0:T(8,128)(2,1)} %get-tuple-element.23.packed_hbm.refs_7_), channel_id=1, source_target_pairs={{0,24},{8,0},{16,8},{24,16},{1,25},{9,1},{17,9},{25,17},{2,26},{10... | collective-permute-start | bytes 73736 | tf_op jit(solution)/shard_map/ppermute | solution.py:548
  20.5 0.6 %copy-start.1 = (bf16[32,384]{1,0:T(8,128)(2,1)}, bf16[32,384]{1,0:T(8,128)(2,1)S(1)}, u32[]{:S(2)}) copy-start(bf16[32,384]{1,0:T(8,128)(2,1)S(1)} %collective-permute-done.refs_8_) | copy-start | bytes 73732
  20.5 0.6 %copy-start.2 = (bf16[32,384]{1,0:T(8,128)(2,1)}, bf16[32,384]{1,0:T(8,128)(2,1)S(1)}, u32[]{:S(2)}) copy-start(bf16[32,384]{1,0:T(8,128)(2,1)S(1)} %collective-permute-done.1.refs_9_) | copy-start | bytes 73732
  20.5 0.6 %copy-start.3 = (bf16[32,384]{1,0:T(8,128)(2,1)}, bf16[32,384]{1,0:T(8,128)(2,1)S(1)}, u32[]{:S(2)}) copy-start(bf16[32,384]{1,0:T(8,128)(2,1)S(1)} %collective-permute-done.2.refs_10_) | copy-start | bytes 73732
  24.7 5.0 %collective-permute-start.4 = (f32[32,384]{1,0:T(8,128)}, f32[32,384]{1,0:T(8,128)S(1)}, u32[]{:S(2)}, u32[]{:S(2)}) collective-permute-start(f32[32,384]{1,0:T(8,128)} %get-tuple-element.31.refs_0_), channel_id=1, source_target_pairs={{0,4},{4,0},{1,5},{5,1},{2,6},{6,2},{3,7},{7,3},{8,12},{12,8},{9,1... | collective-permute-start | bytes 147464 | tf_op jit(solution)/shard_map/ppermute | solution.py:548
  25.3 19.3 %collective-permute-start.3 = (bf16[2,4,128,384]{3,2,1,0:T(8,128)(2,1)}, bf16[2,4,128,384]{3,2,1,0:T(8,128)(2,1)S(1)}, u32[]{:S(2)}, u32[]{:S(2)}) collective-permute-start(bf16[2,4,128,384]{3,2,1,0:T(8,128)(2,1)} %get-tuple-element.30), channel_id=1, source_target_pairs={{0,4},{4,0},{1,5},{5,1},{2,6},{6,2},{3,7},{7,3},{8,12},{12,8},{9,1... | collective-permute-start | bytes 2359304 | tf_op jit(solution)/shard_map/ppermute | solution.py:554
  29.7 0.6 %copy-start.4 = (f32[32,384]{1,0:T(8,128)}, f32[32,384]{1,0:T(8,128)S(1)}, u32[]{:S(2)}) copy-start(f32[32,384]{1,0:T(8,128)S(1)} %collective-permute-done.4.refs_1_) | copy-start | bytes 147460
  33.8 5.9 %collective-permute-start.6 = (f32[8,768]{1,0:T(8,128)}, f32[8,768]{1,0:T(8,128)S(1)}, u32[]{:S(2)}, u32[]{:S(2)}) collective-permute-start(f32[8,768]{1,0:T(8,128)} %get-tuple-element.41.refs_0_), channel_id=1, source_target_pairs={{0,1},{1,2},{2,3},{3,0},{4,5},{5,6},{6,7},{7,4},{8,9},{9,10},{10,1... | collective-permute-start | bytes 73736 | tf_op jit(solution)/shard_map/ppermute | solution.py:548
  35.4 4.9 %collective-permute-start.7 = (f32[8,768]{1,0:T(8,128)}, f32[8,768]{1,0:T(8,128)S(1)}, u32[]{:S(2)}, u32[]{:S(2)}) collective-permute-start(f32[8,768]{1,0:T(8,128)} %get-tuple-element.41.refs_0_), channel_id=1, source_target_pairs={{0,2},{1,3},{2,0},{3,1},{4,6},{5,7},{6,4},{7,5},{8,10},{9,11},{10,... | collective-permute-start | bytes 73736 | tf_op jit(solution)/shard_map/ppermute | solution.py:548
  38.0 4.0 %collective-permute-start.8 = (f32[8,768]{1,0:T(8,128)}, f32[8,768]{1,0:T(8,128)S(1)}, u32[]{:S(2)}, u32[]{:S(2)}) collective-permute-start(f32[8,768]{1,0:T(8,128)} %get-tuple-element.41.refs_0_), channel_id=1, source_target_pairs={{0,3},{1,0},{2,1},{3,2},{4,7},{5,4},{6,5},{7,6},{8,11},{9,8},{10,9... | collective-permute-start | bytes 73736 | tf_op jit(solution)/shard_map/ppermute | solution.py:548
  42.0 0.7 %copy-start = (f32[8,768]{1,0:T(8,128)S(1)}, f32[8,768]{1,0:T(8,128)}, u32[]{:S(2)}) copy-start(f32[8,768]{1,0:T(8,128)} %get-tuple-element.41.refs_0_) | copy-start | bytes 73732

commit v4 on v3

--- a/solution.py
+++ b/solution.py
@@ -14,6 +14,7 @@
 SLOT_LOG = SLOTS.bit_length() - 1
 EMPTY_LOG = -10000.0
 FIRST = 4
+STEP = 2
 VMEM_LIMIT = 63 * 1024 * 1024
 SMALL_LIMIT = 8 * 1024 * 1024
 
@@ -57,6 +58,19 @@
     for r in range(ref.shape[0]):
         picked = jnp.where(row == r, ref[r], picked)
     return picked
+
+
+def live_blocks(lengths, r, start, most):
+    return jnp.clip((lengths[r] - start) >> BLOCK_LOG, 0, most)
+
+
+def offsets(lengths, first, start, most):
+    total = jnp.int32(0)
+    ahead = []
+    for r in range(first, lengths.shape[0]):
+        ahead.append(total)
+        total = total + live_blocks(lengths, r, start, most)
+    return ahead, total
 
 
 def plan(keep, weight, start, len_ref):
@@ -94,7 +108,8 @@
 
 
 def first_kernel(n_seq, len_hbm, keep_hbm, weight_hbm, fresh_hbm, gate_hbm, keys, values, *rest):
-    out, packed, lengths, keep, weight, fresh, gates, raw, rows, sem_s, sem_r, sem_o = rest
+    out, packed, size_ref, lengths, keep, weight, fresh, gates, raw, rows = rest[:10]
+    sem_s, sem_r, sem_o = rest[10:]
     _, sent = half_of("seq", n_seq)
     width = raw.shape[2]
     count = raw.shape[1]
@@ -120,6 +135,10 @@
         copy.wait()
     start = lax.axis_index("seq") * (2 * width) + sent * width
     slot, factor = plan(keep[...], weight[...], start, lengths)
+    most = width // BLOCK
+    _, total = offsets(lengths, count, width, most)
+    sizes = most * (lengths.shape[0] - count) // STEP
+    size_ref[0] = jnp.clip((total - 1) >> (STEP.bit_length() - 1), 0, sizes - 1)
 
     new, gate = fresh[...].astype(jnp.float32), gates[...].astype(jnp.float32)
     req, heads = gate.shape
@@ -154,9 +173,10 @@
         out_shape=(
             jax.ShapeDtypeStruct(rows, jnp.bfloat16),
             jax.ShapeDtypeStruct((fresh.shape[0] + req, width), jnp.bfloat16),
+            jax.ShapeDtypeStruct((1,), jnp.int32),
         ),
         in_specs=[hbm] * 7,
-        out_specs=(hbm, vmem),
+        out_specs=(hbm, vmem, pl.BlockSpec(memory_space=pltpu.SMEM)),
         scratch_shapes=[
             pltpu.SMEM(lengths.shape, jnp.int32),
             pltpu.VMEM((req, half), jnp.int32),
@@ -179,8 +199,8 @@
     n_seq, first, len_hbm, keep_hbm, weight_hbm, forget_hbm, keys, values, packed_hbm, *rest
 ):
     out_k, out_v, chunk, log_ref, level_ref, total_ref = rest[:6]
-    lengths, keep, weight, gates, raw, late, forget, rows, rows_late = rest[6:15]
-    sem_s, sem_l, sem_r, sem_c, sem_o = rest[15:]
+    lengths, keep, weight, gates, raw, late, forget, rows, rows_late, zeros = rest[6:16]
+    sem_s, sem_l, sem_r, sem_c, sem_o, sem_z = rest[16:]
     own, sent = half_of("seq", n_seq)
     seq = lax.axis_index("seq")
     heads, req, pos = forget_hbm.shape
@@ -207,8 +227,18 @@
         ],
         sem_r,
     )
+    zeros[...] = jnp.zeros_like(zeros)
+    stores = fetch(
+        [
+            (zeros, out.at[r, lanes(sent, slots), :])
+            for r in range(first, req)
+            for out in (out_k, out_v)
+        ],
+        sem_z,
+    )
     for copy in small:
         copy.wait()
+    ahead, _ = offsets(lengths, first, seq * pos + sent * half, half // BLOCK)
 
     forget[...] = jnp.zeros_like(forget)
     live = seq * pos + iota((req, pos), 1) < by_row(lengths, iota((req, pos), 0))
@@ -224,7 +254,6 @@
     begins = iota((pos, slots), 0) >> BLOCK_LOG
     last = iota((req * pad, slots), 1) & (SLOTS - 1) == SLOTS - 1
 
-    stores = []
     for i, h in enumerate((own, sent)):
         slot, factor = plan(
             keep[:, lanes(h, half)], weight[:, lanes(h, half)], seq * pos + h * half, lengths
@@ -255,15 +284,12 @@
                     )
                     stores[-1].start()
             elif r >= first:
+                at = pl.ds(pl.multiple_of(ahead[r - first] * SLOTS, SLOTS), slots)
                 for k in range(2):
                     late_slabs[2 * (r - first) + k].wait()
-                    rows_late[k, r - first] = dot(chosen, late[k, r - first]).astype(jnp.bfloat16)
-                stores.append(
-                    pltpu.make_async_copy(
-                        rows_late.at[:, r - first], chunk.at[:, r - first], sem_c.at[r - first]
-                    )
-                )
-                stores[-1].start()
+                    rows_late[k, at, :] = dot(chosen, late[k, r - first]).astype(jnp.bfloat16)
+        if i == 1:
+            stores += fetch([(rows_late, chunk)], sem_c)
         at = [
             jnp.concatenate([x[p * pad : (p + 1) * pad] for x in found], axis=0) for p in range(6)
         ]
@@ -290,7 +316,7 @@
         out_shape=(
             whole,
             whole,
-            jax.ShapeDtypeStruct((2, late, slots, width), jnp.bfloat16),
+            jax.ShapeDtypeStruct((2, late * slots, width), jnp.bfloat16),
             jax.ShapeDtypeStruct((heads, req, 2 * slots), jnp.float32),
             jax.ShapeDtypeStruct((2, req * pad, slots), jnp.float32),
             jax.ShapeDtypeStruct((req * pad, LANES), jnp.float32),
@@ -306,12 +332,14 @@
             pltpu.VMEM((2, late, half, width), jnp.bfloat16),
             pltpu.VMEM((pos // LANES, req * pad, LANES), jnp.float32),
             pltpu.VMEM((2, req, slots, width), jnp.bfloat16),
-            pltpu.VMEM((2, late, slots, width), jnp.bfloat16),
+            pltpu.VMEM((2, late * slots, width), jnp.bfloat16),
+            pltpu.VMEM((slots, width), jnp.bfloat16),
             pltpu.SemaphoreType.DMA((4,)),
             pltpu.SemaphoreType.DMA((2 * late,)),
             pltpu.SemaphoreType.DMA((2 * req,)),
-            pltpu.SemaphoreType.DMA((late,)),
+            pltpu.SemaphoreType.DMA((1,)),
             pltpu.SemaphoreType.DMA((2 * req,)),
+            pltpu.SemaphoreType.DMA((2 * late,)),
         ],
         compiler_params=pltpu.CompilerParams(vmem_limit_bytes=VMEM_LIMIT),
         cost_estimate=LIGHT,
@@ -320,32 +348,41 @@
 
 
 def attend_kernel(n_seq, n_grp, heads, first, *refs):
-    route_hbm, out_k, out_v, early, late, level_hbm, total_hbm = refs[:7]
-    tokens, rest = refs[7 : 7 + n_grp], refs[7 + n_grp :]
+    len_hbm, route_hbm, out_k, out_v, early, late, level_hbm, total_hbm = refs[:8]
+    tokens, rest = refs[8 : 8 + n_grp], refs[8 + n_grp :]
     _, _, _, stats_ref, picked_ref = rest[:5]
-    route, own_rows, sent_rows, level, total, fresh, scores, sem_s, sem_r = rest[5:]
-    own, _ = half_of("seq", n_seq)
+    lengths, route, own_rows, sent_rows, late_rows, level, total, fresh, scores = rest[5:14]
+    sem_s, sem_r = rest[14:]
+    own, sent = half_of("seq", n_seq)
     kinds, width = picked_ref.shape
     req = kinds // 4
     size = width // heads
     slots = own_rows.shape[2]
     pad = total.shape[0] // req
     small = fetch(
-        [(route_hbm, route), (level_hbm, level), (total_hbm, total)]
+        [(len_hbm, lengths), (route_hbm, route), (level_hbm, level), (total_hbm, total)]
         + [(x, fresh.at[k]) for k, x in enumerate(tokens)],
         sem_s,
     )
     slabs = fetch(
         [
             (out_k.at[:, lanes(own, slots), :], own_rows.at[0]),
-            (early, sent_rows.at[:, pl.ds(0, first)]),
-            (late, sent_rows.at[:, pl.ds(first, req - first)]),
+            (early, sent_rows),
+            (late, late_rows),
             (out_v.at[:, lanes(own, slots), :], own_rows.at[1]),
         ],
         sem_r,
     )
     for copy in small:
         copy.wait()
+    start = lax.axis_index("seq") * (4 * slots) + sent * (2 * slots)
+    ahead, _ = offsets(lengths, first, start, slots // SLOTS)
+
+    def sent_part(i, r):
+        if r < first:
+            return sent_rows[i, r]
+        at = pl.multiple_of(ahead[r - first] * SLOTS, SLOTS)
+        return late_rows[i, pl.ds(at, slots), :]
 
     shape = (kinds, kinds)
     to, frm = iota(shape, 0), iota(shape, 1)
@@ -366,7 +403,7 @@
         query = jnp.where(mine, picked[r : r + 1, :], 0.0).astype(jnp.bfloat16)
         here = slice(r * pad, (r + 1) * pad)
         scores[here, :slots] = dot_nt(query, own_rows[0, r])
-        scores[here, slots:] = dot_nt(query, sent_rows[0, r])
+        scores[here, slots:] = dot_nt(query, sent_part(0, r))
     logit = scores[...] * (size**-0.5) + jnp.concatenate([level[0], level[1]], axis=1)
     top = jnp.max(logit, axis=1, keepdims=True)
     weights = jnp.exp(logit - top).astype(jnp.bfloat16).astype(jnp.float32)
@@ -379,14 +416,14 @@
 
     for r in range(req):
         w = weights[r * pad : (r + 1) * pad].astype(jnp.bfloat16)
-        acc = dot(w[:, :slots], own_rows[1, r]) + dot(w[:, slots:], sent_rows[1, r])
+        acc = dot(w[:, :slots], own_rows[1, r]) + dot(w[:, slots:], sent_part(1, r))
         acc = jnp.sum(jnp.where(mine, acc, 0.0), axis=0, keepdims=True)
         for p, x in enumerate((top, mass, total[:, :1])):
             stats_ref[p * req + r : p * req + r + 1, :] = spread_out(x, r)
         stats_ref[3 * req + r : 3 * req + r + 1, :] = acc
 
 
-def attend_part(n_seq, n_grp, heads, route, out_k, out_v, early, late, level, total, tokens):
+def attend_part(n_seq, n_grp, heads, lengths, route, out_k, out_v, early, late, level, total, tokens):
     req, rows, width = out_k.shape
     slots, first = rows // 2, early.shape[1]
     hbm = pl.BlockSpec(memory_space=pl.ANY)
@@ -396,24 +433,26 @@
     return pl.pallas_call(
         functools.partial(attend_kernel, n_seq, n_grp, heads, first),
         out_shape=(whole, whole, jax.ShapeDtypeStruct(late.shape, late.dtype), small, small),
-        in_specs=[hbm] * (7 + n_grp),
+        in_specs=[hbm] * (8 + n_grp),
         out_specs=(hbm, hbm, hbm, vmem, vmem),
         scratch_shapes=[
+            pltpu.SMEM(lengths.shape, jnp.int32),
             pltpu.SMEM(route.shape, jnp.int32),
             pltpu.VMEM((2, req, slots, width), jnp.bfloat16),
-            pltpu.VMEM((2, req, slots, width), jnp.bfloat16),
+            pltpu.VMEM(early.shape, early.dtype),
+            pltpu.VMEM(late.shape, late.dtype),
             pltpu.VMEM(level.shape, level.dtype),
             pltpu.VMEM(total.shape, total.dtype),
             pltpu.VMEM((n_grp,) + tokens[0].shape, tokens[0].dtype),
             pltpu.VMEM((total.shape[0], rows), jnp.float32),
-            pltpu.SemaphoreType.DMA((3 + n_grp,)),
+            pltpu.SemaphoreType.DMA((4 + n_grp,)),
             pltpu.SemaphoreType.DMA((4,)),
         ],
-        input_output_aliases={1: 0, 2: 1, 4: 2},
+        input_output_aliases={2: 0, 3: 1, 5: 2},
         compiler_params=pltpu.CompilerParams(vmem_limit_bytes=VMEM_LIMIT),
         cost_estimate=LIGHT,
         name="attend",
-    )(route, out_k, out_v, early, late, level, total, *tokens)
+    )(lengths, route, out_k, out_v, early, late, level, total, *tokens)
 
 
 def place(n_seq, first, part, out_k, out_v, sem):
@@ -428,12 +467,9 @@
     )
 
 
-def merge_kernel(n_seq, count, relative, size, *refs):
+def merge_kernel(count, relative, size, *refs):
     stats, refs = refs[:count], refs[count:]
-    picked_ref, weight_hbm, log_ref, part, _, _, decay_ref, out_ref, out_k, out_v = refs[:10]
-    weight_ref, sem, sem_w = refs[10:]
-    (load,) = fetch([(weight_hbm, weight_ref)], sem_w)
-    placed = place(n_seq, 0, part, out_k, out_v, sem)
+    picked_ref, weight_ref, log_ref, decay_ref, out_ref = refs
     heads, req, rows = log_ref.shape
     width = picked_ref.shape[1]
     seq = lax.axis_index("seq")
@@ -464,38 +500,24 @@
     beyond = later(seq)
     for h in range(heads):
         decay_ref[h] = jnp.exp(log_ref[h] + beyond[:, h * size : h * size + 1])
-    load.wait()
     out_ref[...] = dot(attended.astype(jnp.bfloat16), weight_ref[...])
-    for copy in placed:
-        copy.wait()
-
-
-def merge_part(n_seq, stats, relative, picked, out_weight, logs, size, part, out_k, out_v):
+
+
+def merge_part(stats, relative, picked, out_weight, logs, size):
     req = logs.shape[1]
     vmem = pl.BlockSpec(memory_space=pltpu.VMEM)
-    hbm = pl.BlockSpec(memory_space=pl.ANY)
-    whole = jax.ShapeDtypeStruct(out_k.shape, out_k.dtype)
-    count = len(stats)
     return pl.pallas_call(
-        functools.partial(merge_kernel, n_seq, count, relative, size),
+        functools.partial(merge_kernel, len(stats), relative, size),
         out_shape=(
             jax.ShapeDtypeStruct(logs.shape, jnp.float32),
             jax.ShapeDtypeStruct((req, out_weight.shape[1]), jnp.float32),
-            whole,
-            whole,
         ),
-        in_specs=[vmem] * (count + 1) + [hbm] + [vmem] * 2 + [hbm] * 2,
-        out_specs=(vmem, vmem, hbm, hbm),
-        scratch_shapes=[
-            pltpu.VMEM(out_weight.shape, out_weight.dtype),
-            pltpu.SemaphoreType.DMA((2,)),
-            pltpu.SemaphoreType.DMA((1,)),
-        ],
-        input_output_aliases={count + 4: 2, count + 5: 3},
-        compiler_params=pltpu.CompilerParams(vmem_limit_bytes=VMEM_LIMIT),
+        in_specs=[vmem] * (len(stats) + 3),
+        out_specs=(vmem, vmem),
+        compiler_params=pltpu.CompilerParams(vmem_limit_bytes=SMALL_LIMIT),
         cost_estimate=MERGE,
         name="merge_and_project",
-    )(*stats, picked, out_weight, logs, part, out_k, out_v)
+    )(*stats, picked, out_weight, logs)
 
 
 def sum_kernel(count, *refs):
@@ -536,10 +558,61 @@
         out_specs=(hbm, hbm),
         scratch_shapes=[pltpu.SemaphoreType.DMA((2,))],
         input_output_aliases={1: 0, 2: 1},
-        compiler_params=pltpu.CompilerParams(vmem_limit_bytes=SMALL_LIMIT),
+        compiler_params=pltpu.CompilerParams(vmem_limit_bytes=VMEM_LIMIT),
         cost_estimate=LIGHT,
         name="place_received",
     )(part, out_k, out_v)
+
+
+def place_late_kernel(n_seq, first, part, len_hbm, old_k, old_v, out_k, out_v, lengths, sem_s, sem):
+    _, sent = half_of("seq", n_seq)
+    (load,) = fetch([(len_hbm, lengths)], sem_s)
+    load.wait()
+    req, rows, _ = out_k.shape
+    slots = rows // 2
+    most = slots // SLOTS
+    seq = lax.axis_index("seq")
+    if n_seq == 2:
+        start = (1 - seq) * (4 * slots) + seq * (2 * slots)
+    else:
+        start = seq * (4 * slots) + sent * (2 * slots)
+    ahead, _ = offsets(lengths, first, start, most)
+    for phase in ("start", "wait"):
+        for j, skip in enumerate(ahead):
+            live = live_blocks(lengths, first + j, start, most)
+            for blocks in range(1, most + 1):
+                size = blocks * SLOTS
+
+                @pl.when(live == blocks)
+                def _(j=j, skip=skip, size=size):
+                    for i, out in enumerate((out_k, out_v)):
+                        source = pl.ds(pl.multiple_of(skip * SLOTS, SLOTS), size)
+                        target = pl.ds(pl.multiple_of(sent * slots, SLOTS), size)
+                        copy = pltpu.make_async_copy(
+                            part.at[i, source, :], out.at[first + j, target, :], sem.at[i, j]
+                        )
+                        getattr(copy, phase)()
+
+
+def place_late_part(n_seq, first, part, lengths, out_k, out_v):
+    hbm = pl.BlockSpec(memory_space=pl.ANY)
+    vmem = pl.BlockSpec(memory_space=pltpu.VMEM)
+    shape = jax.ShapeDtypeStruct(out_k.shape, out_k.dtype)
+    return pl.pallas_call(
+        functools.partial(place_late_kernel, n_seq, first),
+        out_shape=(shape, shape),
+        in_specs=[vmem, hbm, hbm, hbm],
+        out_specs=(hbm, hbm),
+        scratch_shapes=[
+            pltpu.SMEM(lengths.shape, jnp.int32),
+            pltpu.SemaphoreType.DMA((1,)),
+            pltpu.SemaphoreType.DMA((2, lengths.shape[0] - first)),
+        ],
+        input_output_aliases={2: 0, 3: 1},
+        compiler_params=pltpu.CompilerParams(vmem_limit_bytes=VMEM_LIMIT),
+        cost_estimate=LIGHT,
+        name="place_live",
+    )(part, lengths, out_k, out_v)
 
 
 def others(value, axis):
@@ -561,7 +634,7 @@
     heads = log_forget.shape[1]
     size = width // heads
     n_seq, n_grp = lax.axis_size("seq"), lax.axis_size("grp")
-    early, packed = first_part(
+    early, packed, choice = first_part(
         n_seq,
         FIRST,
         lengths,
@@ -587,28 +660,31 @@
         packed,
     )
     out_k, out_v, late, stats, picked = attend_part(
-        n_seq, n_grp, heads, route, out_k, out_v, early, late, level, total, tokens
-    )
+        n_seq, n_grp, heads, lengths, route, out_k, out_v, early, late, level, total, tokens
+    )
+
+    def finish(rows, late, stats, picked, out_weight, logs, lengths, out_k, out_v):
+        if n_seq == 2:
+            all_stats = others(stats, "seq")
+        else:
+            gathered = lax.all_gather(stats, "seq")
+            all_stats = [gathered[i] for i in range(n_seq)]
+        received = exchange(late[:, :rows])
+        decay, partial = merge_part(all_stats, n_seq == 2, picked, out_weight, logs, size)
+        layer_out = sum_part(others(partial, "head"))
+        out_k, out_v = place_late_part(n_seq, FIRST, received, lengths, out_k, out_v)
+        return decay, layer_out, out_k, out_v
+
+    operands = (late, stats, picked, out_weight, logs, lengths, out_k, out_v)
     if n_seq == 2:
-        all_stats = others(stats, "seq")
+        step = STEP * SLOTS
+        branches = [
+            functools.partial(finish, rows) for rows in range(step, late.shape[1] + 1, step)
+        ]
+        decay, layer_out, out_k, out_v = lax.switch(choice[0], branches, *operands)
     else:
-        gathered = lax.all_gather(stats, "seq")
-        all_stats = [gathered[i] for i in range(n_seq)]
-    late_received = exchange(late)
-    decay, partial, out_k, out_v = merge_part(
-        n_seq,
-        all_stats,
-        n_seq == 2,
-        picked,
-        out_weight,
-        logs,
-        size,
-        first_received,
-        out_k,
-        out_v,
-    )
-    layer_out = sum_part(others(partial, "head"))
-    out_k, out_v = place_part(n_seq, FIRST, late_received, out_k, out_v)
+        decay, layer_out, out_k, out_v = finish(late.shape[1], *operands)
+    out_k, out_v = place_part(n_seq, 0, first_received, out_k, out_v)
     if n_seq != 2:
         out_k, out_v = (
             lax.all_to_all(x, "seq", split_axis=1, concat_axis=1, tiled=True) for x in (out_k, out_v)

time: 45.7 us -> 45 us (0.985)
  waiting for transfers between devices: 6.71 us -> 4.99 us
  Pallas kernels: 22.4 us -> 23.3 us
  between operations: 0.72 us -> 1.4 us
    unnamed x10, local copies, waits for them, and re-layouts: 1.94 us -> 0.6 us
    ppermute x2, waiting for transfers between devices: 1.16 us -> 0.01 us  [swap(): return lax.ppermute(value, 'seq', [(0, 1), (1, 0)]) if n_seq == 2 else value]
    pallas_call x1, Pallas kernels: 0.89 us -> 2.03 us  [place_part(): pl.pallas_call(functools.partial(place_kernel, n_seq, first), out_shape=(...]
    pallas_call x1 -> x2, Pallas kernels: 3.48 us -> 4.45 us  [the longest x1 2.49 us: place_late_part(): pl.pallas_call(functools.partial(place_late_kernel, n_seq, first), out_sh...]
    cond x0 -> x2, local copies, waits for them, and re-layouts: none -> 0.84 us
    pallas_call x1, Pallas kernels: 0.64 us -> 0.04 us  [sum_part(): pl.pallas_call(functools.partial(sum_kernel, len(parts)), out_shape=jax.S...]
    ppermute x7, waiting for transfers between devices: 5.55 us -> 4.99 us  [others(): lax.ppermute(value, axis, [(i, (i + k) % count) for i in range(count)])]
  transfers between devices with their start and end apart: 9 -> 9, of which waited for: 5 -> 4; matrix products, arithmetic and copies ran while one was open for 0% -> 0% of each run, Pallas kernels for 38% -> 38%
where the time goes in v4:
time: 45 us; the launch traced here: 44.9 us
  Pallas kernels  23.3 us (52%)
  starting transfers between devices  13.7 us (30%)
  waiting for transfers between devices  4.99 us (11%)
  local copies, waits for them, and re-layouts  1.51 us (3%)
  between operations  1.4 us (3%)
    pallas_call x1, Pallas kernels, own_part(): pl.pallas_call(functools.partial(own_kernel, n_seq, first), out_shape=(wh...  9.18 us
    ppermute x7, starting transfers between devices, others(): lax.ppermute(value, axis, [(i, (i + k) % count) for i in range(count)])  9.1 us
    ppermute x7, waiting for transfers between devices, others(): lax.ppermute(value, axis, [(i, (i + k) % count) for i in range(count)])  4.99 us
    ppermute x2, starting transfers between devices, swap(): return lax.ppermute(value, 'seq', [(0, 1), (1, 0)]) if n_seq == 2 else value  4.57 us
    pallas_call x1, Pallas kernels, first_part(): pl.pallas_call(functools.partial(first_kernel, n_seq), out_shape=(jax.Sha...  4.37 us
    pallas_call x1, Pallas kernels, attend_part(): pl.pallas_call(functools.partial(attend_kernel, n_seq, n_grp, heads, firs...  3.23 us
    pallas_call x1, Pallas kernels, place_late_part(): pl.pallas_call(functools.partial(place_late_kernel, n_seq, first), out_sh...  2.49 us
    pallas_call x1, Pallas kernels, place_part(): pl.pallas_call(functools.partial(place_kernel, n_seq, first), out_shape=(...  2.03 us
  transfers between devices with their start and end apart: 9, of which 4 were waited for; matrix products, arithmetic and copies ran while one was open for 0% of the time, Pallas kernels for 38%

profile of v4, /device:TPU:0, one launch (start us, length us, event | category | flops | bytes accessed | tf_op | source)
XLA Modules:
  0.0 44.9 jit_solution(4436161455831134311)
XLA Ops:
  0.6 0.0 copy-start.8
  0.6 4.4 %compact_first_sent.1 = (bf16[2,4,128,384]{3,2,1,0:T(8,128)(2,1)}, bf16[32,384]{1,0:T(8,128)(2,1)}, s32[1]{0:T(128)}) custom-call(s32[8]{0:T(128)} %refs_0_.1, s32[8,512]{1,0:T(8,128)} %keep_hbm.3, f32[8,512]{1,0:T(8,128)} %weight_hbm.3, bf16[24,384]{1,0:T(8,128)(2,1)} %bitcast.5, bf16[8,6]{1,0:T(8,128)(2,1)} %gate_hbm.1, bf16[8,512,384]{2,1,0:T(8,128)(2,1)} %keys.3, ...), custom_call_target="tpu_custom_call" | custom-call | flops 1 | bytes 1 | tf_op jit(solution)/shard_map/compact_first_sent/pallas_call | solution.py:171
  5.0 3.0 %collective-permute-start.40 = (bf16[2,4,128,384]{3,2,1,0:T(8,128)(2,1)}, bf16[2,4,128,384]{3,2,1,0:T(8,128)(2,1)}, u32[]{:S(2)}, u32[]{:S(2)}) collective-permute-start(bf16[2,4,128,384]{3,2,1,0:T(8,128)(2,1)} %get-tuple-element.248.refs_4_), channel_id=1, source_target_pairs={{0,4},{4,0},{1,5},{5,1},{2,6},{6,2},{3,7},{7,3},{8,12},{12,8},{9,1... | collective-permute-start | bytes 2359304 | tf_op jit(solution)/shard_map/ppermute | solution.py:627
  8.0 0.0 collective-permute-start.41
  8.0 1.6 %collective-permute-start.42 = (bf16[32,384]{1,0:T(8,128)(2,1)}, bf16[32,384]{1,0:T(8,128)(2,1)S(1)}, u32[]{:S(2)}, u32[]{:S(2)}) collective-permute-start(bf16[32,384]{1,0:T(8,128)(2,1)} %get-tuple-element.250.packed_hbm.refs_8_), channel_id=1, source_target_pairs={{0,16},{8,24},{16,0},{24,8},{1,17},{9,25},{17,1},{25,9},{2,18},{10... | collective-permute-start | bytes 73736 | tf_op jit(solution)/shard_map/ppermute | solution.py:621
  9.6 1.4 %collective-permute-start.43 = (bf16[32,384]{1,0:T(8,128)(2,1)}, bf16[32,384]{1,0:T(8,128)(2,1)S(1)}, u32[]{:S(2)}, u32[]{:S(2)}) collective-permute-start(bf16[32,384]{1,0:T(8,128)(2,1)} %get-tuple-element.250.packed_hbm.refs_8_), channel_id=1, source_target_pairs={{0,24},{8,0},{16,8},{24,16},{1,25},{9,1},{17,9},{25,17},{2,26},{10... | collective-permute-start | bytes 73736 | tf_op jit(solution)/shard_map/ppermute | solution.py:621
  11.0 0.0 copy-done.8
  11.0 9.2 %compact_own.1 = (bf16[8,256,384]{2,1,0:T(8,128)(2,1)}, bf16[8,256,384]{2,1,0:T(8,128)(2,1)}, bf16[2,512,384]{2,1,0:T(8,128)(2,1)S(1)}, f32[6,8,256]{2,1,0:T(8,1...) custom-call(s32[8]{0:T(128)S(1)} %copy-done.8, s32[8,512]{1,0:T(8,128)} %keep_hbm.3, f32[8,512]{1,0:T(8,128)} %weight_hbm.3, ...), custom_call_target="tpu_custom_call" | custom-call | flops 1 | bytes 1 | tf_op jit(solution)/shard_map/compact_own/pallas_call | solution.py:314
  20.8 0.0 collective-permute-done.41.refs_9_
  20.9 0.0 copy-start.9
  20.9 0.0 collective-permute-done.42.refs_10_
  20.9 0.0 copy-start.10
  20.9 0.0 collective-permute-done.43.refs_11_
  20.9 0.0 copy-start.11
  20.9 0.5 %copy-done.9 = bf16[32,384]{1,0:T(8,128)(2,1)} copy-done((bf16[32,384]{1,0:T(8,128)(2,1)}, bf16[32,384]{1,0:T(8,128)(2,1)S(1)}, u32[]{:S(2)}) %copy-start.9) | copy-done | bytes 24600
  21.5 0.0 copy-done.10
  21.5 0.0 copy-done.11
  21.5 3.2 %attend.1 = (bf16[8,256,384]{2,1,0:T(8,128)(2,1)}, bf16[8,256,384]{2,1,0:T(8,128)(2,1)}, bf16[2,512,384]{2,1,0:T(8,128)(2,1)S(1)}, f32[32,384]{1,0:T(8,128)S(1)}, f32[32,384]{1,0:T(8,128)}) custom-call(s32[8]{0:T(128)S(1)} %copy-done.8, s32[8]{0:T(128)} %refs_1_.1, ...), custom_call_target="tpu_custom_call", output_to_operand_aliasing={{0}: (2, {}), {1}: (3, {}), {2}: (5, {})} | custom-call | flops 1 | bytes 1 | tf_op jit(solution)/shard_map/attend/pallas_call | solution.py:433
  24.7 18.1 %conditional.1 = (f32[6,8,256]{2,1,0:T(8,128)}, bf16[8,768]{1,0:T(8,128)(2,1)S(1)}, bf16[8,256,384]{2,1,0:T(8,128)(2,1)}, bf16[8,256,384]{2,1,0:T(8,128)(2,1)}) conditional(s32[]{:T(128)} %bitcast.1, (f32[32,384]{1,0:T(8,128)S(1)}, f32[32,384]{1,0:T(8,128)}, bf16[384,768]{1,0:T(8,128)(2,1)}, ...), branch_computations={%region_0.0_spmd, %region_1.0_spmd, %region_2.0_spmd, %region_3.0_... | conditional | flops 68719476736 | bytes 7373063 | solution.py:684
  24.8 0.6 %collective-permute-start.30 = (f32[32,384]{1,0:T(8,128)S(1)}, f32[32,384]{1,0:T(8,128)S(1)}, u32[]{:S(2)}, u32[]{:S(2)}) collective-permute-start(f32[32,384]{1,0:T(8,128)S(1)} %get-tuple-element.200.refs_0_), channel_id=1, source_target_pairs={{0,4},{4,0},{1,5},{5,1},{2,6},{6,2},{3,7},{7,3},{8,12},{12,8},{9,1... | collective-permute-start | bytes 147464 | tf_op jit(solution)/shard_map/cond/branch_6_fun/ppermute | solution.py:621
  25.4 0.1 slice.20
  25.4 1.6 %collective-permute-start.34 = (bf16[2,448,384]{2,1,0:T(8,128)(2,1)S(1)}, bf16[2,448,384]{2,1,0:T(8,128)(2,1)S(1)}, u32[]{:S(2)}, u32[]{:S(2)}) collective-permute-start(bf16[2,448,384]{2,1,0:T(8,128)(2,1)S(1)} %slice.20), channel_id=1, source_target_pairs={{0,4},{4,0},{1,5},{5,1},{2,6},{6,2},{3,7},{7,3},{8,12},{12,8},{9,1... | collective-permute-start | bytes 2064392 | tf_op jit(solution)/shard_map/cond/branch_6_fun/ppermute | solution.py:627
  27.0 2.5 %collective-permute-done.30.refs_1_ = f32[32,384]{1,0:T(8,128)S(1)} collective-permute-done((f32[32,384]{1,0:T(8,128)S(1)}, f32[32,384]{1,0:T(8,128)S(1)}, u32[]{:S(2)}, u32[]{:S(2)}) %collective-permute-start.30) | collective-permute-done | bytes 49184 | tf_op jit(solution)/shard_map/cond/branch_6_fun/ppermute | solution.py:621
  29.5 2.0 %merge_and_project.14 = (f32[6,8,256]{2,1,0:T(8,128)}, f32[8,768]{1,0:T(8,128)S(1)}) custom-call(f32[32,384]{1,0:T(8,128)S(1)} %get-tuple-element.200.refs_0_, f32[32,384]{1,0:T(8,128)S(1)} %collective-permute-done.30.refs_1_, f32[32,384]{1,0:T(8,128)} %get-tuple-element.201.refs_2_, bf16[384,768]{1,0:T(8,128)(2,1)} %get-tuple-element.202.refs_3_, ...), custom_call_target="tpu_custom_call" | custom-call | flops 68719476736 | bytes 1 | tf_op jit(solution)/shard_map/cond/branch_6_fun/merge_and_project/pallas_call | solution.py:509
  31.5 1.6 %collective-permute-start.31 = (f32[8,768]{1,0:T(8,128)S(1)}, f32[8,768]{1,0:T(8,128)S(1)}, u32[]{:S(2)}, u32[]{:S(2)}) collective-permute-start(f32[8,768]{1,0:T(8,128)S(1)} %get-tuple-element.205.refs_0_), channel_id=1, source_target_pairs={{0,1},{1,2},{2,3},{3,0},{4,5},{5,6},{6,7},{7,4},{8,9},{9,10},{10,1... | collective-permute-start | bytes 73736 | tf_op jit(solution)/shard_map/cond/branch_6_fun/ppermute | solution.py:621
  33.1 2.6 %collective-permute-start.32 = (f32[8,768]{1,0:T(8,128)S(1)}, f32[8,768]{1,0:T(8,128)S(1)}, u32[]{:S(2)}, u32[]{:S(2)}) collective-permute-start(f32[8,768]{1,0:T(8,128)S(1)} %get-tuple-element.205.refs_0_), channel_id=1, source_target_pairs={{0,2},{1,3},{2,0},{3,1},{4,6},{5,7},{6,4},{7,5},{8,10},{9,11},{10,... | collective-permute-start | bytes 73736 | tf_op jit(solution)/shard_map/cond/branch_6_fun/ppermute | solution.py:621
  35.6 1.4 %collective-permute-start.33 = (f32[8,768]{1,0:T(8,128)S(1)}, f32[8,768]{1,0:T(8,128)S(1)}, u32[]{:S(2)}, u32[]{:S(2)}) collective-permute-start(f32[8,768]{1,0:T(8,128)S(1)} %get-tuple-element.205.refs_0_), channel_id=1, source_target_pairs={{0,3},{1,0},{2,1},{3,2},{4,7},{5,4},{6,5},{7,6},{8,11},{9,8},{10,9... | collective-permute-start | bytes 73736 | tf_op jit(solution)/shard_map/cond/branch_6_fun/ppermute | solution.py:621
  37.0 0.1 collective-permute-done.31.refs_1_
  37.1 0.7 %collective-permute-done.32.refs_2_ = f32[8,768]{1,0:T(8,128)S(1)} collective-permute-done((f32[8,768]{1,0:T(8,128)S(1)}, f32[8,768]{1,0:T(8,128)S(1)}, u32[]{:S(2)}, u32[]{:S(2)}) %collective-permute-start.32) | collective-permute-done | bytes 24608 | tf_op jit(solution)/shard_map/cond/branch_6_fun/ppermute | solution.py:621
  37.8 1.7 %collective-permute-done.33.refs_3_ = f32[8,768]{1,0:T(8,128)S(1)} collective-permute-done((f32[8,768]{1,0:T(8,128)S(1)}, f32[8,768]{1,0:T(8,128)S(1)}, u32[]{:S(2)}, u32[]{:S(2)}) %collective-permute-start.33) | collective-permute-done | bytes 24608 | tf_op jit(solution)/shard_map/cond/branch_6_fun/ppermute | solution.py:621
  39.5 0.0 collective-permute-done.34.part
  39.5 0.0 copy-start.1
  39.5 0.8 %copy-done.1 = bf16[2,448,384]{2,1,0:T(8,128)(2,1)} copy-done((bf16[2,448,384]{2,1,0:T(8,128)(2,1)}, bf16[2,448,384]{2,1,0:T(8,128)(2,1)S(1)}, u32[]{:S(2)}) %copy-start.1) | copy-done | bytes 688152 | tf_op jit(solution)/shard_map/cond
  40.4 2.5 %place_live.14 = (bf16[8,256,384]{2,1,0:T(8,128)(2,1)}, bf16[8,256,384]{2,1,0:T(8,128)(2,1)}) custom-call(bf16[2,448,384]{2,1,0:T(8,128)(2,1)} %copy-done.1, s32[8]{0:T(128)S(1)} %get-tuple-element.207.len_hbm, bf16[8,256,384]{2,1,0:T(8,128)(2,1)} %get-tuple-element.208.old_k, ...), custom_call_target="tpu_custom_call", output_to_operand_aliasing={{0}: (2, {}), {1}: (3, {})} | custom-call | flops 1 | bytes 1 | tf_op jit(solution)/shard_map/cond/branch_6_fun/place_live/pallas_call | solution.py:601
  42.9 0.0 copy-start.12
  42.9 0.0 collective-permute-done.40.part
  42.9 2.0 %place_received.1 = (bf16[8,256,384]{2,1,0:T(8,128)(2,1)}, bf16[8,256,384]{2,1,0:T(8,128)(2,1)}) custom-call(bf16[2,4,128,384]{3,2,1,0:T(8,128)(2,1)} %collective-permute-done.40.part, bf16[8,256,384]{2,1,0:T(8,128)(2,1)} %get-tuple-element.262.old_k, bf16[8,256,384]{2,1,0:T(8,128)(2,1)} %get-tuple-element.263.old_v), custom_call_target="tpu_custom_call", output_to_operand_aliasing={{0}: (1, {}), {1}: (2, {})} | custom-call | flops 1 | bytes 1 | tf_op jit(solution)/shard_map/place_received/pallas_call | solution.py:554
  44.9 0.0 copy-done.12
  (1 shorter events, 0.0 us)
Async XLA Ops:
  0.6 10.4 %copy-start.8 = (s32[8]{0:T(128)S(1)}, s32[8]{0:T(128)}, u32[]{:S(2)}) copy-start(s32[8]{0:T(128)} %refs_0_.1) | copy-start | bytes 100
  5.0 37.9 %collective-permute-start.40 = (bf16[2,4,128,384]{3,2,1,0:T(8,128)(2,1)}, bf16[2,4,128,384]{3,2,1,0:T(8,128)(2,1)}, u32[]{:S(2)}, u32[]{:S(2)}) collective-permute-start(bf16[2,4,128,384]{3,2,1,0:T(8,128)(2,1)} %get-tuple-element.248.refs_4_), channel_id=1, source_target_pairs={{0,4},{4,0},{1,5},{5,1},{2,6},{6,2},{3,7},{7,3},{8,12},{12,8},{9,1... | collective-permute-start | bytes 2359304 | tf_op jit(solution)/shard_map/ppermute | solution.py:627
  8.0 12.8 %collective-permute-start.41 = (bf16[32,384]{1,0:T(8,128)(2,1)}, bf16[32,384]{1,0:T(8,128)(2,1)S(1)}, u32[]{:S(2)}, u32[]{:S(2)}) collective-permute-start(bf16[32,384]{1,0:T(8,128)(2,1)} %get-tuple-element.250.packed_hbm.refs_8_), channel_id=1, source_target_pairs={{0,8},{8,16},{16,24},{24,0},{1,9},{9,17},{17,25},{25,1},{2,10},{10... | collective-permute-start | bytes 73736 | tf_op jit(solution)/shard_map/ppermute | solution.py:621
  8.0 12.9 %collective-permute-start.42 = (bf16[32,384]{1,0:T(8,128)(2,1)}, bf16[32,384]{1,0:T(8,128)(2,1)S(1)}, u32[]{:S(2)}, u32[]{:S(2)}) collective-permute-start(bf16[32,384]{1,0:T(8,128)(2,1)} %get-tuple-element.250.packed_hbm.refs_8_), channel_id=1, source_target_pairs={{0,16},{8,24},{16,0},{24,8},{1,17},{9,25},{17,1},{25,9},{2,18},{10... | collective-permute-start | bytes 73736 | tf_op jit(solution)/shard_map/ppermute | solution.py:621
  9.6 11.3 %collective-permute-start.43 = (bf16[32,384]{1,0:T(8,128)(2,1)}, bf16[32,384]{1,0:T(8,128)(2,1)S(1)}, u32[]{:S(2)}, u32[]{:S(2)}) collective-permute-start(bf16[32,384]{1,0:T(8,128)(2,1)} %get-tuple-element.250.packed_hbm.refs_8_), channel_id=1, source_target_pairs={{0,24},{8,0},{16,8},{24,16},{1,25},{9,1},{17,9},{25,17},{2,26},{10... | collective-permute-start | bytes 73736 | tf_op jit(solution)/shard_map/ppermute | solution.py:621
  20.9 0.6 %copy-start.9 = (bf16[32,384]{1,0:T(8,128)(2,1)}, bf16[32,384]{1,0:T(8,128)(2,1)S(1)}, u32[]{:S(2)}) copy-start(bf16[32,384]{1,0:T(8,128)(2,1)S(1)} %collective-permute-done.41.refs_9_) | copy-start | bytes 73732
  20.9 0.6 %copy-start.10 = (bf16[32,384]{1,0:T(8,128)(2,1)}, bf16[32,384]{1,0:T(8,128)(2,1)S(1)}, u32[]{:S(2)}) copy-start(bf16[32,384]{1,0:T(8,128)(2,1)S(1)} %collective-permute-done.42.refs_10_) | copy-start | bytes 73732
  20.9 0.6 %copy-start.11 = (bf16[32,384]{1,0:T(8,128)(2,1)}, bf16[32,384]{1,0:T(8,128)(2,1)S(1)}, u32[]{:S(2)}) copy-start(bf16[32,384]{1,0:T(8,128)(2,1)S(1)} %collective-permute-done.43.refs_11_) | copy-start | bytes 73732
  24.8 4.7 %collective-permute-start.30 = (f32[32,384]{1,0:T(8,128)S(1)}, f32[32,384]{1,0:T(8,128)S(1)}, u32[]{:S(2)}, u32[]{:S(2)}) collective-permute-start(f32[32,384]{1,0:T(8,128)S(1)} %get-tuple-element.200.refs_0_), channel_id=1, source_target_pairs={{0,4},{4,0},{1,5},{5,1},{2,6},{6,2},{3,7},{7,3},{8,12},{12,8},{9,1... | collective-permute-start | bytes 147464 | tf_op jit(solution)/shard_map/cond/branch_6_fun/ppermute | solution.py:621
  25.4 14.1 %collective-permute-start.34 = (bf16[2,448,384]{2,1,0:T(8,128)(2,1)S(1)}, bf16[2,448,384]{2,1,0:T(8,128)(2,1)S(1)}, u32[]{:S(2)}, u32[]{:S(2)}) collective-permute-start(bf16[2,448,384]{2,1,0:T(8,128)(2,1)S(1)} %slice.20), channel_id=1, source_target_pairs={{0,4},{4,0},{1,5},{5,1},{2,6},{6,2},{3,7},{7,3},{8,12},{12,8},{9,1... | collective-permute-start | bytes 2064392 | tf_op jit(solution)/shard_map/cond/branch_6_fun/ppermute | solution.py:627
  31.5 5.6 %collective-permute-start.31 = (f32[8,768]{1,0:T(8,128)S(1)}, f32[8,768]{1,0:T(8,128)S(1)}, u32[]{:S(2)}, u32[]{:S(2)}) collective-permute-start(f32[8,768]{1,0:T(8,128)S(1)} %get-tuple-element.205.refs_0_), channel_id=1, source_target_pairs={{0,1},{1,2},{2,3},{3,0},{4,5},{5,6},{6,7},{7,4},{8,9},{9,10},{10,1... | collective-permute-start | bytes 73736 | tf_op jit(solution)/shard_map/cond/branch_6_fun/ppermute | solution.py:621
  33.1 4.7 %collective-permute-start.32 = (f32[8,768]{1,0:T(8,128)S(1)}, f32[8,768]{1,0:T(8,128)S(1)}, u32[]{:S(2)}, u32[]{:S(2)}) collective-permute-start(f32[8,768]{1,0:T(8,128)S(1)} %get-tuple-element.205.refs_0_), channel_id=1, source_target_pairs={{0,2},{1,3},{2,0},{3,1},{4,6},{5,7},{6,4},{7,5},{8,10},{9,11},{10,... | collective-permute-start | bytes 73736 | tf_op jit(solution)/shard_map/cond/branch_6_fun/ppermute | solution.py:621
  35.6 3.8 %collective-permute-start.33 = (f32[8,768]{1,0:T(8,128)S(1)}, f32[8,768]{1,0:T(8,128)S(1)}, u32[]{:S(2)}, u32[]{:S(2)}) collective-permute-start(f32[8,768]{1,0:T(8,128)S(1)} %get-tuple-element.205.refs_0_), channel_id=1, source_target_pairs={{0,3},{1,0},{2,1},{3,2},{4,7},{5,4},{6,5},{7,6},{8,11},{9,8},{10,9... | collective-permute-start | bytes 73736 | tf_op jit(solution)/shard_map/cond/branch_6_fun/ppermute | solution.py:621
  39.5 0.8 %copy-start.1 = (bf16[2,448,384]{2,1,0:T(8,128)(2,1)}, bf16[2,448,384]{2,1,0:T(8,128)(2,1)S(1)}, u32[]{:S(2)}) copy-start(bf16[2,448,384]{2,1,0:T(8,128)(2,1)S(1)} %collective-permute-done.34.part) | copy-start | bytes 2064388 | tf_op jit(solution)/shard_map/cond
  42.9 2.1 %copy-start.12 = (bf16[8,768]{1,0:T(8,128)(2,1)}, bf16[8,768]{1,0:T(8,128)(2,1)S(1)}, u32[]{:S(2)}) copy-start(bf16[8,768]{1,0:T(8,128)(2,1)S(1)} %get-tuple-element.247) | copy-start | bytes 36868

commit v5 on v4

--- a/solution.py
+++ b/solution.py
@@ -16,6 +16,7 @@
 FIRST = 4
 STEP = 2
 VMEM_LIMIT = 63 * 1024 * 1024
+LAST_LIMIT = 60 * 1024 * 1024
 SMALL_LIMIT = 8 * 1024 * 1024
 
 
@@ -521,7 +522,7 @@
 
 
 def sum_kernel(count, *refs):
-    parts, out = refs[:count], refs[count]
+    parts, out = refs[:count], refs[-1]
     me = lax.axis_index("head")
     total = jnp.zeros(out.shape, jnp.float32)
     for place in range(count):
@@ -530,20 +531,22 @@
     out[...] = total.astype(out.dtype)
 
 
-def sum_part(parts):
+def sum_part(parts, placed):
     return pl.pallas_call(
         functools.partial(sum_kernel, len(parts)),
         out_shape=jax.ShapeDtypeStruct(parts[0].shape, jnp.bfloat16),
-        in_specs=[pl.BlockSpec(memory_space=pltpu.VMEM)] * len(parts),
+        in_specs=[pl.BlockSpec(memory_space=pltpu.VMEM)] * (len(parts) + 1),
         out_specs=pl.BlockSpec(memory_space=pltpu.VMEM),
         compiler_params=pltpu.CompilerParams(vmem_limit_bytes=SMALL_LIMIT),
         cost_estimate=LIGHT,
         name="sum_heads",
-    )(*parts)
-
-
-def place_kernel(n_seq, first, part, old_k, old_v, out_k, out_v, sem):
-    for copy in place(n_seq, first, part, out_k, out_v, sem):
+    )(*parts, placed)
+
+
+def place_kernel(n_seq, first, part, old_k, old_v, out_k, out_v, placed_ref, sem):
+    copies = place(n_seq, first, part, out_k, out_v, sem)
+    placed_ref[...] = jnp.zeros_like(placed_ref)
+    for copy in copies:
         copy.wait()
 
 
@@ -553,12 +556,12 @@
     shape = jax.ShapeDtypeStruct(out_k.shape, out_k.dtype)
     return pl.pallas_call(
         functools.partial(place_kernel, n_seq, first),
-        out_shape=(shape, shape),
+        out_shape=(shape, shape, jax.ShapeDtypeStruct((8, LANES), jnp.float32)),
         in_specs=[vmem, hbm, hbm],
-        out_specs=(hbm, hbm),
+        out_specs=(hbm, hbm, vmem),
         scratch_shapes=[pltpu.SemaphoreType.DMA((2,))],
         input_output_aliases={1: 0, 2: 1},
-        compiler_params=pltpu.CompilerParams(vmem_limit_bytes=VMEM_LIMIT),
+        compiler_params=pltpu.CompilerParams(vmem_limit_bytes=LAST_LIMIT),
         cost_estimate=LIGHT,
         name="place_received",
     )(part, out_k, out_v)
@@ -609,7 +612,7 @@
             pltpu.SemaphoreType.DMA((2, lengths.shape[0] - first)),
         ],
         input_output_aliases={2: 0, 3: 1},
-        compiler_params=pltpu.CompilerParams(vmem_limit_bytes=VMEM_LIMIT),
+        compiler_params=pltpu.CompilerParams(vmem_limit_bytes=LAST_LIMIT),
         cost_estimate=LIGHT,
         name="place_live",
     )(part, lengths, out_k, out_v)
@@ -663,7 +666,7 @@
         n_seq, n_grp, heads, lengths, route, out_k, out_v, early, late, level, total, tokens
     )
 
-    def finish(rows, late, stats, picked, out_weight, logs, lengths, out_k, out_v):
+    def finish(rows, early, late, stats, picked, out_weight, logs, lengths, out_k, out_v):
         if n_seq == 2:
             all_stats = others(stats, "seq")
         else:
@@ -671,11 +674,12 @@
             all_stats = [gathered[i] for i in range(n_seq)]
         received = exchange(late[:, :rows])
         decay, partial = merge_part(all_stats, n_seq == 2, picked, out_weight, logs, size)
-        layer_out = sum_part(others(partial, "head"))
+        out_k, out_v, placed = place_part(n_seq, 0, early, out_k, out_v)
+        layer_out = sum_part(others(partial, "head"), placed)
         out_k, out_v = place_late_part(n_seq, FIRST, received, lengths, out_k, out_v)
         return decay, layer_out, out_k, out_v
 
-    operands = (late, stats, picked, out_weight, logs, lengths, out_k, out_v)
+    operands = (first_received, late, stats, picked, out_weight, logs, lengths, out_k, out_v)
     if n_seq == 2:
         step = STEP * SLOTS
         branches = [
@@ -684,7 +688,6 @@
         decay, layer_out, out_k, out_v = lax.switch(choice[0], branches, *operands)
     else:
         decay, layer_out, out_k, out_v = finish(late.shape[1], *operands)
-    out_k, out_v = place_part(n_seq, 0, first_received, out_k, out_v)
     if n_seq != 2:
         out_k, out_v = (
             lax.all_to_all(x, "seq", split_axis=1, concat_axis=1, tiled=True) for x in (out_k, out_v)

time: 45 us -> 47 us (1.044); the launches traced: 44.9 us -> 46.2 us
  local copies, waits for them, and re-layouts: 1.51 us -> 5.48 us
  waiting for transfers between devices: 4.99 us -> 2.25 us
    ppermute x7, waiting for transfers between devices: 4.99 us -> 2.06 us  [others(): lax.ppermute(value, axis, [(i, (i + k) % count) for i in range(count)])]
    slice x1, local copies, waits for them, and re-layouts: 0.07 us -> 1.94 us  [finish(): received = exchange(late[:, :rows])]
    cond x2 -> x12, local copies, waits for them, and re-layouts: 0.84 us -> 2.34 us
    pallas_call x1, Pallas kernels: 2.03 us -> 0.74 us  [place_part(): pl.pallas_call(functools.partial(place_kernel, n_seq, first), out_shape=(...]
    ppermute x2, starting transfers between devices: 4.57 us -> 3.6 us  [swap(): return lax.ppermute(value, 'seq', [(0, 1), (1, 0)]) if n_seq == 2 else value]
    ppermute x7, starting transfers between devices: 9.1 us -> 9.98 us  [others(): lax.ppermute(value, axis, [(i, (i + k) % count) for i in range(count)])]
    pallas_call x1, Pallas kernels: 9.18 us -> 10 us  [own_part(): pl.pallas_call(functools.partial(own_kernel, n_seq, first), out_shape=(wh...]
    unnamed x10 -> x8, local copies, waits for them, and re-layouts: 0.6 us -> 1.2 us
  transfers between devices with their start and end apart: 9 -> 9, of which waited for: 4 -> 3; matrix products, arithmetic and copies ran while one was open for 0% -> 4% of each run, Pallas kernels for 38% -> 36%
where the time goes in v5:
time: 47 us; the launch traced here: 46.2 us
  Pallas kernels  23.4 us (50%)
  starting transfers between devices  13.6 us (29%)
  local copies, waits for them, and re-layouts  5.48 us (12%)
  waiting for transfers between devices  2.25 us (5%)
  between operations  1.36 us (3%)
    pallas_call x1, Pallas kernels, own_part(): pl.pallas_call(functools.partial(own_kernel, n_seq, first), out_shape=(wh...  10 us
    ppermute x7, starting transfers between devices, others(): lax.ppermute(value, axis, [(i, (i + k) % count) for i in range(count)])  9.98 us
    pallas_call x1, Pallas kernels, first_part(): pl.pallas_call(functools.partial(first_kernel, n_seq), out_shape=(jax.Sha...  4.38 us
    pallas_call x1, Pallas kernels, attend_part(): pl.pallas_call(functools.partial(attend_kernel, n_seq, n_grp, heads, firs...  3.62 us
    ppermute x2, starting transfers between devices, swap(): return lax.ppermute(value, 'seq', [(0, 1), (1, 0)]) if n_seq == 2 else value  3.6 us
    pallas_call x1, Pallas kernels, place_late_part(): pl.pallas_call(functools.partial(place_late_kernel, n_seq, first), out_sh...  2.49 us
    cond x12, local copies, waits for them, and re-layouts  2.34 us
    pallas_call x1, Pallas kernels, merge_part(): pl.pallas_call(functools.partial(merge_kernel, len(stats), relative, size...  2.13 us
  transfers between devices with their start and end apart: 9, of which 3 were waited for; matrix products, arithmetic and copies ran while one was open for 4% of the time, Pallas kernels for 36%

profile of v5, /device:TPU:0, one launch (start us, length us, event | category | flops | bytes accessed | tf_op | source)
XLA Modules:
  0.0 46.2 jit_solution(10145078401393129731)
XLA Ops:
  0.6 4.4 %compact_first_sent.1 = (bf16[2,4,128,384]{3,2,1,0:T(8,128)(2,1)}, bf16[32,384]{1,0:T(8,128)(2,1)}, s32[1]{0:T(128)}) custom-call(s32[8]{0:T(128)} %refs_0_.1, s32[8,512]{1,0:T(8,128)} %keep_hbm.3, f32[8,512]{1,0:T(8,128)} %weight_hbm.3, bf16[24,384]{1,0:T(8,128)(2,1)} %bitcast.5, bf16[8,6]{1,0:T(8,128)(2,1)} %gate_hbm.1, bf16[8,512,384]{2,1,0:T(8,128)(2,1)} %keys.3, ...), custom_call_target="tpu_custom_call" | custom-call | flops 1 | bytes 1 | tf_op jit(solution)/shard_map/compact_first_sent/pallas_call | solution.py:172
  5.0 3.0 %collective-permute-start.43 = (bf16[2,4,128,384]{3,2,1,0:T(8,128)(2,1)}, bf16[2,4,128,384]{3,2,1,0:T(8,128)(2,1)S(1)}, u32[]{:S(2)}, u32[]{:S(2)}) collective-permute-start(bf16[2,4,128,384]{3,2,1,0:T(8,128)(2,1)} %get-tuple-element.298.refs_4_), channel_id=1, source_target_pairs={{0,4},{4,0},{1,5},{5,1},{2,6},{6,2},{3,7},{7,3},{8,12},{12,8},{9,1... | collective-permute-start | bytes 2359304 | tf_op jit(solution)/shard_map/ppermute | solution.py:630
  8.0 0.0 collective-permute-start.40
  8.0 1.6 %collective-permute-start.41 = (bf16[32,384]{1,0:T(8,128)(2,1)}, bf16[32,384]{1,0:T(8,128)(2,1)S(1)}, u32[]{:S(2)}, u32[]{:S(2)}) collective-permute-start(bf16[32,384]{1,0:T(8,128)(2,1)} %get-tuple-element.295.packed_hbm.refs_8_), channel_id=1, source_target_pairs={{0,16},{8,24},{16,0},{24,8},{1,17},{9,25},{17,1},{25,9},{2,18},{10... | collective-permute-start | bytes 73736 | tf_op jit(solution)/shard_map/ppermute | solution.py:624
  9.6 1.4 %collective-permute-start.42 = (bf16[32,384]{1,0:T(8,128)(2,1)}, bf16[32,384]{1,0:T(8,128)(2,1)S(1)}, u32[]{:S(2)}, u32[]{:S(2)}) collective-permute-start(bf16[32,384]{1,0:T(8,128)(2,1)} %get-tuple-element.295.packed_hbm.refs_8_), channel_id=1, source_target_pairs={{0,24},{8,0},{16,8},{24,16},{1,25},{9,1},{17,9},{25,17},{2,26},{10... | collective-permute-start | bytes 73736 | tf_op jit(solution)/shard_map/ppermute | solution.py:624
  11.0 10.0 %compact_own.1 = (bf16[8,256,384]{2,1,0:T(8,128)(2,1)}, bf16[8,256,384]{2,1,0:T(8,128)(2,1)}, bf16[2,512,384]{2,1,0:T(8,128)(2,1)}, f32[6,8,256]{2,1,0:T(8,128)}...) custom-call(s32[8]{0:T(128)} %refs_0_.1, s32[8,512]{1,0:T(8,128)} %keep_hbm.3, f32[8,512]{1,0:T(8,128)} %weight_hbm.3, ...), custom_call_target="tpu_custom_call" | custom-call | flops 1 | bytes 1 | tf_op jit(solution)/shard_map/compact_own/pallas_call | solution.py:315
  21.7 0.0 collective-permute-done.40.refs_9_
  21.7 0.0 copy-start.48
  21.7 0.0 collective-permute-done.41.refs_10_
  21.7 0.0 copy-start.49
  21.7 0.0 collective-permute-done.42.refs_11_
  21.7 0.0 copy-start.50
  21.7 0.6 %copy-done.48 = bf16[32,384]{1,0:T(8,128)(2,1)} copy-done((bf16[32,384]{1,0:T(8,128)(2,1)}, bf16[32,384]{1,0:T(8,128)(2,1)S(1)}, u32[]{:S(2)}) %copy-start.48) | copy-done | bytes 24600
  22.3 0.0 copy-done.49
  22.3 0.0 copy-done.50
  22.3 3.6 %attend.1 = (bf16[8,256,384]{2,1,0:T(8,128)(2,1)}, bf16[8,256,384]{2,1,0:T(8,128)(2,1)}, bf16[2,512,384]{2,1,0:T(8,128)(2,1)}, f32[32,384]{1,0:T(8,128)}, f32[32,384]{1,0:T(8,128)}) custom-call(s32[8]{0:T(128)} %refs_0_.1, s32[8]{0:T(128)} %refs_1_.1, ...), custom_call_target="tpu_custom_call", output_to_operand_aliasing={{0}: (2, {}), {1}: (3, {}), {2}: (5, {})} | custom-call | flops 1 | bytes 1 | tf_op jit(solution)/shard_map/attend/pallas_call | solution.py:434
  26.0 0.0 collective-permute-done.43
  26.0 19.6 %conditional.1 = (f32[6,8,256]{2,1,0:T(8,128)}, bf16[8,768]{1,0:T(8,128)(2,1)S(1)}, bf16[8,256,384]{2,1,0:T(8,128)(2,1)}, bf16[8,256,384]{2,1,0:T(8,128)(2,1)}) conditional(s32[]{:T(128)} %bitcast.1, (f32[32,384]{1,0:T(8,128)}, f32[32,384]{1,0:T(8,128)}, bf16[384,768]{1,0:T(8,128)(2,1)}, f32[6,8,256]{2,1,0:T(8,128)}, ...), branch_computations={%region_0.0_spmd, %region_1.0_spmd, %region_2.0_spmd, %region_3.0_... | conditional | flops 68719476736 | bytes 29803028 | solution.py:688
  26.0 1.5 %collective-permute-start.25 = (f32[32,384]{1,0:T(8,128)}, f32[32,384]{1,0:T(8,128)S(1)}, u32[]{:S(2)}, u32[]{:S(2)}) collective-permute-start(f32[32,384]{1,0:T(8,128)} %get-tuple-element.224.refs_0_), channel_id=1, source_target_pairs={{0,4},{4,0},{1,5},{5,1},{2,6},{6,2},{3,7},{7,3},{8,12},{12,8},{9,1... | collective-permute-start | bytes 147464 | tf_op jit(solution)/shard_map/cond/branch_5_fun/ppermute | solution.py:624
  27.5 1.9 %slice.19 = bf16[2,384,384]{2,1,0:T(8,128)(2,1)} slice(bf16[2,512,384]{2,1,0:T(8,128)(2,1)} %get-tuple-element.234), slice={[0:2], [0:384], [0:384]} | slice | bytes 1179648 | tf_op jit(solution)/shard_map/cond/branch_5_fun/slice | solution.py:675
  29.5 0.6 %collective-permute-start.29 = (bf16[2,384,384]{2,1,0:T(8,128)(2,1)}, bf16[2,384,384]{2,1,0:T(8,128)(2,1)}, u32[]{:S(2)}, u32[]{:S(2)}) collective-permute-start(bf16[2,384,384]{2,1,0:T(8,128)(2,1)} %slice.19), channel_id=1, source_target_pairs={{0,4},{4,0},{1,5},{5,1},{2,6},{6,2},{3,7},{7,3},{8,12},{12,8},{9,1... | collective-permute-start | bytes 1769480 | tf_op jit(solution)/shard_map/cond/branch_5_fun/ppermute | solution.py:630
  30.1 0.3 collective-permute-done.25.refs_1_
  30.4 0.0 copy-start.13
  30.4 0.0 copy-start.29
  30.4 2.1 %merge_and_project.13 = (f32[6,8,256]{2,1,0:T(8,128)}, f32[8,768]{1,0:T(8,128)S(1)}) custom-call(f32[32,384]{1,0:T(8,128)} %get-tuple-element.224.refs_0_, f32[32,384]{1,0:T(8,128)S(1)} %collective-permute-done.25.refs_1_, f32[32,384]{1,0:T(8,128)} %get-tuple-element.225.refs_2_, bf16[384,768]{1,0:T(8,128)(2,1)} %get-tuple-element.226.refs_3_, ...), custom_call_target="tpu_custom_call" | custom-call | flops 68719476736 | bytes 1 | tf_op jit(solution)/shard_map/cond/branch_5_fun/merge_and_project/pallas_call | solution.py:510
  32.5 1.6 %collective-permute-start.26 = (f32[8,768]{1,0:T(8,128)S(1)}, f32[8,768]{1,0:T(8,128)S(1)}, u32[]{:S(2)}, u32[]{:S(2)}) collective-permute-start(f32[8,768]{1,0:T(8,128)S(1)} %get-tuple-element.229.refs_0_), channel_id=1, source_target_pairs={{0,1},{1,2},{2,3},{3,0},{4,5},{5,6},{6,7},{7,4},{8,9},{9,10},{10,1... | collective-permute-start | bytes 73736 | tf_op jit(solution)/shard_map/cond/branch_5_fun/ppermute | solution.py:624
  34.1 2.6 %collective-permute-start.27 = (f32[8,768]{1,0:T(8,128)S(1)}, f32[8,768]{1,0:T(8,128)S(1)}, u32[]{:S(2)}, u32[]{:S(2)}) collective-permute-start(f32[8,768]{1,0:T(8,128)S(1)} %get-tuple-element.229.refs_0_), channel_id=1, source_target_pairs={{0,2},{1,3},{2,0},{3,1},{4,6},{5,7},{6,4},{7,5},{8,10},{9,11},{10,... | collective-permute-start | bytes 73736 | tf_op jit(solution)/shard_map/cond/branch_5_fun/ppermute | solution.py:624
  36.7 1.3 %collective-permute-start.28 = (f32[8,768]{1,0:T(8,128)S(1)}, f32[8,768]{1,0:T(8,128)S(1)}, u32[]{:S(2)}, u32[]{:S(2)}) collective-permute-start(f32[8,768]{1,0:T(8,128)S(1)} %get-tuple-element.229.refs_0_), channel_id=1, source_target_pairs={{0,3},{1,0},{2,1},{3,2},{4,7},{5,4},{6,5},{7,6},{8,11},{9,8},{10,9... | collective-permute-start | bytes 73736 | tf_op jit(solution)/shard_map/cond/branch_5_fun/ppermute | solution.py:624
  38.0 0.0 copy-done.13
  38.0 0.0 copy-done.29
  38.0 0.0 copy-start.45
  38.0 0.7 %place_received.13 = (bf16[8,256,384]{2,1,0:T(8,128)(2,1)S(1)}, bf16[8,256,384]{2,1,0:T(8,128)(2,1)S(1)}, f32[8,128]{1,0:T(8,128)}) custom-call(bf16[2,4,128,384]{3,2,1,0:T(8,128)(2,1)S(1)} %get-tuple-element.230.part, bf16[8,256,384]{2,1,0:T(8,128)(2,1)S(1)} %copy-done.13, ...), custom_call_target="tpu_custom_call", output_to_operand_aliasing={{0}: (1, {}), {1}: (2, {})} | custom-call | flops 1 | bytes 1 | tf_op jit(solution)/shard_map/cond/branch_5_fun/place_received/pallas_call | solution.py:557
  38.8 0.0 collective-permute-done.26.refs_1_
  38.8 0.0 collective-permute-done.27.refs_2_
  38.8 1.7 %collective-permute-done.28.refs_3_ = f32[8,768]{1,0:T(8,128)S(1)} collective-permute-done((f32[8,768]{1,0:T(8,128)S(1)}, f32[8,768]{1,0:T(8,128)S(1)}, u32[]{:S(2)}, u32[]{:S(2)}) %collective-permute-start.28) | collective-permute-done | bytes 24608 | tf_op jit(solution)/shard_map/cond/branch_5_fun/ppermute | solution.py:624
  40.5 0.0 copy-start.5
  40.5 0.7 %copy-done.5 = f32[8,128]{1,0:T(8,128)S(1)} copy-done((f32[8,128]{1,0:T(8,128)S(1)}, f32[8,128]{1,0:T(8,128)}, u32[]{:S(2)}) %copy-start.5) | copy-done | bytes 4120 | tf_op jit(solution)/shard_map/cond
  41.2 0.2 collective-permute-done.29.part
  41.4 0.0 copy-done.45
  41.4 2.5 %place_live.13 = (bf16[8,256,384]{2,1,0:T(8,128)(2,1)S(1)}, bf16[8,256,384]{2,1,0:T(8,128)(2,1)S(1)}) custom-call(bf16[2,384,384]{2,1,0:T(8,128)(2,1)} %collective-permute-done.29.part, s32[8]{0:T(128)S(1)} %copy-done.45, bf16[8,256,384]{2,1,0:T(8,128)(2,1)S(1)} %get-tuple-element.236.old_k, ...), custom_call_target="tpu_custom_call", output_to_operand_aliasing={{0}: (2, {}), {1}: (3, {})} | custom-call | flops 1 | bytes 1 | tf_op jit(solution)/shard_map/cond/branch_5_fun/place_live/pallas_call | solution.py:604
  43.9 0.0 copy-start.21
  43.9 0.0 copy-start.37
  43.9 1.1 %copy-done.21 = bf16[8,256,384]{2,1,0:T(8,128)(2,1)} copy-done((bf16[8,256,384]{2,1,0:T(8,128)(2,1)}, bf16[8,256,384]{2,1,0:T(8,128)(2,1)S(1)}, u32[]{:S(2)}) %copy-start.21) | copy-done | bytes 1572888 | tf_op jit(solution)/shard_map/cond
  45.1 0.5 %copy-done.37 = bf16[8,256,384]{2,1,0:T(8,128)(2,1)} copy-done((bf16[8,256,384]{2,1,0:T(8,128)(2,1)}, bf16[8,256,384]{2,1,0:T(8,128)(2,1)S(1)}, u32[]{:S(2)}) %copy-start.37) | copy-done | bytes 1572888 | tf_op jit(solution)/shard_map/cond
  45.6 0.0 copy-start.51
  45.6 0.6 %copy-done.51 = bf16[8,768]{1,0:T(8,128)(2,1)} copy-done((bf16[8,768]{1,0:T(8,128)(2,1)}, bf16[8,768]{1,0:T(8,128)(2,1)S(1)}, u32[]{:S(2)}) %copy-start.51) | copy-done | bytes 12312
  (1 shorter events, 0.0 us)
Async XLA Ops:
  5.0 21.0 %collective-permute-start.43 = (bf16[2,4,128,384]{3,2,1,0:T(8,128)(2,1)}, bf16[2,4,128,384]{3,2,1,0:T(8,128)(2,1)S(1)}, u32[]{:S(2)}, u32[]{:S(2)}) collective-permute-start(bf16[2,4,128,384]{3,2,1,0:T(8,128)(2,1)} %get-tuple-element.298.refs_4_), channel_id=1, source_target_pairs={{0,4},{4,0},{1,5},{5,1},{2,6},{6,2},{3,7},{7,3},{8,12},{12,8},{9,1... | collective-permute-start | bytes 2359304 | tf_op jit(solution)/shard_map/ppermute | solution.py:630
  8.0 13.7 %collective-permute-start.40 = (bf16[32,384]{1,0:T(8,128)(2,1)}, bf16[32,384]{1,0:T(8,128)(2,1)S(1)}, u32[]{:S(2)}, u32[]{:S(2)}) collective-permute-start(bf16[32,384]{1,0:T(8,128)(2,1)} %get-tuple-element.295.packed_hbm.refs_8_), channel_id=1, source_target_pairs={{0,8},{8,16},{16,24},{24,0},{1,9},{9,17},{17,25},{25,1},{2,10},{10... | collective-permute-start | bytes 73736 | tf_op jit(solution)/shard_map/ppermute | solution.py:624
  8.0 13.7 %collective-permute-start.41 = (bf16[32,384]{1,0:T(8,128)(2,1)}, bf16[32,384]{1,0:T(8,128)(2,1)S(1)}, u32[]{:S(2)}, u32[]{:S(2)}) collective-permute-start(bf16[32,384]{1,0:T(8,128)(2,1)} %get-tuple-element.295.packed_hbm.refs_8_), channel_id=1, source_target_pairs={{0,16},{8,24},{16,0},{24,8},{1,17},{9,25},{17,1},{25,9},{2,18},{10... | collective-permute-start | bytes 73736 | tf_op jit(solution)/shard_map/ppermute | solution.py:624
  9.6 12.1 %collective-permute-start.42 = (bf16[32,384]{1,0:T(8,128)(2,1)}, bf16[32,384]{1,0:T(8,128)(2,1)S(1)}, u32[]{:S(2)}, u32[]{:S(2)}) collective-permute-start(bf16[32,384]{1,0:T(8,128)(2,1)} %get-tuple-element.295.packed_hbm.refs_8_), channel_id=1, source_target_pairs={{0,24},{8,0},{16,8},{24,16},{1,25},{9,1},{17,9},{25,17},{2,26},{10... | collective-permute-start | bytes 73736 | tf_op jit(solution)/shard_map/ppermute | solution.py:624
  21.7 0.6 %copy-start.48 = (bf16[32,384]{1,0:T(8,128)(2,1)}, bf16[32,384]{1,0:T(8,128)(2,1)S(1)}, u32[]{:S(2)}) copy-start(bf16[32,384]{1,0:T(8,128)(2,1)S(1)} %collective-permute-done.40.refs_9_) | copy-start | bytes 73732
  21.7 0.6 %copy-start.49 = (bf16[32,384]{1,0:T(8,128)(2,1)}, bf16[32,384]{1,0:T(8,128)(2,1)S(1)}, u32[]{:S(2)}) copy-start(bf16[32,384]{1,0:T(8,128)(2,1)S(1)} %collective-permute-done.41.refs_10_) | copy-start | bytes 73732
  21.7 0.6 %copy-start.50 = (bf16[32,384]{1,0:T(8,128)(2,1)}, bf16[32,384]{1,0:T(8,128)(2,1)S(1)}, u32[]{:S(2)}) copy-start(bf16[32,384]{1,0:T(8,128)(2,1)S(1)} %collective-permute-done.42.refs_11_) | copy-start | bytes 73732
  26.0 4.4 %collective-permute-start.25 = (f32[32,384]{1,0:T(8,128)}, f32[32,384]{1,0:T(8,128)S(1)}, u32[]{:S(2)}, u32[]{:S(2)}) collective-permute-start(f32[32,384]{1,0:T(8,128)} %get-tuple-element.224.refs_0_), channel_id=1, source_target_pairs={{0,4},{4,0},{1,5},{5,1},{2,6},{6,2},{3,7},{7,3},{8,12},{12,8},{9,1... | collective-permute-start | bytes 147464 | tf_op jit(solution)/shard_map/cond/branch_5_fun/ppermute | solution.py:624
  29.5 12.0 %collective-permute-start.29 = (bf16[2,384,384]{2,1,0:T(8,128)(2,1)}, bf16[2,384,384]{2,1,0:T(8,128)(2,1)}, u32[]{:S(2)}, u32[]{:S(2)}) collective-permute-start(bf16[2,384,384]{2,1,0:T(8,128)(2,1)} %slice.19), channel_id=1, source_target_pairs={{0,4},{4,0},{1,5},{5,1},{2,6},{6,2},{3,7},{7,3},{8,12},{12,8},{9,1... | collective-permute-start | bytes 1769480 | tf_op jit(solution)/shard_map/cond/branch_5_fun/ppermute | solution.py:630
  30.4 7.6 %copy-start.13 = (bf16[8,256,384]{2,1,0:T(8,128)(2,1)S(1)}, bf16[8,256,384]{2,1,0:T(8,128)(2,1)}, u32[]{:S(2)}) copy-start(bf16[8,256,384]{2,1,0:T(8,128)(2,1)} %get-tuple-element.231.old_k) | copy-start | bytes 4718596 | tf_op jit(solution)/shard_map/cond
  30.4 7.6 %copy-start.29 = (bf16[8,256,384]{2,1,0:T(8,128)(2,1)S(1)}, bf16[8,256,384]{2,1,0:T(8,128)(2,1)}, u32[]{:S(2)}) copy-start(bf16[8,256,384]{2,1,0:T(8,128)(2,1)} %get-tuple-element.232.old_v) | copy-start | bytes 4718596 | tf_op jit(solution)/shard_map/cond
  32.5 6.3 %collective-permute-start.26 = (f32[8,768]{1,0:T(8,128)S(1)}, f32[8,768]{1,0:T(8,128)S(1)}, u32[]{:S(2)}, u32[]{:S(2)}) collective-permute-start(f32[8,768]{1,0:T(8,128)S(1)} %get-tuple-element.229.refs_0_), channel_id=1, source_target_pairs={{0,1},{1,2},{2,3},{3,0},{4,5},{5,6},{6,7},{7,4},{8,9},{9,10},{10,1... | collective-permute-start | bytes 73736 | tf_op jit(solution)/shard_map/cond/branch_5_fun/ppermute | solution.py:624
  34.1 4.7 %collective-permute-start.27 = (f32[8,768]{1,0:T(8,128)S(1)}, f32[8,768]{1,0:T(8,128)S(1)}, u32[]{:S(2)}, u32[]{:S(2)}) collective-permute-start(f32[8,768]{1,0:T(8,128)S(1)} %get-tuple-element.229.refs_0_), channel_id=1, source_target_pairs={{0,2},{1,3},{2,0},{3,1},{4,6},{5,7},{6,4},{7,5},{8,10},{9,11},{10,... | collective-permute-start | bytes 73736 | tf_op jit(solution)/shard_map/cond/branch_5_fun/ppermute | solution.py:624
  36.7 3.8 %collective-permute-start.28 = (f32[8,768]{1,0:T(8,128)S(1)}, f32[8,768]{1,0:T(8,128)S(1)}, u32[]{:S(2)}, u32[]{:S(2)}) collective-permute-start(f32[8,768]{1,0:T(8,128)S(1)} %get-tuple-element.229.refs_0_), channel_id=1, source_target_pairs={{0,3},{1,0},{2,1},{3,2},{4,7},{5,4},{6,5},{7,6},{8,11},{9,8},{10,9... | collective-permute-start | bytes 73736 | tf_op jit(solution)/shard_map/cond/branch_5_fun/ppermute | solution.py:624
  38.0 3.4 %copy-start.45 = (s32[8]{0:T(128)S(1)}, s32[8]{0:T(128)}, u32[]{:S(2)}) copy-start(s32[8]{0:T(128)} %get-tuple-element.235.len_hbm) | copy-start | bytes 100 | tf_op jit(solution)/shard_map/cond
  40.5 0.7 %copy-start.5 = (f32[8,128]{1,0:T(8,128)S(1)}, f32[8,128]{1,0:T(8,128)}, u32[]{:S(2)}) copy-start(f32[8,128]{1,0:T(8,128)} %get-tuple-element.233.refs_4_) | copy-start | bytes 12292 | tf_op jit(solution)/shard_map/cond
  43.9 1.1 %copy-start.21 = (bf16[8,256,384]{2,1,0:T(8,128)(2,1)}, bf16[8,256,384]{2,1,0:T(8,128)(2,1)S(1)}, u32[]{:S(2)}) copy-start(bf16[8,256,384]{2,1,0:T(8,128)(2,1)S(1)} %get-tuple-element.334) | copy-start | bytes 4718596 | tf_op jit(solution)/shard_map/cond
  43.9 1.7 %copy-start.37 = (bf16[8,256,384]{2,1,0:T(8,128)(2,1)}, bf16[8,256,384]{2,1,0:T(8,128)(2,1)S(1)}, u32[]{:S(2)}) copy-start(bf16[8,256,384]{2,1,0:T(8,128)(2,1)S(1)} %get-tuple-element.335) | copy-start | bytes 4718596 | tf_op jit(solution)/shard_map/cond
  45.6 0.6 %copy-start.51 = (bf16[8,768]{1,0:T(8,128)(2,1)}, bf16[8,768]{1,0:T(8,128)(2,1)S(1)}, u32[]{:S(2)}) copy-start(bf16[8,768]{1,0:T(8,128)(2,1)S(1)} %get-tuple-element.293) | copy-start | bytes 36868
